TPU v7x, 256 devices: a whole 4x4x8 slice. The times are simulated.
256 devices in a mesh: mx: 16 (over z, core), my: 16 (over x, y).
Axes of the slice: x: 4, y: 4, z: 8, core: 2. Of those that a mesh axis runs over, the one named last changes fastest.
Arguments:
- features: bfloat16 [8192, 32, 512], P(('mx', 'my')), may hold values from -6 to 6
- coords: int32 [3, 8192], P(None, ('mx', 'my')), may hold values from 0 to 63, as said below
- counts: int32 [256], P(('mx', 'my')), may hold values from 16 to 32, as said below
- neighbours: int32 [6, 8192], P(None, ('mx', 'my')), may hold values from -1 to 8191, as said below
- fine_weights: bfloat16 [3, 32, 224], replicated, may hold values from -0.375 to 0.375
- down_weight: bfloat16 [2048, 256], replicated, may hold values from -0.25 to 0.25
- up_weight: bfloat16 [256, 2048], replicated, may hold values from -0.375 to 0.375
- norm_gain: float32 [256], replicated, may hold values from 0.1 to 1.9
- norm_bias: float32 [256], replicated, may hold values from -3 to 3
- coarse_weight: bfloat16 [6912, 256], P(None, 'my'), may hold values from -0.078125 to 0.078125
Outputs:
- fine_out: bfloat16 [8192, 32, 512], P(('mx', 'my'))
- coarse_out: bfloat16 [32, 32, 2, 256], P('mx', 'my')
Inputs may be any that keep to these rules, and one draw needn't show every extreme that they name: The live slots of a device are its first counts entries; some device is full in every draw. `coords`: the live blocks of the device with mx index i and my index j lie at z in [i * 4, (i + 1) * 4), y in [j * 4, (j + 1) * 4), x in [0, 4), distinct, in Morton order of their coordinates inside that region; slots that are not live hold 0. `neighbours`: A live block's entry is the slot of the live block one step away in that direction, or -1 if there is none; the relation is symmetric; slots that are not live hold -1.
All inputs are finite; a program needn't handle non-finite values.
Results may differ from a plain program's by a relative error of at most 0.0095.
Values may be sent and summed in bfloat16 or wider, within the bound.
No kernel may reach another device: no remote copies, remote signals or barrier semaphores. Data moves between devices by JAX's collectives and lax.ppermute only.
A program may use at most 128 MiB of HBM per device.

v0:
```python
import functools

import jax
import jax.numpy as jnp
import ml_dtypes
import numpy as np
from jax import lax
from jax.experimental import pallas as pl
from jax.experimental.pallas import tpu as pltpu
from jax.sharding import Mesh
from jax.sharding import PartitionSpec as P

MX = ("mx_0", "mx_1")
MY = ("my_0", "my_1")
MX_MY = MX + MY
BLOCKS = 32
CHANS = 32
VOXELS = 512
COARSE = 256
GROUP = 8
TAPS = 27
HALF_ROWS = TAPS * COARSE // 2
NORM_EPS = 1e-05
bf16 = jnp.bfloat16
f32 = jnp.float32


def octant(z, y, x):
    return z // 4 * 4 + y // 4 * 2 + x // 4


def voxel_zyx():
    voxel = np.arange(VOXELS)
    return voxel // 64, voxel // 8 % 8, voxel % 8


@functools.cache
def tables():
    z, y, x = voxel_zyx()
    voxel = np.arange(VOXELS)
    faces = np.zeros((VOXELS, 256), np.float32)
    y_lane = z % 2 * 64 + z // 2 * 8 + x
    faces[voxel[y == 0], y_lane[y == 0]] = 1
    faces[voxel[y == 7], y_lane[y == 7] + 32] = 1
    z_lane = y * 8 + x
    faces[voxel[z == 0], 128 + 64 + z_lane[z == 0]] = 1
    faces[voxel[z == 7], 128 + z_lane[z == 7]] = 1
    own = np.arange(256) // 32
    pool = (octant(z, y, x)[:, None] == own[None, :]).astype(np.float32) / 64
    spread = (own[:, None] == octant(z, y, x)[None, :]).astype(np.float32)
    lane = np.arange(128)
    y_octant = octant(lane % 32 // 8 * 2 + lane // 64, lane // 32 % 2 * 4, lane % 8)
    z_octant = octant((lane < 64) * 4, lane % 64 // 8, lane % 8)
    y_spread = (own[:, None] == y_octant[None, :]).astype(np.float32)
    z_spread = (own[:, None] == z_octant[None, :]).astype(np.float32)
    cells = [(a, b, c) for a in range(2) for b in range(2) for c in range(2)]
    cells += [(a, b, c) for b in (-1, 2) for a in range(2) for c in range(2)]
    cells += [(a, b, c) for a in (-1, 2) for b in range(2) for c in range(2)]

    def row_of(a, b, c):
        part = (a // 2 + 1) * 3 + b // 2 + 1
        return part * 8 + a % 2 * 4 + b % 2 * 2 + c

    patch = np.zeros((TAPS, 32, 128), np.float32)
    plain = np.zeros((32, 128), np.float32)
    for i, (a, b, c) in enumerate(cells):
        plain[i, row_of(a, b, c)] = 1
        for t in range(TAPS):
            near = (a + t // 9 - 1, b + t // 3 % 3 - 1, c + t % 3 - 1)
            if 0 <= near[2] < 2:
                patch[t, i, row_of(*near)] = 1
    kinds = (faces, pool, spread, y_spread, z_spread, patch.reshape(TAPS * 32, 128), plain)
    return tuple(k.astype(ml_dtypes.bfloat16) for k in kinds)


def lanes():
    return lax.broadcasted_iota(jnp.int32, (CHANS, 128), 1)


def silu(x):
    return x * (1.0 / (1.0 + jnp.exp(-x)))


def tile(k):
    return slice(k * 128, k * 128 + 128)


def take_faces(signal, faces_ref, y_bank, z_bank):
    for i in range(0, BLOCKS, 8):
        block = signal[i : i + 8].reshape(8 * CHANS, VOXELS)
        packed = jnp.dot(block, faces_ref[...], preferred_element_type=f32).astype(bf16)
        y_bank[i : i + 8] = packed[:, :128].reshape(8, CHANS, 128)
        z_bank[i : i + 8] = packed[:, 128:].reshape(8, CHANS, 128)


def fill_planes(coords, counts, y_bank, z_bank, work, outs):
    lane = lanes()
    work[...] = jnp.zeros_like(work)
    in_low = (lane & 32) == 0
    in_back = lane >= 64

    def one(j, carry):
        live = j < counts[0]
        z, y, x = coords[0, j] & 3, coords[1, j] & 3, coords[2, j]
        odd = (x & 1) == 1
        y_row, z_row = (z * 4 + x) >> 1, (y * 4 + x) >> 1
        face = y_bank[j]
        turned = pltpu.roll(face, 32, 1)
        value = jnp.where(odd, turned, face)
        for plane, edge, low in ((0, 0, True), (1, 3, False)):
            row = jnp.where(live & (y == edge), y_row, 8)
            mask = jnp.logical_xor(in_low if low else jnp.logical_not(in_low), odd)
            work[plane, row] = jnp.where(mask, value, work[plane, row])
        face = z_bank[j]
        turned = pltpu.roll(face, 64, 1)
        value = jnp.where(odd, turned, face)
        for plane, edge, low in ((2, 0, True), (3, 3, False)):
            row = jnp.where(live & (z == edge), z_row, 8)
            mask = jnp.logical_xor(in_back if low else jnp.logical_not(in_back), odd)
            work[plane, row] = jnp.where(mask, value, work[plane, row])
        return carry

    lax.fori_loop(0, BLOCKS, one, 0, unroll=4)
    for plane, out in enumerate(outs):
        out[...] = work[plane, :8]


def received(plane_ref, p, back):
    row = plane_ref[p // 2]
    return pltpu.roll(row, back, 1) if p % 2 else row


def bank_received(planes, y_bank, z_bank):
    zero = jnp.zeros((CHANS, 128), bf16)
    y_bank[BLOCKS] = zero
    z_bank[BLOCKS] = zero
    for p in range(16):
        y_bank[33 + p] = received(planes[0], p, 96)
        y_bank[49 + p] = received(planes[1], p, 96)
        z_bank[33 + p] = received(planes[2], p, 64)
        z_bank[49 + p] = received(planes[3], p, 64)


def convolve(coords, links, signal, y_bank, z_bank, weight, taps, finish):
    lane = lanes()
    along_x = lane & 7
    along_yx = lane & 63
    front = lane < 64

    def build(j, slot):
        z, y, x = coords[0, j] & 3, coords[1, j] & 3, coords[2, j]
        y_pos, z_pos = z * 4 + x, y * 4 + x

        def near(direction, inside, remote):
            link = links[direction, j]
            here = link & (BLOCKS - 1)
            if inside is not None:
                here = jnp.where(inside, here, remote)
            return jnp.where(link < 0, BLOCKS, here)

        x_up, x_down = near(0, None, None), near(1, None, None)
        y_up = y_bank[near(2, y < 3, 33 + y_pos)]
        y_down = y_bank[near(3, y > 0, 49 + y_pos)]
        z_up = z_bank[near(4, z < 3, 33 + z_pos)]
        z_down = z_bank[near(5, z > 0, 49 + z_pos)]
        own = [signal[j, :, tile(k)] for k in range(4)]
        half = [z_down] + [pltpu.roll(own[k], 64, 1) for k in range(4)] + [z_up]
        for k in range(4):
            to = tile(k)
            taps[slot, 0:32, to] = own[k]
            taps[slot, 32:64, to] = jnp.where(
                along_x == 7,
                pltpu.roll(signal[x_up, :, to], 7, 1),
                pltpu.roll(own[k], 127, 1),
            )
            taps[slot, 64:96, to] = jnp.where(
                along_x == 0,
                pltpu.roll(signal[x_down, :, to], 121, 1),
                pltpu.roll(own[k], 1, 1),
            )
            taps[slot, 96:128, to] = jnp.where(
                along_yx >= 56, pltpu.roll(y_up, 56 - 8 * k, 1), pltpu.roll(own[k], 120, 1)
            )
            taps[slot, 128:160, to] = jnp.where(
                along_yx < 8, pltpu.roll(y_down, 96 - 8 * k, 1), pltpu.roll(own[k], 8, 1)
            )
            taps[slot, 160:192, to] = jnp.where(front, half[k + 1], half[k + 2])
            taps[slot, 192:224, to] = jnp.where(front, half[k], half[k + 1])

    def some(i, carry):
        for u in range(4):
            build(i * 4 + u, u)
        for u in range(4):
            result = jnp.dot(weight[...], taps[u], preferred_element_type=f32)
            finish(i * 4 + u, result)
        return carry

    lax.fori_loop(0, BLOCKS // 4, some, 0)


def first_faces(coords, counts, features, faces, signal, y_own, z_own, p0, p1, p2, p3, work):
    def one(j, carry):
        signal[j] = silu(features[j].astype(f32)).astype(bf16)
        return carry

    lax.fori_loop(0, BLOCKS, one, 0, unroll=4)
    take_faces(signal, faces, y_own, z_own)
    fill_planes(coords, counts, y_own, z_own, work, (p0, p1, p2, p3))


def first_conv(
    coords, counts, links, features, signal_in, y_own, z_own, r0, r1, r2, r3,
    weight, faces, pool, down,
    level, p0, p1, p2, p3, message,
    signal, y_bank, z_bank, taps, work, gathered,
):
    signal[0:BLOCKS] = signal_in[...]
    signal[BLOCKS] = jnp.zeros((CHANS, VOXELS), bf16)
    y_bank[0:BLOCKS] = y_own[...]
    z_bank[0:BLOCKS] = z_own[...]
    bank_received((r0, r1, r2, r3), y_bank, z_bank)

    def finish(j, result):
        level[j] = (features[j].astype(f32) + result).astype(bf16)

    convolve(coords, links, signal, y_bank, z_bank, weight, taps, finish)
    take_faces(level, faces, y_bank, z_bank)
    fill_planes(coords, counts, y_bank, z_bank, work, (p0, p1, p2, p3))
    gathered[...] = jnp.zeros_like(gathered)
    diagonal = channel_diagonal()
    for i in range(0, BLOCKS, 8):
        block = level[i : i + 8].reshape(8 * CHANS, VOXELS)
        means = jnp.dot(block, pool[...], preferred_element_type=f32)
        for u in range(8):
            j = i + u
            part = jnp.where(diagonal, means[u * CHANS : (u + 1) * CHANS], 0.0)
            cell, pos = place(coords, j)
            pos = jnp.where(j < counts[0], pos, 8)
            gathered[pos, pl.ds(cell, 1), :] = jnp.sum(part, axis=0, keepdims=True)
    total = jnp.zeros((16, COARSE), f32)
    for pos in range(8):
        total += jnp.dot(
            gathered[pos].astype(bf16), down[pos * 256 : pos * 256 + 256], preferred_element_type=f32
        )
    total = total[:8]
    mean = jnp.mean(total, axis=0, keepdims=True)
    spread = jnp.sum((total - mean) * (total - mean), axis=0, keepdims=True)
    row = lax.broadcasted_iota(jnp.int32, (8, COARSE), 0)
    extra = jnp.where(row == 0, mean, jnp.where(row == 1, spread, 0.0))
    for i in range(16):
        message[i, 0:8] = total
        message[i, 8:16] = extra


def channel_diagonal():
    channel = lax.broadcasted_iota(jnp.int32, (CHANS, 256), 0)
    return channel == (lax.broadcasted_iota(jnp.int32, (CHANS, 256), 1) & 31)


def place(coords, j):
    z, y, x = coords[0, j] & 3, coords[1, j] & 3, coords[2, j]
    cell = (z >> 1) * 4 + (y >> 1) * 2 + (x >> 1)
    return cell, (z & 1) * 4 + (y & 1) * 2 + (x & 1)


def merged_sums(means, spreads, entries):
    mean = jnp.mean(means, axis=0, keepdims=True)
    away = means - mean
    return mean, jnp.sum(spreads + entries * away * away, axis=0, keepdims=True)


def row_sums(where, message, partial, strip):
    mean, spread = merged_sums(message[:, 8, :], message[:, 9, :], 8.0)
    row = lax.broadcasted_iota(jnp.int32, (8, COARSE), 0)
    both = jnp.where(row == 0, mean, jnp.where(row == 1, spread, 0.0))
    for i in range(16):
        partial[i] = both
    minor = where[1]
    for step in range(3):
        strip[step] = message[jnp.clip(minor + step - 1, 0, 15), 0:8]


def group_total(x):
    lane = lax.broadcasted_iota(jnp.int32, x.shape, 1)
    for width in (1, 2, 4):
        x = x + jnp.where(
            (lane & width) == 0, pltpu.roll(x, COARSE - width, 1), pltpu.roll(x, width, 1)
        )
    return x


def second_conv(
    coords, counts, links, where, level, r0, r1, r2, r3, partial, s_low, s_own, s_high,
    near_half, far_half, gain, bias, up, weight, faces, spread, y_spread, z_spread, patch, plain,
    second, signal2, y_own, z_own, p0, p1, p2, p3, coarse,
    joined, signal, y_bank, z_bank, taps, work, active, raw, patches, lifted, rows,
):
    major, minor = where[0], where[1]
    mean, spread_sum = merged_sums(partial[:, 0, :], partial[:, 1, :], 128.0)
    group_mean = group_total(mean) * (1.0 / GROUP)
    away = mean - group_mean
    variance = group_total(spread_sum + 2048.0 * away * away) * (1.0 / (2048 * GROUP))
    scale = gain[...] / jnp.sqrt(variance + NORM_EPS)
    active[...] = jnp.zeros_like(active)
    raw[...] = jnp.zeros_like(raw)
    for dz, strip in enumerate((s_low, s_own, s_high)):
        inside_z = (major + dz >= 1) & (major + dz <= 16)
        for dy in range(3):
            inside = inside_z & (minor + dy >= 1) & (minor + dy <= 16)
            value = strip[dy]
            at = (dz * 3 + dy) * 8
            raw[at : at + 8] = value
            normed = silu((value - group_mean) * scale + bias[...])
            active[at : at + 8] = jnp.where(inside, normed, 0.0)
    grid = active[...].astype(bf16)
    cells = jnp.dot(patch[...], grid, preferred_element_type=f32).astype(bf16)
    for t in range(TAPS):
        patches[2 * t] = cells[t * 32 : t * 32 + 32, :128]
        patches[2 * t + 1] = cells[t * 32 : t * 32 + 32, 128:]
    rest = raw[...]
    total = jnp.zeros((32, COARSE), f32)
    for _ in range(3):
        high = rest.astype(bf16)
        rest = rest - high.astype(f32)
        total += jnp.dot(plain[...], high, preferred_element_type=f32)
    core = major & 1
    contract = (((1,), (1,)), ((), ()))
    for half, base in ((near_half, core * TAPS), (far_half, (1 - core) * TAPS)):
        for t in range(TAPS):
            total += lax.dot_general(
                patches[base + t], half[:, tile(t)], contract, preferred_element_type=f32
            )
    result = total.astype(bf16)
    coarse[...] = result[0:8]
    for pos in range(8):
        lifted[pos] = jnp.dot(
            result, up[:, pos * 256 : pos * 256 + 256], preferred_element_type=f32
        )
    diagonal = channel_diagonal()

    def row_block(pos, cell):
        return jnp.where(diagonal, lifted[pos, pl.ds(cell, 1), :], 0.0).astype(bf16)

    for i in range(0, BLOCKS, 8):
        for u in range(8):
            cell, pos = place(coords, i + u)
            rows[u * CHANS : (u + 1) * CHANS] = row_block(pos, cell)
        term = jnp.dot(rows[...], spread[...], preferred_element_type=f32)
        base = level[i : i + 8].reshape(8 * CHANS, VOXELS).astype(f32)
        merged = (base + term).astype(bf16)
        joined[i : i + 8] = merged.reshape(8, CHANS, VOXELS)
        signal[i : i + 8] = silu(merged.astype(f32)).astype(bf16).reshape(8, CHANS, VOXELS)
    signal[BLOCKS] = jnp.zeros((CHANS, VOXELS), bf16)
    take_faces(signal, faces, y_bank, z_bank)
    zero = jnp.zeros((CHANS, 128), bf16)
    y_bank[BLOCKS] = zero
    z_bank[BLOCKS] = zero
    kinds = (
        (r0, y_bank, 33, 12, y_spread, 96, 4, 0, 2),
        (r1, y_bank, 49, 8, y_spread, 96, 4, 1, 2),
        (r2, z_bank, 33, 20, z_spread, 64, 2, 0, 4),
        (r3, z_bank, 49, 16, z_spread, 64, 2, 1, 4),
    )
    for plane, bank, entry, first, expand, back, stride, far, edge in kinds:
        for i in range(0, 16, 8):
            for u in range(8):
                p = i + u
                a, x = p // 4, p % 4
                pos = a % 2 * stride + far * edge + x % 2
                cell = first + a // 2 * 2 + x // 2
                rows[u * CHANS : (u + 1) * CHANS] = jnp.where(
                    diagonal, lifted[pos, cell : cell + 1, :], 0.0
                ).astype(bf16)
            term = jnp.dot(rows[...], expand[...], preferred_element_type=f32)
            for u in range(8):
                face = received(plane, i + u, back).astype(f32)
                merged = (face + term[u * CHANS : (u + 1) * CHANS]).astype(bf16)
                bank[entry + i + u] = silu(merged.astype(f32)).astype(bf16)

    def finish(j, value):
        out = (joined[j].astype(f32) + value).astype(bf16)
        second[j] = out
        signal2[j] = silu(out.astype(f32)).astype(bf16)

    convolve(coords, links, signal, y_bank, z_bank, weight, taps, finish)
    take_faces(signal2, faces, y_own, z_own)
    fill_planes(coords, counts, y_own, z_own, work, (p0, p1, p2, p3))


def third_conv(
    coords, counts, links, second, signal_in, y_own, z_own, r0, r1, r2, r3, weight,
    out, signal, y_bank, z_bank, taps,
):
    signal[0:BLOCKS] = signal_in[...]
    signal[BLOCKS] = jnp.zeros((CHANS, VOXELS), bf16)
    y_bank[0:BLOCKS] = y_own[...]
    z_bank[0:BLOCKS] = z_own[...]
    bank_received((r0, r1, r2, r3), y_bank, z_bank)

    def finish(j, result):
        value = second[j].astype(f32) + result
        out[j] = jnp.where(j < counts[0], value, 0.0).astype(bf16)

    convolve(coords, links, signal, y_bank, z_bank, weight, taps, finish)


def call(kernel, scalars, arrays, outs, scratch, mebibytes):
    smem = pl.BlockSpec(memory_space=pltpu.SMEM)
    vmem = pl.BlockSpec(memory_space=pltpu.VMEM)
    return pl.pallas_call(
        kernel,
        in_specs=[smem] * len(scalars) + [vmem] * len(arrays),
        out_specs=[vmem] * len(outs),
        out_shape=[jax.ShapeDtypeStruct(s, d) for s, d in outs],
        scratch_shapes=[pltpu.VMEM(s, d) for s, d in scratch],
        compiler_params=pltpu.CompilerParams(vmem_limit_bytes=mebibytes << 20),
    )(*scalars, *arrays)


FIELD = ((BLOCKS, CHANS, VOXELS), bf16)
FACES = ((BLOCKS, CHANS, 128), bf16)
PLANE = ((8, CHANS, 128), bf16)
SIGNAL = ((BLOCKS + 1, CHANS, VOXELS), bf16)
BANK = ((BLOCKS + 33, CHANS, 128), bf16)
TAP_STACK = ((4, 7 * CHANS, VOXELS), bf16)
WORK = ((4, 9, CHANS, 128), bf16)


def shifted(x, axes, step):
    count = lax.axis_size(axes)
    return lax.ppermute(x, axes, [(i, (i + step) % count) for i in range(count)])


def swap_planes(planes):
    y_low, y_high, z_low, z_high = planes
    return (
        shifted(y_low, MY, -1),
        shifted(y_high, MY, 1),
        shifted(z_low, MX, -1),
        shifted(z_high, MX, 1),
    )


def local(
    features, coords, counts, neighbours, fine_weights, down_weight, up_weight, norm_gain, norm_bias,
    coarse_weight,
):
    faces, pool, spread, y_spread, z_spread, patch, plain = map(jnp.asarray, tables())
    major = lax.axis_index(MX)
    minor = lax.axis_index(MY)
    where = jnp.stack([major, minor]).astype(jnp.int32)
    part = lax.dynamic_slice_in_dim(
        coarse_weight.T, lax.axis_index("mx_1") * HALF_ROWS, HALF_ROWS, 1
    )
    near_half = lax.all_gather(part, MY, axis=0, tiled=True)
    far_half = lax.ppermute(near_half, "mx_1", [(0, 1), (1, 0)])

    signal, y_own, z_own, *planes = call(
        first_faces, (coords, counts), (features, faces),
        (FIELD, FACES, FACES) + (PLANE,) * 4, (WORK,), 16,
    )
    planes = swap_planes(planes)
    level, *planes, message = call(
        first_conv, (coords, counts, neighbours),
        (features, signal, y_own, z_own, *planes, fine_weights[0], faces, pool, down_weight),
        (FIELD,) + (PLANE,) * 4 + (((16, 16, COARSE), f32),),
        (SIGNAL, BANK, BANK, TAP_STACK, WORK, ((9, 16, COARSE), f32)), 24,
    )
    message = lax.all_to_all(message, MY, 0, 0)
    partial, strip = call(
        row_sums, (where,), (message,),
        (((16, 8, COARSE), f32), ((3, 8, COARSE), f32)), (), 8,
    )
    strip_low = shifted(strip, MX, 1)
    strip_high = shifted(strip, MX, -1)
    planes = swap_planes(planes)
    partial = lax.all_to_all(partial, MX, 0, 0)
    second, signal, y_own, z_own, *planes, coarse = call(
        second_conv, (coords, counts, neighbours, where),
        (level, *planes, partial, strip_low, strip, strip_high, near_half, far_half,
         norm_gain.reshape(1, COARSE), norm_bias.reshape(1, COARSE), up_weight, fine_weights[1],
         faces, spread, y_spread, z_spread, patch, plain),
        (FIELD, FIELD, FACES, FACES) + (PLANE,) * 4 + (((8, COARSE), bf16),),
        (FIELD, SIGNAL, BANK, BANK, TAP_STACK, WORK, ((128, COARSE), f32), ((128, COARSE), f32),
         ((2 * TAPS, 32, 128), bf16), ((8, 32, COARSE), f32), ((256, 256), bf16)), 32,
    )
    planes = swap_planes(planes)
    (fine_out,) = call(
        third_conv, (coords, counts, neighbours),
        (second, signal, y_own, z_own, *planes, fine_weights[2]),
        (FIELD,), (SIGNAL, BANK, BANK, TAP_STACK), 24,
    )
    return fine_out, coarse.reshape(2, 2, 2, COARSE)


def solution(mesh):
    split = Mesh(mesh.devices.reshape(8, 2, 4, 4), ("mx_0", "mx_1", "my_0", "my_1"))
    placed = (
        P(MX_MY, None, None), P(None, MX_MY), P(MX_MY), P(None, MX_MY),
        P(), P(), P(), P(), P(), P(None, MY),
    )
    return jax.shard_map(
        local,
        mesh=split,
        in_specs=placed,
        out_specs=(P(MX_MY, None, None), P(MX, MY, None, None)),
        check_vma=False,
    )
```

profile of v0, /device:TPU:1, one launch (start us, length us, event | category | flops | bytes accessed | tf_op | source)
XLA Modules:
  0.0 181.3 jit_solution(11998406309453566963)
XLA Ops:
  7.3 0.8 copy-done
  8.8 54.4 %all-gather.2.cloned.1.call-done.near_half = bf16[256,3456]{1,0:T(8,128)(2,1)} async-done(((bf16[16,3456]{1,0:T(8,128)(2,1)}), bf16[256,3456]{1,0:T(8,128)(2,1)}) %all-gather.2.cloned.1.call-update) | async-done | bytes 1769488 | tf_op jit(solution)/shard_map/all_gather | solution.py:455
  63.2 2.0 %collective-permute-start.10 = (bf16[256,3456]{1,0:T(8,128)(2,1)}, bf16[256,3456]{1,0:T(8,128)(2,1)}, u32[]{:S(2)}, u32[]{:S(2)}) collective-permute-start(bf16[256,3456]{1,0:T(8,128)(2,1)} %all-gather.2.cloned.1.call-done.near_half), channel_id=1, source_target_pairs={{0,16},{16,0},{1,17},{17,1},{2,18},{18,2},{3,19},{19,3},{4,20},{20... | collective-permute-start | bytes 5308424 | tf_op jit(solution)/shard_map/ppermute | solution.py:456
  65.8 1.2 copy-done.1
  67.1 0.9 copy-done.3
  68.7 2.8 %shard_map.176 = (bf16[32,32,512]{2,1,0:T(8,128)(2,1)S(1)}, bf16[32,32,128]{2,1,0:T(8,128)(2,1)S(1)}, bf16[32,32,128]{2,1,0:T(8,128)(2,1)S(1)}, bf16[8,32,128]{2...) custom-call(s32[3,32]{1,0:T(4,128)S(1)} %copy-done.30, ...), custom_call_target="tpu_custom_call" | custom-call | tf_op jit(solution)/shard_map/pallas_call | solution.py:410
  71.5 2.5 %collective-permute-start = (bf16[8,32,128]{2,1,0:T(8,128)(2,1)S(1)}, bf16[8,32,128]{2,1,0:T(8,128)(2,1)S(1)}, u32[]{:S(2)}, u32[]{:S(2)}) collective-permute-start(bf16[8,32,128]{2,1,0:T(8,128)(2,1)S(1)} %get-tuple-element.29), channel_id=1, source_target_pairs={{0,15},{1,0},{2,1},{3,2},{4,3},{5,4},{6,5},{7,6},{8,7},{9,8},{10,9... | collective-permute-start | bytes 196616 | tf_op jit(solution)/shard_map/ppermute | solution.py:431
  74.3 1.5 collective-permute-start.3
  75.7 0.8 slice_bitcast_fusion
  76.5 3.9 %collective-permute-done.1.r1 = bf16[8,32,128]{2,1,0:T(8,128)(2,1)S(1)} collective-permute-done((bf16[8,32,128]{2,1,0:T(8,128)(2,1)S(1)}, bf16[8,32,128]{2,1,0:T(8,128)(2,1)S(1)}, u32[]{:S(2)}, u32[]{:S(2)}) %collective-permute-start.1) | collective-permute-done | bytes 65568 | tf_op jit(solution)/shard_map/ppermute | solution.py:431
  80.5 1.2 copy-done.6
  81.7 0.9 copy-done.13
  82.6 9.1 %shard_map.177 = (bf16[32,32,512]{2,1,0:T(8,128)(2,1)S(1)}, bf16[8,32,128]{2,1,0:T(8,128)(2,1)S(1)}, bf16[8,32,128]{2,1,0:T(8,128)(2,1)S(1)}, bf16[8,32,128]{2,1...) custom-call(s32[3,32]{1,0:T(4,128)S(1)} %copy-done.31, s32[1]{0:T(128)S(6)} %copy.19.counts, ...), custom_call_target="tpu_custom_call" | custom-call | tf_op jit(solution)/shard_map/pallas_call | solution.py:410
  91.8 1.0 copy-done.10
  92.7 3.9 %all-to-all-start = ((f32[16,16,256]{2,1,0:T(8,128)}), f32[16,16,256]{2,1,0:T(8,128)S(1)}, u32[]{:S(2)}, u32[]{:S(2)}) async-start(f32[16,16,256]{2,1,0:T(8,128)} %get-tuple-element.38), calls=%async_computation | async-start | bytes 524288 | tf_op jit(solution)/shard_map/all_to_all | solution.py:469
  96.7 7.2 %all-to-all-done.message = f32[16,16,256]{2,1,0:T(8,128)S(1)} async-done(((f32[16,16,256]{2,1,0:T(8,128)}), f32[16,16,256]{2,1,0:T(8,128)S(1)}, u32[]{:S(2)}, u32[]{:S(2)}) %all-to-all-start) | async-done | bytes 262176 | tf_op jit(solution)/shard_map/all_to_all | solution.py:469
  103.9 1.2 shard_map.178
  105.2 9.8 %all-to-all-start.1 = ((f32[16,8,256]{2,1,0:T(8,128)}), f32[16,8,256]{2,1,0:T(8,128)S(1)}, u32[]{:S(2)}, u32[]{:S(2)}) async-start(f32[16,8,256]{2,1,0:T(8,128)} %get-tuple-element.39), calls=%async_computation.1 | async-start | bytes 262144 | tf_op jit(solution)/shard_map/all_to_all | solution.py:477
  115.0 1.0 collective-permute-start.4
  116.4 0.7 collective-permute-start.6
  117.2 1.5 collective-permute-start.7
  119.2 0.8 collective-permute-start.9
  120.1 2.4 %collective-permute-done.5.r1 = bf16[8,32,128]{2,1,0:T(8,128)(2,1)S(1)} collective-permute-done((bf16[8,32,128]{2,1,0:T(8,128)(2,1)S(1)}, bf16[8,32,128]{2,1,0:T(8,128)(2,1)S(1)}, u32[]{:S(2)}, u32[]{:S(2)}) %collective-permute-start.5) | collective-permute-done | bytes 65568 | tf_op jit(solution)/shard_map/ppermute | solution.py:431
  123.1 3.1 %collective-permute-start.8 = (f32[3,8,256]{2,1,0:T(8,128)S(1)}, f32[3,8,256]{2,1,0:T(8,128)S(1)}, u32[]{:S(2)}, u32[]{:S(2)}) collective-permute-start(f32[3,8,256]{2,1,0:T(8,128)S(1)} %get-tuple-element.40.s_own), channel_id=1, source_target_pairs={{0,16},{16,32},{32,48},{48,64},{64,80},{80,96},{96,112},{112,128},... | collective-permute-start | bytes 73736 | tf_op jit(solution)/shard_map/ppermute | solution.py:431
  128.6 1.2 copy-done.9
  129.8 1.2 copy-done.11
  131.1 0.9 copy-done.12
  132.0 0.9 copy-done.18
  133.0 0.8 copy-done.20
  133.8 0.8 copy-done.22
  134.6 0.8 copy-done.24
  135.5 0.8 copy-done.26
  136.3 0.8 copy-done.28
  137.2 0.7 copy-done.33
  137.9 0.7 copy-done.35
  138.6 0.7 copy-done.37
  140.7 14.0 %shard_map.179 = (bf16[32,32,512]{2,1,0:T(8,128)(2,1)S(1)}, bf16[32,32,512]{2,1,0:T(8,128)(2,1)S(1)}, bf16[32,32,128]{2,1,0:T(8,128)(2,1)S(1)}, bf16[32,32,128]{...) custom-call(s32[3,32]{1,0:T(4,128)S(1)} %copy-done.31, ...), custom_call_target="tpu_custom_call" | custom-call | tf_op jit(solution)/shard_map/pallas_call | solution.py:410
  154.7 1.0 copy-done.7
  155.7 0.7 copy-done.14
  156.4 0.7 copy-done.16
  157.1 0.7 collective-permute-start.11
  157.8 0.8 collective-permute-start.12
  158.5 3.3 %collective-permute-start.13 = (bf16[8,32,128]{2,1,0:T(8,128)(2,1)}, bf16[8,32,128]{2,1,0:T(8,128)(2,1)S(1)}, u32[]{:S(2)}, u32[]{:S(2)}) collective-permute-start(bf16[8,32,128]{2,1,0:T(8,128)(2,1)} %get-tuple-element.47), channel_id=1, source_target_pairs={{0,240},{16,0},{32,16},{48,32},{64,48},{80,64},{96,80},{112,96},{1... | collective-permute-start | bytes 196616 | tf_op jit(solution)/shard_map/ppermute | solution.py:431
  162.5 2.0 %collective-permute-done.12.r1 = bf16[8,32,128]{2,1,0:T(8,128)(2,1)S(1)} collective-permute-done((bf16[8,32,128]{2,1,0:T(8,128)(2,1)}, bf16[8,32,128]{2,1,0:T(8,128)(2,1)S(1)}, u32[]{:S(2)}, u32[]{:S(2)}) %collective-permute-start.12) | collective-permute-done | bytes 65568 | tf_op jit(solution)/shard_map/ppermute | solution.py:431
  164.4 1.2 copy-done.8
  165.7 0.9 copy-done.15
  166.6 0.9 copy-done.17
  167.6 6.8 %shard_map.180 = bf16[32,32,512]{2,1,0:T(8,128)(2,1)} custom-call(s32[3,32]{1,0:T(4,128)S(1)} %copy-done.31, s32[1]{0:T(128)S(6)} %copy.19.counts, s32[6,32]{1,0:T(8,128)S(1)} %copy-done.29, bf16[32,32,512]{2,1,0:T(8,128)(2,1)S(1)} %get-tuple-element.41.second, bf16[32,32,512]{2,1,0:T(8,128)(2,1)S(1)} %copy-done.8, bf16[32,32,128]{2,1,0:T(8,128)(2,1)S(1)} %copy-done.15, ...), custom_call_target="tpu_custom_call" | custom-call | tf_op jit(solution)/shard_map/pallas_call | solution.py:410
  (80 shorter events, 7.9 us)
Async XLA Ops:
  7.2 0.9 copy-start
  7.2 73.2 %copy-start.4 = (bf16[512,256]{1,0:T(8,128)(2,1)S(1)}, bf16[512,256]{1,0:T(8,128)(2,1)}, u32[]{:S(2)}) copy-start(bf16[512,256]{1,0:T(8,128)(2,1)} %constant.43.clone.faces) | copy-start | bytes 786436
  7.2 73.2 %copy-start.31 = (s32[3,32]{1,0:T(4,128)S(1)}, s32[3,32]{1,0:T(4,128)}, u32[]{:S(2)}) copy-start(s32[3,32]{1,0:T(4,128)} %coords.7) | copy-start | bytes 1156
  7.2 73.2 %copy-start.29 = (s32[6,32]{1,0:T(8,128)S(1)}, s32[6,32]{1,0:T(8,128)}, u32[]{:S(2)}) copy-start(s32[6,32]{1,0:T(8,128)} %links.5) | copy-start | bytes 2308
  7.2 56.0 %all-gather.2.cloned.1.call-start = ((), (), s32[]{:S(2)}) async-start(), calls=%async_computation.2 | async-start | bytes 1880064 | tf_op jit(solution)/shard_map/all_gather | solution.py:455
  63.2 65.4 %collective-permute-start.10 = (bf16[256,3456]{1,0:T(8,128)(2,1)}, bf16[256,3456]{1,0:T(8,128)(2,1)}, u32[]{:S(2)}, u32[]{:S(2)}) collective-permute-start(bf16[256,3456]{1,0:T(8,128)(2,1)} %all-gather.2.cloned.1.call-done.near_half), channel_id=1, source_target_pairs={{0,16},{16,0},{1,17},{17,1},{2,18},{18,2},{3,19},{19,3},{4,20},{20... | collective-permute-start | bytes 5308424 | tf_op jit(solution)/shard_map/ppermute | solution.py:456
  65.8 1.2 copy-start.1
  67.1 0.9 copy-start.3
  68.7 11.7 %copy-start.2 = (bf16[32,32,512]{2,1,0:T(8,128)(2,1)S(1)}, bf16[32,32,512]{2,1,0:T(8,128)(2,1)}, u32[]{:S(2)}) copy-start(bf16[32,32,512]{2,1,0:T(8,128)(2,1)} %features.3) | copy-start | bytes 3145732
  71.5 5.0 %collective-permute-start = (bf16[8,32,128]{2,1,0:T(8,128)(2,1)S(1)}, bf16[8,32,128]{2,1,0:T(8,128)(2,1)S(1)}, u32[]{:S(2)}, u32[]{:S(2)}) collective-permute-start(bf16[8,32,128]{2,1,0:T(8,128)(2,1)S(1)} %get-tuple-element.29), channel_id=1, source_target_pairs={{0,15},{1,0},{2,1},{3,2},{4,3},{5,4},{6,5},{7,6},{8,7},{9,8},{10,9... | collective-permute-start | bytes 196616 | tf_op jit(solution)/shard_map/ppermute | solution.py:431
  74.0 6.4 %collective-permute-start.1 = (bf16[8,32,128]{2,1,0:T(8,128)(2,1)S(1)}, bf16[8,32,128]{2,1,0:T(8,128)(2,1)S(1)}, u32[]{:S(2)}, u32[]{:S(2)}) collective-permute-start(bf16[8,32,128]{2,1,0:T(8,128)(2,1)S(1)} %get-tuple-element.30), channel_id=1, source_target_pairs={{0,1},{1,2},{2,3},{3,4},{4,5},{5,6},{6,7},{7,8},{8,9},{9,10},{10,1... | collective-permute-start | bytes 196616 | tf_op jit(solution)/shard_map/ppermute | solution.py:431
  74.0 6.4 %collective-permute-start.2 = (bf16[8,32,128]{2,1,0:T(8,128)(2,1)S(1)}, bf16[8,32,128]{2,1,0:T(8,128)(2,1)S(1)}, u32[]{:S(2)}, u32[]{:S(2)}) collective-permute-start(bf16[8,32,128]{2,1,0:T(8,128)(2,1)S(1)} %get-tuple-element.31), channel_id=1, source_target_pairs={{0,240},{16,0},{32,16},{48,32},{64,48},{80,64},{96,80},{112,96},{1... | collective-permute-start | bytes 196616 | tf_op jit(solution)/shard_map/ppermute | solution.py:431
  74.3 6.2 %collective-permute-start.3 = (bf16[8,32,128]{2,1,0:T(8,128)(2,1)S(1)}, bf16[8,32,128]{2,1,0:T(8,128)(2,1)S(1)}, u32[]{:S(2)}, u32[]{:S(2)}) collective-permute-start(bf16[8,32,128]{2,1,0:T(8,128)(2,1)S(1)} %get-tuple-element.32), channel_id=1, source_target_pairs={{0,16},{16,32},{32,48},{48,64},{64,80},{80,96},{96,112},{112,128},... | collective-permute-start | bytes 196616 | tf_op jit(solution)/shard_map/ppermute | solution.py:431
  80.4 1.2 copy-start.6
  81.7 0.9 copy-start.13
  82.6 46.0 %copy-start.5 = (bf16[256,3456]{1,0:T(8,128)(2,1)S(1)}, bf16[256,3456]{1,0:T(8,128)(2,1)}, u32[]{:S(2)}) copy-start(bf16[256,3456]{1,0:T(8,128)(2,1)} %all-gather.2.cloned.1.call-done.near_half) | copy-start | bytes 5308420
  82.6 46.0 %copy-start.19 = (bf16[256,128]{1,0:T(8,128)(2,1)S(1)}, bf16[256,128]{1,0:T(8,128)(2,1)}, u32[]{:S(2)}) copy-start(bf16[256,128]{1,0:T(8,128)(2,1)} %constant.47.clone.z_spread) | copy-start | bytes 196612
  82.6 46.0 %copy-start.38 = (bf16[32,128]{1,0:T(8,128)(2,1)S(1)}, bf16[32,128]{1,0:T(8,128)(2,1)}, u32[]{:S(2)}) copy-start(bf16[32,128]{1,0:T(8,128)(2,1)} %constant.49.clone.plain) | copy-start | bytes 24580
  91.8 1.0 copy-start.10
  92.7 11.2 %all-to-all-start = ((f32[16,16,256]{2,1,0:T(8,128)}), f32[16,16,256]{2,1,0:T(8,128)S(1)}, u32[]{:S(2)}, u32[]{:S(2)}) async-start(f32[16,16,256]{2,1,0:T(8,128)} %get-tuple-element.38), calls=%async_computation | async-start | bytes 524288 | tf_op jit(solution)/shard_map/all_to_all | solution.py:469
  105.2 23.4 %copy-start.32 = (f32[3,8,256]{2,1,0:T(8,128)}, f32[3,8,256]{2,1,0:T(8,128)S(1)}, u32[]{:S(2)}) copy-start(f32[3,8,256]{2,1,0:T(8,128)S(1)} %get-tuple-element.40.s_own) | copy-start | bytes 73732
  105.2 23.4 %all-to-all-start.1 = ((f32[16,8,256]{2,1,0:T(8,128)}), f32[16,8,256]{2,1,0:T(8,128)S(1)}, u32[]{:S(2)}, u32[]{:S(2)}) async-start(f32[16,8,256]{2,1,0:T(8,128)} %get-tuple-element.39), calls=%async_computation.1 | async-start | bytes 262144 | tf_op jit(solution)/shard_map/all_to_all | solution.py:477
  115.0 3.7 %collective-permute-start.4 = (bf16[8,32,128]{2,1,0:T(8,128)(2,1)S(1)}, bf16[8,32,128]{2,1,0:T(8,128)(2,1)S(1)}, u32[]{:S(2)}, u32[]{:S(2)}) collective-permute-start(bf16[8,32,128]{2,1,0:T(8,128)(2,1)S(1)} %get-tuple-element.34), channel_id=1, source_target_pairs={{0,15},{1,0},{2,1},{3,2},{4,3},{5,4},{6,5},{7,6},{8,7},{9,8},{10,9... | collective-permute-start | bytes 196616 | tf_op jit(solution)/shard_map/ppermute | solution.py:431
  116.0 6.4 %collective-permute-start.5 = (bf16[8,32,128]{2,1,0:T(8,128)(2,1)S(1)}, bf16[8,32,128]{2,1,0:T(8,128)(2,1)S(1)}, u32[]{:S(2)}, u32[]{:S(2)}) collective-permute-start(bf16[8,32,128]{2,1,0:T(8,128)(2,1)S(1)} %get-tuple-element.35), channel_id=1, source_target_pairs={{0,1},{1,2},{2,3},{3,4},{4,5},{5,6},{6,7},{7,8},{8,9},{9,10},{10,1... | collective-permute-start | bytes 196616 | tf_op jit(solution)/shard_map/ppermute | solution.py:431
  116.4 9.7 %collective-permute-start.6 = (bf16[8,32,128]{2,1,0:T(8,128)(2,1)S(1)}, bf16[8,32,128]{2,1,0:T(8,128)(2,1)S(1)}, u32[]{:S(2)}, u32[]{:S(2)}) collective-permute-start(bf16[8,32,128]{2,1,0:T(8,128)(2,1)S(1)} %get-tuple-element.36), channel_id=1, source_target_pairs={{0,240},{16,0},{32,16},{48,32},{64,48},{80,64},{96,80},{112,96},{1... | collective-permute-start | bytes 196616 | tf_op jit(solution)/shard_map/ppermute | solution.py:431
  117.2 9.6 %collective-permute-start.7 = (bf16[8,32,128]{2,1,0:T(8,128)(2,1)S(1)}, bf16[8,32,128]{2,1,0:T(8,128)(2,1)S(1)}, u32[]{:S(2)}, u32[]{:S(2)}) collective-permute-start(bf16[8,32,128]{2,1,0:T(8,128)(2,1)S(1)} %get-tuple-element.37), channel_id=1, source_target_pairs={{0,16},{16,32},{32,48},{48,64},{64,80},{80,96},{96,112},{112,128},... | collective-permute-start | bytes 196616 | tf_op jit(solution)/shard_map/ppermute | solution.py:431
  119.2 8.1 %collective-permute-start.9 = (f32[3,8,256]{2,1,0:T(8,128)S(1)}, f32[3,8,256]{2,1,0:T(8,128)S(1)}, u32[]{:S(2)}, u32[]{:S(2)}) collective-permute-start(f32[3,8,256]{2,1,0:T(8,128)S(1)} %get-tuple-element.40.s_own), channel_id=1, source_target_pairs={{0,240},{16,0},{32,16},{48,32},{64,48},{80,64},{96,80},{112,96},{1... | collective-permute-start | bytes 73736 | tf_op jit(solution)/shard_map/ppermute | solution.py:431
  123.1 4.9 %collective-permute-start.8 = (f32[3,8,256]{2,1,0:T(8,128)S(1)}, f32[3,8,256]{2,1,0:T(8,128)S(1)}, u32[]{:S(2)}, u32[]{:S(2)}) collective-permute-start(f32[3,8,256]{2,1,0:T(8,128)S(1)} %get-tuple-element.40.s_own), channel_id=1, source_target_pairs={{0,16},{16,32},{32,48},{48,64},{64,80},{80,96},{96,112},{112,128},... | collective-permute-start | bytes 73736 | tf_op jit(solution)/shard_map/ppermute | solution.py:431
  128.6 1.2 copy-start.9
  129.8 1.2 copy-start.11
  131.1 0.9 copy-start.12
  132.0 0.9 copy-start.18
  133.0 0.8 copy-start.20
  133.8 0.8 copy-start.22
  134.6 0.8 copy-start.24
  135.5 0.8 copy-start.26
  136.3 0.8 copy-start.28
  137.2 0.7 copy-start.33
  137.9 0.7 copy-start.35
  138.6 0.7 copy-start.37
  154.7 1.0 copy-start.7
  157.1 5.4 %collective-permute-start.11 = (bf16[8,32,128]{2,1,0:T(8,128)(2,1)}, bf16[8,32,128]{2,1,0:T(8,128)(2,1)S(1)}, u32[]{:S(2)}, u32[]{:S(2)}) collective-permute-start(bf16[8,32,128]{2,1,0:T(8,128)(2,1)} %get-tuple-element.45), channel_id=1, source_target_pairs={{0,15},{1,0},{2,1},{3,2},{4,3},{5,4},{6,5},{7,6},{8,7},{9,8},{10,9... | collective-permute-start | bytes 196616 | tf_op jit(solution)/shard_map/ppermute | solution.py:431
  157.8 6.6 %collective-permute-start.12 = (bf16[8,32,128]{2,1,0:T(8,128)(2,1)}, bf16[8,32,128]{2,1,0:T(8,128)(2,1)S(1)}, u32[]{:S(2)}, u32[]{:S(2)}) collective-permute-start(bf16[8,32,128]{2,1,0:T(8,128)(2,1)} %get-tuple-element.46), channel_id=1, source_target_pairs={{0,1},{1,2},{2,3},{3,4},{4,5},{5,6},{6,7},{7,8},{8,9},{9,10},{10,1... | collective-permute-start | bytes 196616 | tf_op jit(solution)/shard_map/ppermute | solution.py:431
  158.5 5.9 %collective-permute-start.13 = (bf16[8,32,128]{2,1,0:T(8,128)(2,1)}, bf16[8,32,128]{2,1,0:T(8,128)(2,1)S(1)}, u32[]{:S(2)}, u32[]{:S(2)}) collective-permute-start(bf16[8,32,128]{2,1,0:T(8,128)(2,1)} %get-tuple-element.47), channel_id=1, source_target_pairs={{0,240},{16,0},{32,16},{48,32},{64,48},{80,64},{96,80},{112,96},{1... | collective-permute-start | bytes 196616 | tf_op jit(solution)/shard_map/ppermute | solution.py:431
  161.8 2.6 %collective-permute-start.14 = (bf16[8,32,128]{2,1,0:T(8,128)(2,1)}, bf16[8,32,128]{2,1,0:T(8,128)(2,1)S(1)}, u32[]{:S(2)}, u32[]{:S(2)}) collective-permute-start(bf16[8,32,128]{2,1,0:T(8,128)(2,1)} %get-tuple-element.48), channel_id=1, source_target_pairs={{0,16},{16,32},{32,48},{48,64},{64,80},{80,96},{96,112},{112,128},... | collective-permute-start | bytes 196616 | tf_op jit(solution)/shard_map/ppermute | solution.py:431
  164.4 1.2 copy-start.8
  165.7 0.9 copy-start.15
  166.6 0.9 copy-start.17
  (11 other events, 7.1 us)
Sparse Core Ops, SparseCore 0:
  11.1 52.0 all-gather.1
where the time goes:
time: 184 us; the launch traced here: 181 us
  waiting for transfers between devices  70 us (38%)
  Pallas kernels  34 us (18%)
  starting transfers between devices  32.2 us (18%)
  local copies, waits for them, and re-layouts  30.2 us (16%)
  between operations  14.9 us (8%)
    all_gather x1, waiting for transfers between devices, local(): near_half = lax.all_gather(part, MY, axis=0, tiled=True)  54.4 us
    pallas_call x5, Pallas kernels, call(): pl.pallas_call(kernel, in_specs=[smem] * len(scalars) + [vmem] * len(arra...  34 us
    unnamed x82, local copies, waits for them, and re-layouts  28.1 us
    ppermute x14, starting transfers between devices, shifted(): lax.ppermute(x, axes, [(i, (i + step) % count) for i in range(count)])  16.6 us
    all_to_all x1, starting transfers between devices, local(): partial = lax.all_to_all(partial, MX, 0, 0)  9.76 us
    ppermute x14, waiting for transfers between devices, shifted(): lax.ppermute(x, axes, [(i, (i + step) % count) for i in range(count)])  8.3 us
    all_to_all x1, waiting for transfers between devices, local(): message = lax.all_to_all(message, MY, 0, 0)  7.23 us
    all_to_all x1, starting transfers between devices, local(): message = lax.all_to_all(message, MY, 0, 0)  3.89 us
  transfers between devices with their start and end apart: 18, of which 5 were waited for; matrix products, arithmetic and copies ran while one was open for 1% of the time, Pallas kernels for 7%

commit v1 on v0

--- a/solution.py
+++ b/solution.py
@@ -198,39 +198,45 @@
     lax.fori_loop(0, BLOCKS // 4, some, 0)
 
 
-def first_faces(coords, counts, features, faces, signal, y_own, z_own, p0, p1, p2, p3, work):
+def first_faces(ins, outs, work):
+    features, faces, coords, counts = ins
+    signal, y_own, z_own, *planes = outs
+    base = features.get()
+
     def one(j, carry):
-        signal[j] = silu(features[j].astype(f32)).astype(bf16)
+        signal.ref[j] = silu(base[j].astype(f32)).astype(bf16)
         return carry
 
     lax.fori_loop(0, BLOCKS, one, 0, unroll=4)
-    take_faces(signal, faces, y_own, z_own)
-    fill_planes(coords, counts, y_own, z_own, work, (p0, p1, p2, p3))
-
-
-def first_conv(
-    coords, counts, links, features, signal_in, y_own, z_own, r0, r1, r2, r3,
-    weight, faces, pool, down,
-    level, p0, p1, p2, p3, message,
-    signal, y_bank, z_bank, taps, work, gathered,
-):
-    signal[0:BLOCKS] = signal_in[...]
+    signal.send()
+    take_faces(signal.ref, faces.get(), y_own.ref, z_own.ref)
+    y_own.send()
+    z_own.send()
+    fill_planes(coords.get(), counts.get(), y_own.ref, z_own.ref, work, [p.ref for p in planes])
+
+
+def first_conv(ins, outs, signal, y_bank, z_bank, taps, work, gathered):
+    (coords, counts, links, weights, signal_in, y_own, z_own, *planes, features, faces, pool, down) = ins
+    level, *sent, message = outs
+    coords, counts, links, weight = coords.get(), counts.get(), links.get(), weights.get().at[0]
     signal[BLOCKS] = jnp.zeros((CHANS, VOXELS), bf16)
-    y_bank[0:BLOCKS] = y_own[...]
-    z_bank[0:BLOCKS] = z_own[...]
-    bank_received((r0, r1, r2, r3), y_bank, z_bank)
+    bank_received([p.get() for p in planes], y_bank, z_bank)
+    for one in (signal_in, y_own, z_own):
+        one.get()
+    base = features.get()
+    level_ref = level.ref
 
     def finish(j, result):
-        level[j] = (features[j].astype(f32) + result).astype(bf16)
+        level_ref[j] = (base[j].astype(f32) + result).astype(bf16)
 
     convolve(coords, links, signal, y_bank, z_bank, weight, taps, finish)
-    take_faces(level, faces, y_bank, z_bank)
-    fill_planes(coords, counts, y_bank, z_bank, work, (p0, p1, p2, p3))
+    level.send()
     gathered[...] = jnp.zeros_like(gathered)
     diagonal = channel_diagonal()
+    mean_of = pool.get()
     for i in range(0, BLOCKS, 8):
-        block = level[i : i + 8].reshape(8 * CHANS, VOXELS)
-        means = jnp.dot(block, pool[...], preferred_element_type=f32)
+        block = level_ref[i : i + 8].reshape(8 * CHANS, VOXELS)
+        means = jnp.dot(block, mean_of[...], preferred_element_type=f32)
         for u in range(8):
             j = i + u
             part = jnp.where(diagonal, means[u * CHANS : (u + 1) * CHANS], 0.0)
@@ -238,9 +244,10 @@
             pos = jnp.where(j < counts[0], pos, 8)
             gathered[pos, pl.ds(cell, 1), :] = jnp.sum(part, axis=0, keepdims=True)
     total = jnp.zeros((16, COARSE), f32)
+    rows = down.get()
     for pos in range(8):
         total += jnp.dot(
-            gathered[pos].astype(bf16), down[pos * 256 : pos * 256 + 256], preferred_element_type=f32
+            gathered[pos].astype(bf16), rows[pos * 256 : pos * 256 + 256], preferred_element_type=f32
         )
     total = total[:8]
     mean = jnp.mean(total, axis=0, keepdims=True)
@@ -248,8 +255,11 @@
     row = lax.broadcasted_iota(jnp.int32, (8, COARSE), 0)
     extra = jnp.where(row == 0, mean, jnp.where(row == 1, spread, 0.0))
     for i in range(16):
-        message[i, 0:8] = total
-        message[i, 8:16] = extra
+        message.ref[i, 0:8] = total
+        message.ref[i, 8:16] = extra
+    message.send()
+    take_faces(level_ref, faces.get(), y_bank, z_bank)
+    fill_planes(coords, counts, y_bank, z_bank, work, [p.ref for p in sent])
 
 
 def channel_diagonal():
@@ -269,7 +279,9 @@
     return mean, jnp.sum(spreads + entries * away * away, axis=0, keepdims=True)
 
 
-def row_sums(where, message, partial, strip):
+def row_sums(ins, outs):
+    where, message = (one.get() for one in ins)
+    partial, strip = (one.ref for one in outs)
     mean, spread = merged_sums(message[:, 8, :], message[:, 9, :], 8.0)
     row = lax.broadcasted_iota(jnp.int32, (8, COARSE), 0)
     both = jnp.where(row == 0, mean, jnp.where(row == 1, spread, 0.0))
@@ -290,20 +302,22 @@
 
 
 def second_conv(
-    coords, counts, links, where, level, r0, r1, r2, r3, partial, s_low, s_own, s_high,
-    near_half, far_half, gain, bias, up, weight, faces, spread, y_spread, z_spread, patch, plain,
-    second, signal2, y_own, z_own, p0, p1, p2, p3, coarse,
-    joined, signal, y_bank, z_bank, taps, work, active, raw, patches, lifted, rows,
+    ins, outs, joined, signal, y_bank, z_bank, taps, work, active, raw, patches, lifted, rows
 ):
+    (where, partial, s_low, s_own, s_high, gain, bias, patch, plain, near_half, far_half, up, coords,
+     counts, links, weights, spread, level, faces, y_spread, z_spread, *planes) = ins
+    second, signal2, y_own, z_own, *sent, coarse = outs
+    where, partial = where.get(), partial.get()
     major, minor = where[0], where[1]
     mean, spread_sum = merged_sums(partial[:, 0, :], partial[:, 1, :], 128.0)
     group_mean = group_total(mean) * (1.0 / GROUP)
     away = mean - group_mean
     variance = group_total(spread_sum + 2048.0 * away * away) * (1.0 / (2048 * GROUP))
+    gain, bias = gain.get(), bias.get()
     scale = gain[...] / jnp.sqrt(variance + NORM_EPS)
     active[...] = jnp.zeros_like(active)
     raw[...] = jnp.zeros_like(raw)
-    for dz, strip in enumerate((s_low, s_own, s_high)):
+    for dz, strip in enumerate((s_low.get(), s_own.get(), s_high.get())):
         inside_z = (major + dz >= 1) & (major + dz <= 16)
         for dy in range(3):
             inside = inside_z & (minor + dy >= 1) & (minor + dy <= 16)
@@ -313,11 +327,12 @@
             normed = silu((value - group_mean) * scale + bias[...])
             active[at : at + 8] = jnp.where(inside, normed, 0.0)
     grid = active[...].astype(bf16)
-    cells = jnp.dot(patch[...], grid, preferred_element_type=f32).astype(bf16)
+    cells = jnp.dot(patch.get()[...], grid, preferred_element_type=f32).astype(bf16)
     for t in range(TAPS):
         patches[2 * t] = cells[t * 32 : t * 32 + 32, :128]
         patches[2 * t + 1] = cells[t * 32 : t * 32 + 32, 128:]
     rest = raw[...]
+    plain = plain.get()
     total = jnp.zeros((32, COARSE), f32)
     for _ in range(3):
         high = rest.astype(bf16)
@@ -326,17 +341,23 @@
     core = major & 1
     contract = (((1,), (1,)), ((), ()))
     for half, base in ((near_half, core * TAPS), (far_half, (1 - core) * TAPS)):
+        half = half.get()
         for t in range(TAPS):
             total += lax.dot_general(
                 patches[base + t], half[:, tile(t)], contract, preferred_element_type=f32
             )
     result = total.astype(bf16)
-    coarse[...] = result[0:8]
+    coarse.ref[...] = result[0:8]
+    up = up.get()
     for pos in range(8):
         lifted[pos] = jnp.dot(
             result, up[:, pos * 256 : pos * 256 + 256], preferred_element_type=f32
         )
     diagonal = channel_diagonal()
+    coords, counts, links, weight = coords.get(), counts.get(), links.get(), weights.get().at[1]
+    spread, level, faces = spread.get(), level.get(), faces.get()
+    y_spread, z_spread = y_spread.get(), z_spread.get()
+    r0, r1, r2, r3 = (p.get() for p in planes)
 
     def row_block(pos, cell):
         return jnp.where(diagonal, lifted[pos, pl.ds(cell, 1), :], 0.0).astype(bf16)
@@ -377,44 +398,106 @@
                 merged = (face + term[u * CHANS : (u + 1) * CHANS]).astype(bf16)
                 bank[entry + i + u] = silu(merged.astype(f32)).astype(bf16)
 
+    second_ref, signal2_ref = second.ref, signal2.ref
+
     def finish(j, value):
         out = (joined[j].astype(f32) + value).astype(bf16)
-        second[j] = out
-        signal2[j] = silu(out.astype(f32)).astype(bf16)
+        second_ref[j] = out
+        signal2_ref[j] = silu(out.astype(f32)).astype(bf16)
 
     convolve(coords, links, signal, y_bank, z_bank, weight, taps, finish)
-    take_faces(signal2, faces, y_own, z_own)
-    fill_planes(coords, counts, y_own, z_own, work, (p0, p1, p2, p3))
-
-
-def third_conv(
-    coords, counts, links, second, signal_in, y_own, z_own, r0, r1, r2, r3, weight,
-    out, signal, y_bank, z_bank, taps,
-):
-    signal[0:BLOCKS] = signal_in[...]
+    second.send()
+    signal2.send()
+    take_faces(signal2_ref, faces, y_own.ref, z_own.ref)
+    y_own.send()
+    z_own.send()
+    fill_planes(coords, counts, y_own.ref, z_own.ref, work, [p.ref for p in sent])
+
+
+def third_conv(ins, outs, signal, y_bank, z_bank, taps):
+    (coords, counts, links, weights, signal_in, y_own, z_own, *planes, second) = ins
+    coords, counts, links, weight = coords.get(), counts.get(), links.get(), weights.get().at[2]
     signal[BLOCKS] = jnp.zeros((CHANS, VOXELS), bf16)
-    y_bank[0:BLOCKS] = y_own[...]
-    z_bank[0:BLOCKS] = z_own[...]
-    bank_received((r0, r1, r2, r3), y_bank, z_bank)
+    bank_received([p.get() for p in planes], y_bank, z_bank)
+    for one in (signal_in, y_own, z_own):
+        one.get()
+    base = second.get()
+    out = outs[0].ref
 
     def finish(j, result):
-        value = second[j].astype(f32) + result
+        value = base[j].astype(f32) + result
         out[j] = jnp.where(j < counts[0], value, 0.0).astype(bf16)
 
     convolve(coords, links, signal, y_bank, z_bank, weight, taps, finish)
 
 
-def call(kernel, scalars, arrays, outs, scratch, mebibytes):
-    smem = pl.BlockSpec(memory_space=pltpu.SMEM)
-    vmem = pl.BlockSpec(memory_space=pltpu.VMEM)
+class Arriving:
+    def __init__(self, copy, ref):
+        self.copy, self.ref = copy, ref
+        copy.start()
+
+    def get(self):
+        if self.copy is not None:
+            self.copy.wait()
+            self.copy = None
+        return self.ref
+
+
+class Leaving:
+    def __init__(self, copy, ref):
+        self.copy, self.ref, self.sent = copy, ref, False
+
+    def send(self):
+        self.copy.start()
+        self.sent = True
+
+
+def call(kernel, arrays, outs, scratch, microseconds, spare=()):
+    own = [(i, to) for i, (_, to) in enumerate(arrays) if to is None or to == "smem"]
+    count, total = len(arrays), len(arrays) + len(spare)
+
+    def body(*refs):
+        ins, results = refs[:count], refs[total : total + len(outs)]
+        rest = refs[total + len(outs) :]
+        buffers, rest = rest[: len(own)], rest[len(own) :]
+        staged, rest = rest[: len(outs)], rest[len(outs) :]
+        work, (in_sem, out_sem) = rest[:-2], rest[-2:]
+        placed = {i: buffer for (i, _), buffer in zip(own, buffers)}
+        arriving = []
+        for i, (_, to) in enumerate(arrays):
+            ref = placed[i] if i in placed else to(*work)
+            arriving.append(Arriving(pltpu.make_async_copy(ins[i], ref, in_sem.at[i]), ref))
+        leaving = [
+            Leaving(pltpu.make_async_copy(staged[i], results[i], out_sem.at[i]), staged[i])
+            for i in range(len(outs))
+        ]
+        kernel(arriving, leaving, *work)
+        for one in arriving:
+            one.get()
+        for one in leaving:
+            if not one.sent:
+                one.send()
+        for one in leaving:
+            one.copy.wait()
+
+    hbm = pl.BlockSpec(memory_space=pltpu.HBM)
+    spaces = {None: pltpu.VMEM, "smem": pltpu.SMEM}
+    buffers = [spaces[to](arrays[i][0].shape, arrays[i][0].dtype) for i, to in own]
+    buffers += [pltpu.VMEM(s, d) for s, d in (*outs, *scratch)]
     return pl.pallas_call(
-        kernel,
-        in_specs=[smem] * len(scalars) + [vmem] * len(arrays),
-        out_specs=[vmem] * len(outs),
+        body,
+        in_specs=[hbm] * total,
+        out_specs=[hbm] * len(outs),
         out_shape=[jax.ShapeDtypeStruct(s, d) for s, d in outs],
-        scratch_shapes=[pltpu.VMEM(s, d) for s, d in scratch],
-        compiler_params=pltpu.CompilerParams(vmem_limit_bytes=mebibytes << 20),
-    )(*scalars, *arrays)
+        scratch_shapes=buffers
+        + [pltpu.SemaphoreType.DMA((count,)), pltpu.SemaphoreType.DMA((len(outs),))],
+        compiler_params=pltpu.CompilerParams(vmem_limit_bytes=60 << 20),
+        cost_estimate=pl.CostEstimate(
+            flops=microseconds * 1_000_000_000,
+            bytes_accessed=microseconds * 3_000_000,
+            transcendentals=0,
+        ),
+    )(*[a for a, _ in arrays], *spare)
 
 
 FIELD = ((BLOCKS, CHANS, VOXELS), bf16)
@@ -453,42 +536,52 @@
         coarse_weight.T, lax.axis_index("mx_1") * HALF_ROWS, HALF_ROWS, 1
     )
     near_half = lax.all_gather(part, MY, axis=0, tiled=True)
-    far_half = lax.ppermute(near_half, "mx_1", [(0, 1), (1, 0)])
-
-    signal, y_own, z_own, *planes = call(
-        first_faces, (coords, counts), (features, faces),
-        (FIELD, FACES, FACES) + (PLANE,) * 4, (WORK,), 16,
-    )
+
+    def plainly(*arrays):
+        return tuple((x, None) for x in arrays)
+
+    live = ((coords, "smem"), (counts, "smem"), (neighbours, "smem"))
+    place_own = (
+        lambda signal, *rest: signal.at[0:BLOCKS],
+        lambda signal, y_bank, *rest: y_bank.at[0:BLOCKS],
+        lambda signal, y_bank, z_bank, *rest: z_bank.at[0:BLOCKS],
+    )
+    *own, low_y, high_y, low_z, high_z = call(
+        first_faces, (*plainly(features, faces), *live[:2]),
+        (FIELD, FACES, FACES) + (PLANE,) * 4, (WORK,), 3,
+    )
+    planes = swap_planes((low_y, high_y, low_z, high_z))
+    level, *planes, message = call(
+        first_conv,
+        (*live, (fine_weights, None), *zip(own, place_own), *plainly(*planes, features, faces, pool, down_weight)),
+        (FIELD,) + (PLANE,) * 4 + (((16, 16, COARSE), f32),),
+        (SIGNAL, BANK, BANK, TAP_STACK, WORK, ((9, 16, COARSE), f32)), 9,
+    )
+    message = lax.all_to_all(message, MY, 0, 0)
     planes = swap_planes(planes)
-    level, *planes, message = call(
-        first_conv, (coords, counts, neighbours),
-        (features, signal, y_own, z_own, *planes, fine_weights[0], faces, pool, down_weight),
-        (FIELD,) + (PLANE,) * 4 + (((16, 16, COARSE), f32),),
-        (SIGNAL, BANK, BANK, TAP_STACK, WORK, ((9, 16, COARSE), f32)), 24,
-    )
-    message = lax.all_to_all(message, MY, 0, 0)
     partial, strip = call(
-        row_sums, (where,), (message,),
-        (((16, 8, COARSE), f32), ((3, 8, COARSE), f32)), (), 8,
-    )
+        row_sums, ((where, "smem"), (message, None)),
+        (((16, 8, COARSE), f32), ((3, 8, COARSE), f32)), (), 1, planes,
+    )
+    partial = lax.all_to_all(partial, MX, 0, 0)
     strip_low = shifted(strip, MX, 1)
     strip_high = shifted(strip, MX, -1)
-    planes = swap_planes(planes)
-    partial = lax.all_to_all(partial, MX, 0, 0)
-    second, signal, y_own, z_own, *planes, coarse = call(
-        second_conv, (coords, counts, neighbours, where),
-        (level, *planes, partial, strip_low, strip, strip_high, near_half, far_half,
-         norm_gain.reshape(1, COARSE), norm_bias.reshape(1, COARSE), up_weight, fine_weights[1],
-         faces, spread, y_spread, z_spread, patch, plain),
+    near_half, strip_low = lax.optimization_barrier((near_half, strip_low))
+    far_half = lax.ppermute(near_half, "mx_1", [(0, 1), (1, 0)])
+    second, *own, low_y, high_y, low_z, high_z, coarse = call(
+        second_conv,
+        ((where, "smem"),
+         *plainly(partial, strip_low, strip, strip_high, norm_gain.reshape(1, COARSE),
+                  norm_bias.reshape(1, COARSE), patch, plain, near_half, far_half, up_weight),
+         *live, *plainly(fine_weights, spread, level, faces, y_spread, z_spread, *planes)),
         (FIELD, FIELD, FACES, FACES) + (PLANE,) * 4 + (((8, COARSE), bf16),),
         (FIELD, SIGNAL, BANK, BANK, TAP_STACK, WORK, ((128, COARSE), f32), ((128, COARSE), f32),
-         ((2 * TAPS, 32, 128), bf16), ((8, 32, COARSE), f32), ((256, 256), bf16)), 32,
-    )
-    planes = swap_planes(planes)
+         ((2 * TAPS, 32, 128), bf16), ((8, 32, COARSE), f32), ((256, 256), bf16)), 14,
+    )
+    planes = swap_planes((low_y, high_y, low_z, high_z))
     (fine_out,) = call(
-        third_conv, (coords, counts, neighbours),
-        (second, signal, y_own, z_own, *planes, fine_weights[2]),
-        (FIELD,), (SIGNAL, BANK, BANK, TAP_STACK), 24,
+        third_conv, (*live, (fine_weights, None), *zip(own, place_own), *plainly(*planes, second)),
+        (FIELD,), (SIGNAL, BANK, BANK, TAP_STACK), 7,
     )
     return fine_out, coarse.reshape(2, 2, 2, COARSE)
 

time: 184 us -> 123 us (0.67); the launches traced: 181 us -> 122 us
  waiting for transfers between devices: 70 us -> 25.1 us
  local copies, waits for them, and re-layouts: 30.2 us -> 6.65 us
  starting transfers between devices: 32.2 us -> 36.8 us
  Pallas kernels: 34 us -> 38.4 us
    all_gather x1, waiting for transfers between devices: 54.4 us -> 0.01 us  [local(): near_half = lax.all_gather(part, MY, axis=0, tiled=True)]
    unnamed x82 -> x36, local copies, waits for them, and re-layouts: 28.1 us -> 4.73 us
    ppermute x14, waiting for transfers between devices: 8.3 us -> 21.8 us  [shifted(): lax.ppermute(x, axes, [(i, (i + step) % count) for i in range(count)])]
    all_to_all x1, waiting for transfers between devices: 7.23 us -> 0.01 us  [local(): message = lax.all_to_all(message, MY, 0, 0)]
    ppermute x14, starting transfers between devices: 16.6 us -> 22.7 us  [shifted(): lax.ppermute(x, axes, [(i, (i + step) % count) for i in range(count)])]
    all_to_all x1, starting transfers between devices: 9.76 us -> 4.09 us  [local(): partial = lax.all_to_all(partial, MX, 0, 0)]
    pallas_call x5, Pallas kernels: 34 us -> 38.4 us  [call(): pl.pallas_call(body, in_specs=[hbm] * total, out_specs=[hbm] * len(outs),...]
    all_to_all x1, waiting for transfers between devices: 0.01 us -> 3.26 us  [local(): partial = lax.all_to_all(partial, MX, 0, 0)]
  transfers between devices with their start and end apart: 18 -> 18, of which waited for: 5 -> 7; matrix products, arithmetic and copies ran while one was open for 1% -> 2% of each run, Pallas kernels for 7% -> 13%
where the time goes in v1:
time: 123 us; the launch traced here: 122 us
  Pallas kernels  38.4 us (31%)
  starting transfers between devices  36.8 us (30%)
  waiting for transfers between devices  25.1 us (20%)
  between operations  14.8 us (12%)
  local copies, waits for them, and re-layouts  6.65 us (5%)
    pallas_call x5, Pallas kernels, call(): pl.pallas_call(body, in_specs=[hbm] * total, out_specs=[hbm] * len(outs),...  38.4 us
    ppermute x14, starting transfers between devices, shifted(): lax.ppermute(x, axes, [(i, (i + step) % count) for i in range(count)])  22.7 us
    ppermute x14, waiting for transfers between devices, shifted(): lax.ppermute(x, axes, [(i, (i + step) % count) for i in range(count)])  21.8 us
    all_to_all x1, starting transfers between devices, local(): message = lax.all_to_all(message, MY, 0, 0)  6.18 us
    unnamed x36, local copies, waits for them, and re-layouts  4.73 us
    all_to_all x1, starting transfers between devices, local(): partial = lax.all_to_all(partial, MX, 0, 0)  4.09 us
    ppermute x1, starting transfers between devices, local(): far_half = lax.ppermute(near_half, 'mx_1', [(0, 1), (1, 0)])  3.77 us
    all_to_all x1, waiting for transfers between devices, local(): partial = lax.all_to_all(partial, MX, 0, 0)  3.26 us
  transfers between devices with their start and end apart: 18, of which 7 were waited for; matrix products, arithmetic and copies ran while one was open for 2% of the time, Pallas kernels for 13%

profile of v1, /device:TPU:1, one launch (start us, length us, event | category | flops | bytes accessed | tf_op | source)
XLA Modules:
  0.0 122.4 jit_solution(16377216076468770357)
XLA Ops:
  7.2 0.0 copy-start
  7.2 0.0 all-gather.2.cloned.1.call-start
  7.2 0.9 copy-done
  8.1 0.6 dynamic-slice_bitcast_fusion
  8.8 0.0 all-gather.2.cloned.1.call-update
  9.4 4.3 %shard_map.176 = (bf16[32,32,512]{2,1,0:T(8,128)(2,1)}, bf16[32,32,128]{2,1,0:T(8,128)(2,1)}, bf16[32,32,128]{2,1,0:T(8,128)(2,1)}, bf16[8,32,128]{2,1,0:T(8,128...) custom-call(bf16[32,32,512]{2,1,0:T(8,128)(2,1)} %refs_11_.2, ...), custom_call_target="tpu_custom_call" | custom-call | flops 3000000000 | bytes 9000000 | tf_op jit(solution)/shard_map/pallas_call | solution.py:487
  13.7 5.8 %collective-permute-start = (bf16[8,32,128]{2,1,0:T(8,128)(2,1)}, bf16[8,32,128]{2,1,0:T(8,128)(2,1)S(1)}, u32[]{:S(2)}, u32[]{:S(2)}) collective-permute-start(bf16[8,32,128]{2,1,0:T(8,128)(2,1)} %get-tuple-element.31), channel_id=1, source_target_pairs={{0,15},{1,0},{2,1},{3,2},{4,3},{5,4},{6,5},{7,6},{8,7},{9,8},{10,9... | collective-permute-start | bytes 196616 | tf_op jit(solution)/shard_map/ppermute | solution.py:514
  19.6 0.0 collective-permute-start.1
  19.6 1.0 collective-permute-start.2
  20.5 1.5 %collective-permute-start.3 = (bf16[8,32,128]{2,1,0:T(8,128)(2,1)}, bf16[8,32,128]{2,1,0:T(8,128)(2,1)S(1)}, u32[]{:S(2)}, u32[]{:S(2)}) collective-permute-start(bf16[8,32,128]{2,1,0:T(8,128)(2,1)} %get-tuple-element.34), channel_id=1, source_target_pairs={{0,16},{16,32},{32,48},{48,64},{64,80},{80,96},{96,112},{112,128},... | collective-permute-start | bytes 196616 | tf_op jit(solution)/shard_map/ppermute | solution.py:514
  22.0 4.2 %collective-permute-done.1.refs_8_ = bf16[8,32,128]{2,1,0:T(8,128)(2,1)S(1)} collective-permute-done((bf16[8,32,128]{2,1,0:T(8,128)(2,1)}, bf16[8,32,128]{2,1,0:T(8,128)(2,1)S(1)}, u32[]{:S(2)}, u32[]{:S(2)}) %collective-permute-start.1) | collective-permute-done | bytes 65568 | tf_op jit(solution)/shard_map/ppermute | solution.py:514
  26.2 0.0 collective-permute-done.2.refs_9_
  26.2 0.3 collective-permute-done.3.refs_10_
  26.5 0.3 copy-done.9
  26.8 0.0 copy-done.11
  26.9 0.2 copy-done.13
  27.1 10.4 %shard_map.177 = (bf16[32,32,512]{2,1,0:T(8,128)(2,1)}, bf16[8,32,128]{2,1,0:T(8,128)(2,1)}, bf16[8,32,128]{2,1,0:T(8,128)(2,1)}, bf16[8,32,128]{2,1,0:T(8,128)(...) custom-call(s32[3,32]{1,0:T(4,128)} %refs_0_.5, s32[1]{0:T(128)S(6)} %copy.19.refs_3_.refs_1_.refs_13_, ...), custom_call_target="tpu_custom_call" | custom-call | flops 8999999488 | bytes 27000000 | tf_op jit(solution)/shard_map/pallas_call | solution.py:487
  37.5 6.2 %all-to-all-start = ((f32[16,16,256]{2,1,0:T(8,128)}), f32[16,16,256]{2,1,0:T(8,128)S(1)}, u32[]{:S(2)}, u32[]{:S(2)}) async-start(f32[16,16,256]{2,1,0:T(8,128)} %get-tuple-element.35), calls=%async_computation | async-start | bytes 524288 | tf_op jit(solution)/shard_map/all_to_all | solution.py:560
  43.7 4.7 %collective-permute-start.4 = (bf16[8,32,128]{2,1,0:T(8,128)(2,1)}, bf16[8,32,128]{2,1,0:T(8,128)(2,1)S(1)}, u32[]{:S(2)}, u32[]{:S(2)}) collective-permute-start(bf16[8,32,128]{2,1,0:T(8,128)(2,1)} %get-tuple-element.36), channel_id=1, source_target_pairs={{0,15},{1,0},{2,1},{3,2},{4,3},{5,4},{6,5},{7,6},{8,7},{9,8},{10,9... | collective-permute-start | bytes 196616 | tf_op jit(solution)/shard_map/ppermute | solution.py:514
  48.4 0.0 collective-permute-start.5
  48.4 5.0 %collective-permute-start.6 = (bf16[8,32,128]{2,1,0:T(8,128)(2,1)}, bf16[8,32,128]{2,1,0:T(8,128)(2,1)S(1)}, u32[]{:S(2)}, u32[]{:S(2)}) collective-permute-start(bf16[8,32,128]{2,1,0:T(8,128)(2,1)} %get-tuple-element.38), channel_id=1, source_target_pairs={{0,240},{16,0},{32,16},{48,32},{64,48},{80,64},{96,80},{112,96},{1... | collective-permute-start | bytes 196616 | tf_op jit(solution)/shard_map/ppermute | solution.py:514
  53.4 0.6 pad_add_fusion.refs_0_
  54.0 3.3 %collective-permute-done.5.refs_3_.refs_22_ = bf16[8,32,128]{2,1,0:T(8,128)(2,1)S(1)} collective-permute-done((bf16[8,32,128]{2,1,0:T(8,128)(2,1)}, bf16[8,32,128]{2,1,0:T(8,128)(2,1)S(1)}, u32[]{:S(2)}, u32[]{:S(2)}) %collective-permute-start.5) | collective-permute-done | bytes 65568 | tf_op jit(solution)/shard_map/ppermute | solution.py:514
  57.4 0.6 copy-done.5
  57.9 0.0 copy-done.6
  58.0 0.0 copy-done.7
  58.0 0.7 copy-done.1
  58.7 1.7 %shard_map.178 = (f32[16,8,256]{2,1,0:T(8,128)}, f32[3,8,256]{2,1,0:T(8,128)}) custom-call(s32[2]{0:T(128)} %pad_add_fusion.refs_0_, f32[16,16,256]{2,1,0:T(8,128)} %copy-done.1, bf16[8,32,128]{2,1,0:T(8,128)(2,1)} %copy-done.4, bf16[8,32,128]{2,1,0:T(8,128)(2,1)} %copy-done.5, bf16[8,32,128]{2,1,0:T(8,128)(2,1)} %copy-done.6, bf16[8,32,128]{2,1,0:T(8,128)(2,1)} %copy-done.7), custom_call_target="tpu_custom_call" | custom-call | flops 1000000000 | bytes 3000000 | tf_op jit(solution)/shard_map/pallas_call | solution.py:487
  60.4 1.4 %collective-permute-start.8 = (f32[3,8,256]{2,1,0:T(8,128)}, f32[3,8,256]{2,1,0:T(8,128)S(1)}, u32[]{:S(2)}, u32[]{:S(2)}) collective-permute-start(f32[3,8,256]{2,1,0:T(8,128)} %get-tuple-element.41.refs_3_), channel_id=1, source_target_pairs={{0,16},{16,32},{32,48},{48,64},{64,80},{80,96},{96,112},{112,128},... | collective-permute-start | bytes 73736 | tf_op jit(solution)/shard_map/ppermute | solution.py:514
  61.8 4.2 %collective-permute-done.8.refs_2_ = f32[3,8,256]{2,1,0:T(8,128)S(1)} collective-permute-done((f32[3,8,256]{2,1,0:T(8,128)}, f32[3,8,256]{2,1,0:T(8,128)S(1)}, u32[]{:S(2)}, u32[]{:S(2)}) %collective-permute-start.8) | collective-permute-done | bytes 24608 | tf_op jit(solution)/shard_map/ppermute | solution.py:514
  66.0 3.8 %collective-permute-start.10 = (bf16[256,3456]{1,0:T(8,128)(2,1)}, bf16[256,3456]{1,0:T(8,128)(2,1)S(1)}, u32[]{:S(2)}, u32[]{:S(2)}) collective-permute-start(bf16[256,3456]{1,0:T(8,128)(2,1)} %all-gather.2.cloned.1.call-done.refs_9_), channel_id=1, source_target_pairs={{0,16},{16,0},{1,17},{17,1},{2,18},{18,2},{3,19},{19,3},{4,20},{20... | collective-permute-start | bytes 5308424 | tf_op jit(solution)/shard_map/ppermute | solution.py:570
  69.8 4.1 %all-to-all-start.1 = ((f32[16,8,256]{2,1,0:T(8,128)}), f32[16,8,256]{2,1,0:T(8,128)S(1)}, u32[]{:S(2)}, u32[]{:S(2)}) async-start(f32[16,8,256]{2,1,0:T(8,128)} %get-tuple-element.40), calls=%async_computation.1 | async-start | bytes 262144 | tf_op jit(solution)/shard_map/all_to_all | solution.py:566
  73.8 0.1 collective-permute-start.9
  74.0 5.8 %collective-permute-done.9.refs_4_ = f32[3,8,256]{2,1,0:T(8,128)S(1)} collective-permute-done((f32[3,8,256]{2,1,0:T(8,128)}, f32[3,8,256]{2,1,0:T(8,128)S(1)}, u32[]{:S(2)}, u32[]{:S(2)}) %collective-permute-start.9) | collective-permute-done | bytes 24608 | tf_op jit(solution)/shard_map/ppermute | solution.py:514
  79.8 3.3 %all-to-all-done.1.refs_1_ = f32[16,8,256]{2,1,0:T(8,128)S(1)} async-done(((f32[16,8,256]{2,1,0:T(8,128)}), f32[16,8,256]{2,1,0:T(8,128)S(1)}, u32[]{:S(2)}, u32[]{:S(2)}) %all-to-all-start.1) | async-done | bytes 131104 | tf_op jit(solution)/shard_map/all_to_all | solution.py:566
  83.0 0.6 copy-done.2
  83.7 0.6 copy-done.3
  84.3 14.0 %shard_map.179 = (bf16[32,32,512]{2,1,0:T(8,128)(2,1)}, bf16[32,32,512]{2,1,0:T(8,128)(2,1)}, bf16[32,32,128]{2,1,0:T(8,128)(2,1)}, bf16[32,32,128]{2,1,0:T(8,12...) custom-call(s32[2]{0:T(128)} %pad_add_fusion.refs_0_, ...), custom_call_target="tpu_custom_call" | custom-call | flops 14000000000 | bytes 42000000 | tf_op jit(solution)/shard_map/pallas_call | solution.py:487
  98.3 1.3 %collective-permute-start.11 = (bf16[8,32,128]{2,1,0:T(8,128)(2,1)}, bf16[8,32,128]{2,1,0:T(8,128)(2,1)S(1)}, u32[]{:S(2)}, u32[]{:S(2)}) collective-permute-start(bf16[8,32,128]{2,1,0:T(8,128)(2,1)} %get-tuple-element.48), channel_id=1, source_target_pairs={{0,15},{1,0},{2,1},{3,2},{4,3},{5,4},{6,5},{7,6},{8,7},{9,8},{10,9... | collective-permute-start | bytes 196616 | tf_op jit(solution)/shard_map/ppermute | solution.py:514
  99.6 0.2 collective-permute-start.12
  99.8 0.2 collective-permute-start.13
  100.1 1.5 %collective-permute-start.14 = (bf16[8,32,128]{2,1,0:T(8,128)(2,1)}, bf16[8,32,128]{2,1,0:T(8,128)(2,1)S(1)}, u32[]{:S(2)}, u32[]{:S(2)}) collective-permute-start(bf16[8,32,128]{2,1,0:T(8,128)(2,1)} %get-tuple-element.51), channel_id=1, source_target_pairs={{0,16},{16,32},{32,48},{48,64},{64,80},{80,96},{96,112},{112,128},... | collective-permute-start | bytes 196616 | tf_op jit(solution)/shard_map/ppermute | solution.py:514
  101.6 1.3 %reshape.15 = bf16[2,2,2,256]{3,2,1,0:T(2,128)(2,1)} reshape(bf16[8,256]{1,0:T(8,128)(2,1)} %get-tuple-element.53) | data formatting | bytes 8192 | tf_op jit(solution)/shard_map/reshape | solution.py:586
  102.9 4.1 %collective-permute-done.12.refs_8_ = bf16[8,32,128]{2,1,0:T(8,128)(2,1)S(1)} collective-permute-done((bf16[8,32,128]{2,1,0:T(8,128)(2,1)}, bf16[8,32,128]{2,1,0:T(8,128)(2,1)S(1)}, u32[]{:S(2)}, u32[]{:S(2)}) %collective-permute-start.12) | collective-permute-done | bytes 65568 | tf_op jit(solution)/shard_map/ppermute | solution.py:514
  107.0 0.6 copy-done.12
  107.6 0.0 copy-done.14
  107.6 0.0 copy-done.15
  107.6 8.0 %shard_map.180 = bf16[32,32,512]{2,1,0:T(8,128)(2,1)} custom-call(s32[3,32]{1,0:T(4,128)} %refs_0_.5, s32[1]{0:T(128)S(6)} %copy.19.refs_3_.refs_1_.refs_13_, s32[6,32]{1,0:T(8,128)} %refs_2_.5, bf16[3,32,224]{2,1,0:T(8,128)(2,1)} %refs_3_.4, bf16[32,32,512]{2,1,0:T(8,128)(2,1)} %get-tuple-element.45.refs_4_, ...), custom_call_target="tpu_custom_call" | custom-call | flops 7000000000 | bytes 21000000 | tf_op jit(solution)/shard_map/pallas_call | solution.py:487
  (33 shorter events, 0.1 us)
Async XLA Ops:
  7.2 0.9 copy-start
  7.2 58.8 %all-gather.2.cloned.1.call-start = ((), (), s32[]{:S(2)}) async-start(), calls=%async_computation.2 | async-start | bytes 1880064 | tf_op jit(solution)/shard_map/all_gather | solution.py:538
  13.7 8.3 %collective-permute-start = (bf16[8,32,128]{2,1,0:T(8,128)(2,1)}, bf16[8,32,128]{2,1,0:T(8,128)(2,1)S(1)}, u32[]{:S(2)}, u32[]{:S(2)}) collective-permute-start(bf16[8,32,128]{2,1,0:T(8,128)(2,1)} %get-tuple-element.31), channel_id=1, source_target_pairs={{0,15},{1,0},{2,1},{3,2},{4,3},{5,4},{6,5},{7,6},{8,7},{9,8},{10,9... | collective-permute-start | bytes 196616 | tf_op jit(solution)/shard_map/ppermute | solution.py:514
  19.6 6.6 %collective-permute-start.1 = (bf16[8,32,128]{2,1,0:T(8,128)(2,1)}, bf16[8,32,128]{2,1,0:T(8,128)(2,1)S(1)}, u32[]{:S(2)}, u32[]{:S(2)}) collective-permute-start(bf16[8,32,128]{2,1,0:T(8,128)(2,1)} %get-tuple-element.32), channel_id=1, source_target_pairs={{0,1},{1,2},{2,3},{3,4},{4,5},{5,6},{6,7},{7,8},{8,9},{9,10},{10,1... | collective-permute-start | bytes 196616 | tf_op jit(solution)/shard_map/ppermute | solution.py:514
  19.6 6.6 %collective-permute-start.2 = (bf16[8,32,128]{2,1,0:T(8,128)(2,1)}, bf16[8,32,128]{2,1,0:T(8,128)(2,1)S(1)}, u32[]{:S(2)}, u32[]{:S(2)}) collective-permute-start(bf16[8,32,128]{2,1,0:T(8,128)(2,1)} %get-tuple-element.33), channel_id=1, source_target_pairs={{0,240},{16,0},{32,16},{48,32},{64,48},{80,64},{96,80},{112,96},{1... | collective-permute-start | bytes 196616 | tf_op jit(solution)/shard_map/ppermute | solution.py:514
  20.5 6.0 %collective-permute-start.3 = (bf16[8,32,128]{2,1,0:T(8,128)(2,1)}, bf16[8,32,128]{2,1,0:T(8,128)(2,1)S(1)}, u32[]{:S(2)}, u32[]{:S(2)}) collective-permute-start(bf16[8,32,128]{2,1,0:T(8,128)(2,1)} %get-tuple-element.34), channel_id=1, source_target_pairs={{0,16},{16,32},{32,48},{48,64},{64,80},{80,96},{96,112},{112,128},... | collective-permute-start | bytes 196616 | tf_op jit(solution)/shard_map/ppermute | solution.py:514
  22.0 4.4 %copy-start.8 = (bf16[8,32,128]{2,1,0:T(8,128)(2,1)}, bf16[8,32,128]{2,1,0:T(8,128)(2,1)S(1)}, u32[]{:S(2)}) copy-start(bf16[8,32,128]{2,1,0:T(8,128)(2,1)S(1)} %collective-permute-done.refs_7_) | copy-start | bytes 196612
  26.2 0.6 copy-start.9
  26.2 0.6 copy-start.11
  26.5 0.6 copy-start.13
  37.5 19.8 %all-to-all-start = ((f32[16,16,256]{2,1,0:T(8,128)}), f32[16,16,256]{2,1,0:T(8,128)S(1)}, u32[]{:S(2)}, u32[]{:S(2)}) async-start(f32[16,16,256]{2,1,0:T(8,128)} %get-tuple-element.35), calls=%async_computation | async-start | bytes 524288 | tf_op jit(solution)/shard_map/all_to_all | solution.py:560
  43.7 10.3 %collective-permute-start.4 = (bf16[8,32,128]{2,1,0:T(8,128)(2,1)}, bf16[8,32,128]{2,1,0:T(8,128)(2,1)S(1)}, u32[]{:S(2)}, u32[]{:S(2)}) collective-permute-start(bf16[8,32,128]{2,1,0:T(8,128)(2,1)} %get-tuple-element.36), channel_id=1, source_target_pairs={{0,15},{1,0},{2,1},{3,2},{4,3},{5,4},{6,5},{7,6},{8,7},{9,8},{10,9... | collective-permute-start | bytes 196616 | tf_op jit(solution)/shard_map/ppermute | solution.py:514
  48.4 8.9 %collective-permute-start.5 = (bf16[8,32,128]{2,1,0:T(8,128)(2,1)}, bf16[8,32,128]{2,1,0:T(8,128)(2,1)S(1)}, u32[]{:S(2)}, u32[]{:S(2)}) collective-permute-start(bf16[8,32,128]{2,1,0:T(8,128)(2,1)} %get-tuple-element.37), channel_id=1, source_target_pairs={{0,1},{1,2},{2,3},{3,4},{4,5},{5,6},{6,7},{7,8},{8,9},{9,10},{10,1... | collective-permute-start | bytes 196616 | tf_op jit(solution)/shard_map/ppermute | solution.py:514
  48.4 8.9 %collective-permute-start.6 = (bf16[8,32,128]{2,1,0:T(8,128)(2,1)}, bf16[8,32,128]{2,1,0:T(8,128)(2,1)S(1)}, u32[]{:S(2)}, u32[]{:S(2)}) collective-permute-start(bf16[8,32,128]{2,1,0:T(8,128)(2,1)} %get-tuple-element.38), channel_id=1, source_target_pairs={{0,240},{16,0},{32,16},{48,32},{64,48},{80,64},{96,80},{112,96},{1... | collective-permute-start | bytes 196616 | tf_op jit(solution)/shard_map/ppermute | solution.py:514
  53.4 4.0 %collective-permute-start.7 = (bf16[8,32,128]{2,1,0:T(8,128)(2,1)}, bf16[8,32,128]{2,1,0:T(8,128)(2,1)S(1)}, u32[]{:S(2)}, u32[]{:S(2)}) collective-permute-start(bf16[8,32,128]{2,1,0:T(8,128)(2,1)} %get-tuple-element.39), channel_id=1, source_target_pairs={{0,16},{16,32},{32,48},{48,64},{64,80},{80,96},{96,112},{112,128},... | collective-permute-start | bytes 196616 | tf_op jit(solution)/shard_map/ppermute | solution.py:514
  54.0 3.4 %copy-start.4 = (bf16[8,32,128]{2,1,0:T(8,128)(2,1)}, bf16[8,32,128]{2,1,0:T(8,128)(2,1)S(1)}, u32[]{:S(2)}) copy-start(bf16[8,32,128]{2,1,0:T(8,128)(2,1)S(1)} %collective-permute-done.4.refs_2_.refs_21_) | copy-start | bytes 196612
  57.3 0.6 copy-start.5
  57.3 0.6 copy-start.6
  57.3 0.7 copy-start.7
  58.0 0.7 copy-start.1
  60.4 5.6 %collective-permute-start.8 = (f32[3,8,256]{2,1,0:T(8,128)}, f32[3,8,256]{2,1,0:T(8,128)S(1)}, u32[]{:S(2)}, u32[]{:S(2)}) collective-permute-start(f32[3,8,256]{2,1,0:T(8,128)} %get-tuple-element.41.refs_3_), channel_id=1, source_target_pairs={{0,16},{16,32},{32,48},{48,64},{64,80},{80,96},{96,112},{112,128},... | collective-permute-start | bytes 73736 | tf_op jit(solution)/shard_map/ppermute | solution.py:514
  66.0 17.0 %copy-start.16 = (f32[3,8,256]{2,1,0:T(8,128)}, f32[3,8,256]{2,1,0:T(8,128)S(1)}, u32[]{:S(2)}) copy-start(f32[3,8,256]{2,1,0:T(8,128)S(1)} %collective-permute-done.8.refs_2_) | copy-start | bytes 73732
  66.0 17.0 %collective-permute-start.10 = (bf16[256,3456]{1,0:T(8,128)(2,1)}, bf16[256,3456]{1,0:T(8,128)(2,1)S(1)}, u32[]{:S(2)}, u32[]{:S(2)}) collective-permute-start(bf16[256,3456]{1,0:T(8,128)(2,1)} %all-gather.2.cloned.1.call-done.refs_9_), channel_id=1, source_target_pairs={{0,16},{16,0},{1,17},{17,1},{2,18},{18,2},{3,19},{19,3},{4,20},{20... | collective-permute-start | bytes 5308424 | tf_op jit(solution)/shard_map/ppermute | solution.py:570
  69.8 13.3 %all-to-all-start.1 = ((f32[16,8,256]{2,1,0:T(8,128)}), f32[16,8,256]{2,1,0:T(8,128)S(1)}, u32[]{:S(2)}, u32[]{:S(2)}) async-start(f32[16,8,256]{2,1,0:T(8,128)} %get-tuple-element.40), calls=%async_computation.1 | async-start | bytes 262144 | tf_op jit(solution)/shard_map/all_to_all | solution.py:566
  73.8 5.9 %collective-permute-start.9 = (f32[3,8,256]{2,1,0:T(8,128)}, f32[3,8,256]{2,1,0:T(8,128)S(1)}, u32[]{:S(2)}, u32[]{:S(2)}) collective-permute-start(f32[3,8,256]{2,1,0:T(8,128)} %get-tuple-element.41.refs_3_), channel_id=1, source_target_pairs={{0,240},{16,0},{32,16},{48,32},{64,48},{80,64},{96,80},{112,96},{1... | collective-permute-start | bytes 73736 | tf_op jit(solution)/shard_map/ppermute | solution.py:514
  79.7 3.3 %copy-start.17 = (f32[3,8,256]{2,1,0:T(8,128)}, f32[3,8,256]{2,1,0:T(8,128)S(1)}, u32[]{:S(2)}) copy-start(f32[3,8,256]{2,1,0:T(8,128)S(1)} %collective-permute-done.9.refs_4_) | copy-start | bytes 73732
  83.0 0.7 copy-start.2
  83.0 1.2 %copy-start.3 = (bf16[256,3456]{1,0:T(8,128)(2,1)}, bf16[256,3456]{1,0:T(8,128)(2,1)S(1)}, u32[]{:S(2)}) copy-start(bf16[256,3456]{1,0:T(8,128)(2,1)S(1)} %collective-permute-done.10.refs_10_) | copy-start | bytes 5308420
  98.3 4.6 %collective-permute-start.11 = (bf16[8,32,128]{2,1,0:T(8,128)(2,1)}, bf16[8,32,128]{2,1,0:T(8,128)(2,1)S(1)}, u32[]{:S(2)}, u32[]{:S(2)}) collective-permute-start(bf16[8,32,128]{2,1,0:T(8,128)(2,1)} %get-tuple-element.48), channel_id=1, source_target_pairs={{0,15},{1,0},{2,1},{3,2},{4,3},{5,4},{6,5},{7,6},{8,7},{9,8},{10,9... | collective-permute-start | bytes 196616 | tf_op jit(solution)/shard_map/ppermute | solution.py:514
  99.6 7.3 %collective-permute-start.12 = (bf16[8,32,128]{2,1,0:T(8,128)(2,1)}, bf16[8,32,128]{2,1,0:T(8,128)(2,1)S(1)}, u32[]{:S(2)}, u32[]{:S(2)}) collective-permute-start(bf16[8,32,128]{2,1,0:T(8,128)(2,1)} %get-tuple-element.49), channel_id=1, source_target_pairs={{0,1},{1,2},{2,3},{3,4},{4,5},{5,6},{6,7},{7,8},{8,9},{9,10},{10,1... | collective-permute-start | bytes 196616 | tf_op jit(solution)/shard_map/ppermute | solution.py:514
  99.8 7.1 %collective-permute-start.13 = (bf16[8,32,128]{2,1,0:T(8,128)(2,1)}, bf16[8,32,128]{2,1,0:T(8,128)(2,1)S(1)}, u32[]{:S(2)}, u32[]{:S(2)}) collective-permute-start(bf16[8,32,128]{2,1,0:T(8,128)(2,1)} %get-tuple-element.50), channel_id=1, source_target_pairs={{0,240},{16,0},{32,16},{48,32},{64,48},{80,64},{96,80},{112,96},{1... | collective-permute-start | bytes 196616 | tf_op jit(solution)/shard_map/ppermute | solution.py:514
  100.1 6.9 %collective-permute-start.14 = (bf16[8,32,128]{2,1,0:T(8,128)(2,1)}, bf16[8,32,128]{2,1,0:T(8,128)(2,1)S(1)}, u32[]{:S(2)}, u32[]{:S(2)}) collective-permute-start(bf16[8,32,128]{2,1,0:T(8,128)(2,1)} %get-tuple-element.51), channel_id=1, source_target_pairs={{0,16},{16,32},{32,48},{48,64},{64,80},{80,96},{96,112},{112,128},... | collective-permute-start | bytes 196616 | tf_op jit(solution)/shard_map/ppermute | solution.py:514
  102.9 4.1 %copy-start.10 = (bf16[8,32,128]{2,1,0:T(8,128)(2,1)}, bf16[8,32,128]{2,1,0:T(8,128)(2,1)S(1)}, u32[]{:S(2)}) copy-start(bf16[8,32,128]{2,1,0:T(8,128)(2,1)S(1)} %collective-permute-done.11.refs_7_) | copy-start | bytes 196612
  106.9 0.6 copy-start.12
  106.9 0.6 copy-start.14
  106.9 0.7 copy-start.15
Sparse Core Ops, SparseCore 0:
  10.5 53.7 all-gather.1

commit v2 on v1

--- a/solution.py
+++ b/solution.py
@@ -122,7 +122,7 @@
 
     lax.fori_loop(0, BLOCKS, one, 0, unroll=4)
     for plane, out in enumerate(outs):
-        out[...] = work[plane, :8]
+        out[0:8] = work[plane, :8]
 
 
 def received(plane_ref, p, back):
@@ -200,24 +200,51 @@
 
 def first_faces(ins, outs, work):
     features, faces, coords, counts = ins
-    signal, y_own, z_own, *planes = outs
-    base = features.get()
-
-    def one(j, carry):
-        signal.ref[j] = silu(base[j].astype(f32)).astype(bf16)
-        return carry
-
-    lax.fori_loop(0, BLOCKS, one, 0, unroll=4)
-    signal.send()
-    take_faces(signal.ref, faces.get(), y_own.ref, z_own.ref)
+    y_own, z_own, *planes = outs
+    base, faces = features.get(), faces.get()
+    for i in range(0, BLOCKS, 8):
+        block = base[i : i + 8].reshape(8 * CHANS, VOXELS)
+        packed = silu(jnp.dot(block, faces[...], preferred_element_type=f32)).astype(bf16)
+        y_own.ref[i : i + 8] = packed[:, :128].reshape(8, CHANS, 128)
+        z_own.ref[i : i + 8] = packed[:, 128:].reshape(8, CHANS, 128)
     y_own.send()
     z_own.send()
     fill_planes(coords.get(), counts.get(), y_own.ref, z_own.ref, work, [p.ref for p in planes])
 
 
-def first_conv(ins, outs, signal, y_bank, z_bank, taps, work, gathered):
-    (coords, counts, links, weights, signal_in, y_own, z_own, *planes, features, faces, pool, down) = ins
-    level, *sent, message = outs
+def activate(ins, outs):
+    base, signal = ins[0].get(), outs[0].ref
+
+    def one(j, carry):
+        signal[j] = silu(base[j].astype(f32)).astype(bf16)
+        return carry
+
+    lax.fori_loop(0, BLOCKS, one, 0, unroll=4)
+
+
+def packed_tile(tile_rows):
+    high = tile_rows.astype(bf16).astype(f32)
+    low = tile_rows - high
+    return jnp.concatenate([high[:, :128], high[:, 128:], low[:, :128], low[:, 128:]], axis=0).astype(bf16)
+
+
+def unpacked_tile(rows):
+    both = rows.astype(f32)
+    both = both[0:16] + both[16:32]
+    return jnp.concatenate([both[0:8], both[8:16]], axis=1)
+
+
+def stat_rows(mean, spread):
+    return jnp.concatenate([mean, spread, jnp.zeros((4, 128), f32)], axis=0)
+
+
+def halves(row):
+    return jnp.concatenate([row[:, :128], row[:, 128:]], axis=0)
+
+
+def first_conv(ins, outs, signal, y_bank, z_bank, taps, gathered):
+    (coords, counts, links, weights, signal_in, y_own, z_own, *planes, features, pool, down) = ins
+    level, own_tile, message = outs
     coords, counts, links, weight = coords.get(), counts.get(), links.get(), weights.get().at[0]
     signal[BLOCKS] = jnp.zeros((CHANS, VOXELS), bf16)
     bank_received([p.get() for p in planes], y_bank, z_bank)
@@ -252,14 +279,19 @@
     total = total[:8]
     mean = jnp.mean(total, axis=0, keepdims=True)
     spread = jnp.sum((total - mean) * (total - mean), axis=0, keepdims=True)
-    row = lax.broadcasted_iota(jnp.int32, (8, COARSE), 0)
-    extra = jnp.where(row == 0, mean, jnp.where(row == 1, spread, 0.0))
+    extra = stat_rows(halves(mean), halves(spread))
     for i in range(16):
-        message.ref[i, 0:8] = total
-        message.ref[i, 8:16] = extra
-    message.send()
-    take_faces(level_ref, faces.get(), y_bank, z_bank)
-    fill_planes(coords, counts, y_bank, z_bank, work, [p.ref for p in sent])
+        message.ref[i] = extra
+    own_tile.ref[...] = total
+
+
+def level_faces(ins, outs, y_bank, z_bank, work):
+    coords, counts, level, faces, own_tile = (one.get() for one in ins)
+    take_faces(level, faces, y_bank, z_bank)
+    fill_planes(coords, counts, y_bank, z_bank, work, [p.ref for p in outs])
+    packed = packed_tile(own_tile[...])
+    outs[0].ref[8] = packed
+    outs[1].ref[8] = packed
 
 
 def channel_diagonal():
@@ -280,44 +312,59 @@
 
 
 def row_sums(ins, outs):
-    where, message = (one.get() for one in ins)
-    partial, strip = (one.ref for one in outs)
-    mean, spread = merged_sums(message[:, 8, :], message[:, 9, :], 8.0)
-    row = lax.broadcasted_iota(jnp.int32, (8, COARSE), 0)
-    both = jnp.where(row == 0, mean, jnp.where(row == 1, spread, 0.0))
+    message, own_tile, y_above, y_below, z_low, z_high = (one.get() for one in ins)
+    partial, z_low_out, z_high_out = (one.ref for one in outs)
+    mean, spread = merged_sums(message[:, 0:2, :], message[:, 2:4, :], 8.0)
+    both = stat_rows(mean[0], spread[0])
     for i in range(16):
         partial[i] = both
-    minor = where[1]
-    for step in range(3):
-        strip[step] = message[jnp.clip(minor + step - 1, 0, 15), 0:8]
+    packed = packed_tile(own_tile[...])
+    for out, plane in ((z_low_out, z_low), (z_high_out, z_high)):
+        out[0:8] = plane[...]
+        out[8] = y_below[8]
+        out[9] = packed
+        out[10] = y_above[8]
 
 
 def group_total(x):
     lane = lax.broadcasted_iota(jnp.int32, x.shape, 1)
     for width in (1, 2, 4):
         x = x + jnp.where(
-            (lane & width) == 0, pltpu.roll(x, COARSE - width, 1), pltpu.roll(x, width, 1)
+            (lane & width) == 0, pltpu.roll(x, 128 - width, 1), pltpu.roll(x, width, 1)
         )
     return x
 
 
-def second_conv(
-    ins, outs, joined, signal, y_bank, z_bank, taps, work, active, raw, patches, lifted, rows
-):
-    (where, partial, s_low, s_own, s_high, gain, bias, patch, plain, near_half, far_half, up, coords,
-     counts, links, weights, spread, level, faces, y_spread, z_spread, *planes) = ins
-    second, signal2, y_own, z_own, *sent, coarse = outs
+def times_half(total, near, half):
+    for t in range(TAPS):
+        total += lax.dot_general(
+            near(t), half[:, tile(t)], (((1,), (1,)), ((), ())), preferred_element_type=f32
+        )
+    return total
+
+
+def coarse_front(ins, outs, active, raw, patches):
+    where, partial, own_tile, gain, bias, patch, plain, near_half, *planes = ins
     where, partial = where.get(), partial.get()
     major, minor = where[0], where[1]
-    mean, spread_sum = merged_sums(partial[:, 0, :], partial[:, 1, :], 128.0)
+    mean, spread_sum = merged_sums(partial[:, 0:2, :], partial[:, 2:4, :], 128.0)
+    mean, spread_sum = mean[0], spread_sum[0]
     group_mean = group_total(mean) * (1.0 / GROUP)
     away = mean - group_mean
     variance = group_total(spread_sum + 2048.0 * away * away) * (1.0 / (2048 * GROUP))
     gain, bias = gain.get(), bias.get()
+    group_mean = jnp.concatenate([group_mean[0:1], group_mean[1:2]], axis=1)
+    variance = jnp.concatenate([variance[0:1], variance[1:2]], axis=1)
     scale = gain[...] / jnp.sqrt(variance + NORM_EPS)
+    r0, r1, r2, r3 = (p.get() for p in planes)
+    tiles = [
+        [unpacked_tile(r3[8]), unpacked_tile(r3[9]), unpacked_tile(r3[10])],
+        [unpacked_tile(r1[8]), own_tile.get()[...], unpacked_tile(r0[8])],
+        [unpacked_tile(r2[8]), unpacked_tile(r2[9]), unpacked_tile(r2[10])],
+    ]
     active[...] = jnp.zeros_like(active)
     raw[...] = jnp.zeros_like(raw)
-    for dz, strip in enumerate((s_low.get(), s_own.get(), s_high.get())):
+    for dz, strip in enumerate(tiles):
         inside_z = (major + dz >= 1) & (major + dz <= 16)
         for dy in range(3):
             inside = inside_z & (minor + dy >= 1) & (minor + dy <= 16)
@@ -338,14 +385,20 @@
         high = rest.astype(bf16)
         rest = rest - high.astype(f32)
         total += jnp.dot(plain[...], high, preferred_element_type=f32)
-    core = major & 1
-    contract = (((1,), (1,)), ((), ()))
-    for half, base in ((near_half, core * TAPS), (far_half, (1 - core) * TAPS)):
-        half = half.get()
-        for t in range(TAPS):
-            total += lax.dot_general(
-                patches[base + t], half[:, tile(t)], contract, preferred_element_type=f32
-            )
+    base = (major & 1) * TAPS
+    half = near_half.get()
+    outs[0].ref[...] = times_half(total, lambda t: patches[base + t], half)
+    for t in range(TAPS):
+        outs[1].ref[t] = patches[TAPS - base + t]
+
+
+def second_conv(ins, outs, joined, signal, y_bank, z_bank, taps, work, lifted, rows):
+    (total, far_patches, far_half, up, coords, counts, links, weights, spread, level, faces,
+     y_spread, z_spread, *planes) = ins
+    second, signal2, y_own, z_own, *sent, coarse = outs
+    far_patches = far_patches.get()
+    total = times_half(total.get()[...], lambda t: far_patches[t], far_half.get())
+    r0, r1, r2, r3 = (p.get() for p in planes)
     result = total.astype(bf16)
     coarse.ref[...] = result[0:8]
     up = up.get()
@@ -357,7 +410,6 @@
     coords, counts, links, weight = coords.get(), counts.get(), links.get(), weights.get().at[1]
     spread, level, faces = spread.get(), level.get(), faces.get()
     y_spread, z_spread = y_spread.get(), z_spread.get()
-    r0, r1, r2, r3 = (p.get() for p in planes)
 
     def row_block(pos, cell):
         return jnp.where(diagonal, lifted[pos, pl.ds(cell, 1), :], 0.0).astype(bf16)
@@ -506,6 +558,7 @@
 SIGNAL = ((BLOCKS + 1, CHANS, VOXELS), bf16)
 BANK = ((BLOCKS + 33, CHANS, 128), bf16)
 TAP_STACK = ((4, 7 * CHANS, VOXELS), bf16)
+SUMS = ((16, 8, 128), f32)
 WORK = ((4, 9, CHANS, 128), bf16)
 
 
@@ -548,35 +601,48 @@
     )
     *own, low_y, high_y, low_z, high_z = call(
         first_faces, (*plainly(features, faces), *live[:2]),
-        (FIELD, FACES, FACES) + (PLANE,) * 4, (WORK,), 3,
+        (FACES, FACES) + (PLANE,) * 4, (WORK,), 3,
     )
     planes = swap_planes((low_y, high_y, low_z, high_z))
-    level, *planes, message = call(
+    (signal,) = call(activate, plainly(features), (FIELD,), (), 3)
+    level, own_tile, message = call(
         first_conv,
-        (*live, (fine_weights, None), *zip(own, place_own), *plainly(*planes, features, faces, pool, down_weight)),
-        (FIELD,) + (PLANE,) * 4 + (((16, 16, COARSE), f32),),
-        (SIGNAL, BANK, BANK, TAP_STACK, WORK, ((9, 16, COARSE), f32)), 9,
+        (*live, (fine_weights, None), *zip((signal, *own), place_own),
+         *plainly(*planes, features, pool, down_weight)),
+        (FIELD, ((8, COARSE), f32), SUMS),
+        (SIGNAL, BANK, BANK, TAP_STACK, ((9, 16, COARSE), f32)), 8,
     )
     message = lax.all_to_all(message, MY, 0, 0)
-    planes = swap_planes(planes)
-    partial, strip = call(
-        row_sums, ((where, "smem"), (message, None)),
-        (((16, 8, COARSE), f32), ((3, 8, COARSE), f32)), (), 1, planes,
+    low_y, high_y, low_z, high_z = call(
+        level_faces, (*live[:2], *plainly(level, faces, own_tile)),
+        (((9, CHANS, 128), bf16),) * 2 + (PLANE,) * 2, (FACES, FACES, WORK), 3,
+    )
+    y_above, y_below = shifted(low_y, MY, -1), shifted(high_y, MY, 1)
+    partial, low_z, high_z = call(
+        row_sums, plainly(message, own_tile, y_above, y_below, low_z, high_z),
+        (SUMS,) + (((11, CHANS, 128), bf16),) * 2, (), 1,
     )
     partial = lax.all_to_all(partial, MX, 0, 0)
-    strip_low = shifted(strip, MX, 1)
-    strip_high = shifted(strip, MX, -1)
-    near_half, strip_low = lax.optimization_barrier((near_half, strip_low))
+    z_above, z_below = shifted(low_z, MX, -1), shifted(high_z, MX, 1)
+    near_half, partial, z_above, z_below = lax.optimization_barrier(
+        (near_half, partial, z_above, z_below)
+    )
     far_half = lax.ppermute(near_half, "mx_1", [(0, 1), (1, 0)])
+    planes = (y_above, y_below, z_above, z_below)
+    front = call(
+        coarse_front,
+        ((where, "smem"),
+         *plainly(partial, own_tile, norm_gain.reshape(1, COARSE), norm_bias.reshape(1, COARSE),
+                  patch, plain, near_half, *planes)),
+        (((32, COARSE), f32), ((TAPS, 32, 128), bf16)),
+        (((128, COARSE), f32), ((128, COARSE), f32), ((2 * TAPS, 32, 128), bf16)), 4,
+    )
     second, *own, low_y, high_y, low_z, high_z, coarse = call(
         second_conv,
-        ((where, "smem"),
-         *plainly(partial, strip_low, strip, strip_high, norm_gain.reshape(1, COARSE),
-                  norm_bias.reshape(1, COARSE), patch, plain, near_half, far_half, up_weight),
-         *live, *plainly(fine_weights, spread, level, faces, y_spread, z_spread, *planes)),
+        (*plainly(*front, far_half, up_weight), *live,
+         *plainly(fine_weights, spread, level, faces, y_spread, z_spread, *planes)),
         (FIELD, FIELD, FACES, FACES) + (PLANE,) * 4 + (((8, COARSE), bf16),),
-        (FIELD, SIGNAL, BANK, BANK, TAP_STACK, WORK, ((128, COARSE), f32), ((128, COARSE), f32),
-         ((2 * TAPS, 32, 128), bf16), ((8, 32, COARSE), f32), ((256, 256), bf16)), 14,
+        (FIELD, SIGNAL, BANK, BANK, TAP_STACK, WORK, ((8, 32, COARSE), f32), ((256, 256), bf16)), 12,
     )
     planes = swap_planes((low_y, high_y, low_z, high_z))
     (fine_out,) = call(

time: 123 us -> 120 us (0.976)
  waiting for transfers between devices: 25.1 us -> 11.2 us
  blocking collectives: 0 us -> 12.7 us
  starting transfers between devices: 36.8 us -> 28.9 us
  Pallas kernels: 38.4 us -> 45.1 us
    ppermute x14 -> x12, waiting for transfers between devices: 21.8 us -> 8.66 us  [shifted(): lax.ppermute(x, axes, [(i, (i + step) % count) for i in range(count)])]
    all_to_all x0 -> x1, blocking collectives: none -> 12.7 us  [local(): message = lax.all_to_all(message, MY, 0, 0)]
    pallas_call x5 -> x8, Pallas kernels: 38.4 us -> 45.1 us  [call(): pl.pallas_call(body, in_specs=[hbm] * total, out_specs=[hbm] * len(outs),...]
    all_to_all x1 -> x0, starting transfers between devices: 6.18 us -> none  [local(): message = lax.all_to_all(message, MY, 0, 0)]
    all_to_all x1, starting transfers between devices: 4.09 us -> 9.89 us  [local(): partial = lax.all_to_all(partial, MX, 0, 0)]
    ppermute x14 -> x12, starting transfers between devices: 22.7 us -> 18.2 us  [shifted(): lax.ppermute(x, axes, [(i, (i + step) % count) for i in range(count)])]
    ppermute x1, starting transfers between devices: 3.77 us -> 0.74 us  [local(): far_half = lax.ppermute(near_half, 'mx_1', [(0, 1), (1, 0)])]
    unnamed x36 -> x32, local copies, waits for them, and re-layouts: 4.73 us -> 4.06 us
  transfers between devices with their start and end apart: 18 -> 15, of which waited for: 7 -> 5; matrix products, arithmetic and copies ran while one was open for 2% -> 2% of each run, Pallas kernels for 13% -> 21%
where the time goes in v2:
time: 120 us; the launch traced here: 119 us
  Pallas kernels  45.1 us (38%)
  starting transfers between devices  28.9 us (24%)
  between operations  14.9 us (12%)
  blocking collectives  12.7 us (11%)
  waiting for transfers between devices  11.2 us (9%)
  local copies, waits for them, and re-layouts  6 us (5%)
    pallas_call x8, Pallas kernels, call(): pl.pallas_call(body, in_specs=[hbm] * total, out_specs=[hbm] * len(outs),...  45.1 us
    ppermute x12, starting transfers between devices, shifted(): lax.ppermute(x, axes, [(i, (i + step) % count) for i in range(count)])  18.2 us
    all_to_all x1, blocking collectives, local(): message = lax.all_to_all(message, MY, 0, 0)  12.7 us
    all_to_all x1, starting transfers between devices, local(): partial = lax.all_to_all(partial, MX, 0, 0)  9.89 us
    ppermute x12, waiting for transfers between devices, shifted(): lax.ppermute(x, axes, [(i, (i + step) % count) for i in range(count)])  8.66 us
    unnamed x32, local copies, waits for them, and re-layouts  4.06 us
    all_to_all x1, waiting for transfers between devices, local(): partial = lax.all_to_all(partial, MX, 0, 0)  2.52 us
  transfers between devices with their start and end apart: 15, of which 5 were waited for; matrix products, arithmetic and copies ran while one was open for 2% of the time, Pallas kernels for 21%

profile of v2, /device:TPU:1, one launch (start us, length us, event | category | flops | bytes accessed | tf_op | source)
XLA Modules:
  0.0 119.3 jit_solution(5708295668055261776)
XLA Ops:
  7.2 0.0 copy-start
  7.2 0.0 all-gather.2.cloned.1.call-start
  7.2 0.9 copy-done
  8.1 0.7 dynamic-slice_bitcast_fusion
  8.8 0.0 all-gather.2.cloned.1.call-update
  9.4 3.8 %shard_map.177 = (bf16[32,32,128]{2,1,0:T(8,128)(2,1)}, bf16[32,32,128]{2,1,0:T(8,128)(2,1)}, bf16[8,32,128]{2,1,0:T(8,128)(2,1)}, bf16[8,32,128]{2,1,0:T(8,128)...) custom-call(bf16[32,32,512]{2,1,0:T(8,128)(2,1)} %refs_11_.2, ...), custom_call_target="tpu_custom_call" | custom-call | flops 3000000000 | bytes 9000000 | tf_op jit(solution)/shard_map/pallas_call | solution.py:539
  13.2 5.8 %collective-permute-start = (bf16[8,32,128]{2,1,0:T(8,128)(2,1)}, bf16[8,32,128]{2,1,0:T(8,128)(2,1)S(1)}, u32[]{:S(2)}, u32[]{:S(2)}) collective-permute-start(bf16[8,32,128]{2,1,0:T(8,128)(2,1)} %get-tuple-element.35), channel_id=1, source_target_pairs={{0,15},{1,0},{2,1},{3,2},{4,3},{5,4},{6,5},{7,6},{8,7},{9,8},{10,9... | collective-permute-start | bytes 196616 | tf_op jit(solution)/shard_map/ppermute | solution.py:567
  19.0 0.0 collective-permute-start.1
  19.1 1.0 collective-permute-start.2
  20.0 1.5 %collective-permute-start.3 = (bf16[8,32,128]{2,1,0:T(8,128)(2,1)}, bf16[8,32,128]{2,1,0:T(8,128)(2,1)S(1)}, u32[]{:S(2)}, u32[]{:S(2)}) collective-permute-start(bf16[8,32,128]{2,1,0:T(8,128)(2,1)} %get-tuple-element.38), channel_id=1, source_target_pairs={{0,16},{16,32},{32,48},{48,64},{64,80},{80,96},{96,112},{112,128},... | collective-permute-start | bytes 196616 | tf_op jit(solution)/shard_map/ppermute | solution.py:567
  21.5 2.9 %shard_map.176.refs_4_ = bf16[32,32,512]{2,1,0:T(8,128)(2,1)} custom-call(bf16[32,32,512]{2,1,0:T(8,128)(2,1)} %refs_11_.2), custom_call_target="tpu_custom_call" | custom-call | flops 3000000000 | bytes 9000000 | tf_op jit(solution)/shard_map/pallas_call | solution.py:539
  24.4 1.3 %collective-permute-done.1.refs_8_ = bf16[8,32,128]{2,1,0:T(8,128)(2,1)S(1)} collective-permute-done((bf16[8,32,128]{2,1,0:T(8,128)(2,1)}, bf16[8,32,128]{2,1,0:T(8,128)(2,1)S(1)}, u32[]{:S(2)}, u32[]{:S(2)}) %collective-permute-start.1) | collective-permute-done | bytes 65568 | tf_op jit(solution)/shard_map/ppermute | solution.py:567
  25.7 0.0 collective-permute-done.2.refs_9_
  25.7 0.3 collective-permute-done.3.refs_10_
  26.0 0.3 copy-done.10
  26.3 0.0 copy-done.12
  26.3 0.3 copy-done.14
  26.6 8.7 %shard_map.178 = (bf16[32,32,512]{2,1,0:T(8,128)(2,1)}, f32[8,256]{1,0:T(8,128)}, f32[16,8,128]{2,1,0:T(8,128)}) custom-call(s32[3,32]{1,0:T(4,128)} %refs_0_.9, s32[1]{0:T(128)S(6)} %copy.19.refs_3_.refs_1_.refs_5_, s32[6,32]{1,0:T(8,128)} %refs_2_.5, bf16[3,32,224]{2,1,0:T(8,128)(2,1)} %refs_3_.7, bf16[32,32,512]{2,1,0:T(8,128)(2,1)} %shard_map.176.refs_4_, ...), custom_call_target="tpu_custom_call" | custom-call | flops 8000000000 | bytes 24000000 | tf_op jit(solution)/shard_map/pallas_call | solution.py:539
  35.3 3.6 %shard_map.179 = (bf16[9,32,128]{2,1,0:T(8,128)(2,1)}, bf16[9,32,128]{2,1,0:T(8,128)(2,1)}, bf16[8,32,128]{2,1,0:T(8,128)(2,1)}, bf16[8,32,128]{2,1,0:T(8,128)(2,1)}) custom-call(s32[3,32]{1,0:T(4,128)} %refs_0_.9, s32[1]{0:T(128)S(6)} %copy.19.refs_3_.refs_1_.refs_5_, bf16[32,32,512]{2,1,0:T(8,128)(2,1)} %get-tuple-element.41.refs_2_.refs_9_, ...), custom_call_target="tpu_custom_call" | custom-call | flops 3000000000 | bytes 9000000 | tf_op jit(solution)/shard_map/pallas_call | solution.py:539
  39.0 4.9 %collective-permute-start.4 = (bf16[9,32,128]{2,1,0:T(8,128)(2,1)}, bf16[9,32,128]{2,1,0:T(8,128)(2,1)S(1)}, u32[]{:S(2)}, u32[]{:S(2)}) collective-permute-start(bf16[9,32,128]{2,1,0:T(8,128)(2,1)} %get-tuple-element.42), channel_id=1, source_target_pairs={{0,15},{1,0},{2,1},{3,2},{4,3},{5,4},{6,5},{7,6},{8,7},{9,8},{10,9... | collective-permute-start | bytes 221192 | tf_op jit(solution)/shard_map/ppermute | solution.py:567
  43.8 12.7 %all_to_all.10.refs_0_ = f32[16,8,128]{2,1,0:T(8,128)} all-to-all(f32[16,8,128]{2,1,0:T(8,128)S(1)} %copy-done.2), channel_id=1, replica_groups=mesh['mx_0'=8,'mx_1'=2,'my_0'=4,'my_1'=4] {'my_0','my_1'}, dimensions={0} | all-to-all | bytes 131072 | tf_op jit(solution)/shard_map/all_to_all | solution.py:615
  56.5 0.0 collective-permute-done.4.refs_2_.refs_8_.refs_13_
  56.5 0.0 collective-permute-done.5.refs_3_.refs_9_.refs_14_
  56.5 0.6 copy-done.6
  57.1 0.0 copy-done.7
  57.2 1.8 %shard_map.180 = (f32[16,8,128]{2,1,0:T(8,128)}, bf16[11,32,128]{2,1,0:T(8,128)(2,1)}, bf16[11,32,128]{2,1,0:T(8,128)(2,1)}) custom-call(f32[16,8,128]{2,1,0:T(8,128)} %all_to_all.10.refs_0_, f32[8,256]{1,0:T(8,128)} %get-tuple-element.40.refs_4_.refs_1_.refs_2_, bf16[9,32,128]{2,1,0:T(8,128)(2,1)} %copy-done.6, bf16[9,32,128]{2,1,0:T(8,128)(2,1)} %copy-done.7, ...), custom_call_target="tpu_custom_call" | custom-call | flops 1000000000 | bytes 3000000 | tf_op jit(solution)/shard_map/pallas_call | solution.py:539
  59.0 9.9 %all-to-all-start.1 = ((f32[16,8,128]{2,1,0:T(8,128)}), f32[16,8,128]{2,1,0:T(8,128)S(1)}, u32[]{:S(2)}, u32[]{:S(2)}) async-start(f32[16,8,128]{2,1,0:T(8,128)} %get-tuple-element.46), calls=%async_computation.1 | async-start | bytes 131072 | tf_op jit(solution)/shard_map/all_to_all | solution.py:625
  68.9 0.1 collective-permute-start.6
  69.0 1.6 %collective-permute-start.7 = (bf16[11,32,128]{2,1,0:T(8,128)(2,1)}, bf16[11,32,128]{2,1,0:T(8,128)(2,1)S(1)}, u32[]{:S(2)}, u32[]{:S(2)}) collective-permute-start(bf16[11,32,128]{2,1,0:T(8,128)(2,1)} %get-tuple-element.48), channel_id=1, source_target_pairs={{0,16},{16,32},{32,48},{48,64},{64,80},{80,96},{96,112},{112,128},... | collective-permute-start | bytes 270344 | tf_op jit(solution)/shard_map/ppermute | solution.py:567
  70.6 3.6 %collective-permute-done.6.refs_10_.refs_15_ = bf16[11,32,128]{2,1,0:T(8,128)(2,1)S(1)} collective-permute-done((bf16[11,32,128]{2,1,0:T(8,128)(2,1)}, bf16[11,32,128]{2,1,0:T(8,128)(2,1)S(1)}, u32[]{:S(2)}, u32[]{:S(2)}) %collective-permute-start.6) | collective-permute-done | bytes 90144 | tf_op jit(solution)/shard_map/ppermute | solution.py:567
  74.2 2.5 %all-to-all-done.1.refs_1_ = f32[16,8,128]{2,1,0:T(8,128)S(1)} async-done(((f32[16,8,128]{2,1,0:T(8,128)}), f32[16,8,128]{2,1,0:T(8,128)S(1)}, u32[]{:S(2)}, u32[]{:S(2)}) %all-to-all-start.1) | async-done | bytes 65568 | tf_op jit(solution)/shard_map/all_to_all | solution.py:625
  76.7 0.7 collective-permute-start.8
  77.5 0.6 pad_add_fusion.refs_0_
  78.1 3.8 %shard_map.181 = (f32[32,256]{1,0:T(8,128)}, bf16[27,32,128]{2,1,0:T(8,128)(2,1)}) custom-call(s32[2]{0:T(128)} %pad_add_fusion.refs_0_, f32[16,8,128]{2,1,0:T(8,128)} %copy-done.1, f32[8,256]{1,0:T(8,128)} %get-tuple-element.40.refs_4_.refs_1_.refs_2_, f32[1,256]{1,0:T(1,128)} %bitcast.6, f32[1,256]{1,0:T(1,128)} %bitcast.7, ...), custom_call_target="tpu_custom_call" | custom-call | flops 4000000000 | bytes 12000000 | tf_op jit(solution)/shard_map/pallas_call | solution.py:539
  81.9 0.0 collective-permute-done.8.refs_2_
  81.9 1.2 %copy-done.3 = bf16[256,3456]{1,0:T(8,128)(2,1)} copy-done((bf16[256,3456]{1,0:T(8,128)(2,1)}, bf16[256,3456]{1,0:T(8,128)(2,1)S(1)}, u32[]{:S(2)}) %copy-start.3) | copy-done | bytes 1769496
  83.2 12.5 %shard_map.182 = (bf16[32,32,512]{2,1,0:T(8,128)(2,1)}, bf16[32,32,512]{2,1,0:T(8,128)(2,1)}, bf16[32,32,128]{2,1,0:T(8,128)(2,1)}, bf16[32,32,128]{2,1,0:T(8,12...) custom-call(f32[32,256]{1,0:T(8,128)} %get-tuple-element.53.refs_0_,, ...), custom_call_target="tpu_custom_call" | custom-call | flops 12000000000 | bytes 36000000 | tf_op jit(solution)/shard_map/pallas_call | solution.py:539
  95.7 1.4 %collective-permute-start.9 = (bf16[8,32,128]{2,1,0:T(8,128)(2,1)}, bf16[8,32,128]{2,1,0:T(8,128)(2,1)S(1)}, u32[]{:S(2)}, u32[]{:S(2)}) collective-permute-start(bf16[8,32,128]{2,1,0:T(8,128)(2,1)} %get-tuple-element.58), channel_id=1, source_target_pairs={{0,15},{1,0},{2,1},{3,2},{4,3},{5,4},{6,5},{7,6},{8,7},{9,8},{10,9... | collective-permute-start | bytes 196616 | tf_op jit(solution)/shard_map/ppermute | solution.py:567
  97.2 0.1 collective-permute-start.10
  97.2 0.6 collective-permute-start.11
  97.8 1.2 collective-permute-start.12
  99.0 1.3 %reshape.15 = bf16[2,2,2,256]{3,2,1,0:T(2,128)(2,1)} reshape(bf16[8,256]{1,0:T(8,128)(2,1)} %get-tuple-element.63) | data formatting | bytes 8192 | tf_op jit(solution)/shard_map/reshape | solution.py:652
  100.3 3.5 %collective-permute-done.10.refs_8_ = bf16[8,32,128]{2,1,0:T(8,128)(2,1)S(1)} collective-permute-done((bf16[8,32,128]{2,1,0:T(8,128)(2,1)}, bf16[8,32,128]{2,1,0:T(8,128)(2,1)S(1)}, u32[]{:S(2)}, u32[]{:S(2)}) %collective-permute-start.10) | collective-permute-done | bytes 65568 | tf_op jit(solution)/shard_map/ppermute | solution.py:567
  103.8 0.0 collective-permute-done.11.refs_9_
  103.8 0.6 copy-done.11
  104.4 0.0 copy-done.13
  104.5 0.0 copy-done.15
  104.5 8.0 %shard_map.183 = bf16[32,32,512]{2,1,0:T(8,128)(2,1)} custom-call(s32[3,32]{1,0:T(4,128)} %refs_0_.9, s32[1]{0:T(128)S(6)} %copy.19.refs_3_.refs_1_.refs_5_, s32[6,32]{1,0:T(8,128)} %refs_2_.5, bf16[3,32,224]{2,1,0:T(8,128)(2,1)} %refs_3_.7, bf16[32,32,512]{2,1,0:T(8,128)(2,1)} %get-tuple-element.55.refs_4_, bf16[32,32,128]{2,1,0:T(8,128)(2,1)} %get-tuple-element.56.refs_5_, ...), custom_call_target="tpu_custom_call" | custom-call | flops 7000000000 | bytes 21000000 | tf_op jit(solution)/shard_map/pallas_call | solution.py:539
  (27 shorter events, 0.1 us)
Async XLA Ops:
  7.2 0.9 copy-start
  7.2 69.5 %all-gather.2.cloned.1.call-start = ((), (), s32[]{:S(2)}) async-start(), calls=%async_computation.2 | async-start | bytes 1880064 | tf_op jit(solution)/shard_map/all_gather | solution.py:591
  13.2 11.2 %collective-permute-start = (bf16[8,32,128]{2,1,0:T(8,128)(2,1)}, bf16[8,32,128]{2,1,0:T(8,128)(2,1)S(1)}, u32[]{:S(2)}, u32[]{:S(2)}) collective-permute-start(bf16[8,32,128]{2,1,0:T(8,128)(2,1)} %get-tuple-element.35), channel_id=1, source_target_pairs={{0,15},{1,0},{2,1},{3,2},{4,3},{5,4},{6,5},{7,6},{8,7},{9,8},{10,9... | collective-permute-start | bytes 196616 | tf_op jit(solution)/shard_map/ppermute | solution.py:567
  19.0 6.6 %collective-permute-start.1 = (bf16[8,32,128]{2,1,0:T(8,128)(2,1)}, bf16[8,32,128]{2,1,0:T(8,128)(2,1)S(1)}, u32[]{:S(2)}, u32[]{:S(2)}) collective-permute-start(bf16[8,32,128]{2,1,0:T(8,128)(2,1)} %get-tuple-element.36), channel_id=1, source_target_pairs={{0,1},{1,2},{2,3},{3,4},{4,5},{5,6},{6,7},{7,8},{8,9},{9,10},{10,1... | collective-permute-start | bytes 196616 | tf_op jit(solution)/shard_map/ppermute | solution.py:567
  19.1 6.6 %collective-permute-start.2 = (bf16[8,32,128]{2,1,0:T(8,128)(2,1)}, bf16[8,32,128]{2,1,0:T(8,128)(2,1)S(1)}, u32[]{:S(2)}, u32[]{:S(2)}) collective-permute-start(bf16[8,32,128]{2,1,0:T(8,128)(2,1)} %get-tuple-element.37), channel_id=1, source_target_pairs={{0,240},{16,0},{32,16},{48,32},{64,48},{80,64},{96,80},{112,96},{1... | collective-permute-start | bytes 196616 | tf_op jit(solution)/shard_map/ppermute | solution.py:567
  20.0 6.0 %collective-permute-start.3 = (bf16[8,32,128]{2,1,0:T(8,128)(2,1)}, bf16[8,32,128]{2,1,0:T(8,128)(2,1)S(1)}, u32[]{:S(2)}, u32[]{:S(2)}) collective-permute-start(bf16[8,32,128]{2,1,0:T(8,128)(2,1)} %get-tuple-element.38), channel_id=1, source_target_pairs={{0,16},{16,32},{32,48},{48,64},{64,80},{80,96},{96,112},{112,128},... | collective-permute-start | bytes 196616 | tf_op jit(solution)/shard_map/ppermute | solution.py:567
  24.4 1.6 %copy-start.8 = (bf16[8,32,128]{2,1,0:T(8,128)(2,1)}, bf16[8,32,128]{2,1,0:T(8,128)(2,1)S(1)}, u32[]{:S(2)}) copy-start(bf16[8,32,128]{2,1,0:T(8,128)(2,1)S(1)} %collective-permute-done.refs_7_) | copy-start | bytes 196612
  25.7 0.6 copy-start.10
  25.7 0.6 copy-start.12
  26.0 0.6 copy-start.14
  35.3 8.5 %copy-start.2 = (f32[16,8,128]{2,1,0:T(8,128)S(1)}, f32[16,8,128]{2,1,0:T(8,128)}, u32[]{:S(2)}) copy-start(f32[16,8,128]{2,1,0:T(8,128)} %get-tuple-element.39) | copy-start | bytes 196612
  39.0 17.6 %collective-permute-start.4 = (bf16[9,32,128]{2,1,0:T(8,128)(2,1)}, bf16[9,32,128]{2,1,0:T(8,128)(2,1)S(1)}, u32[]{:S(2)}, u32[]{:S(2)}) collective-permute-start(bf16[9,32,128]{2,1,0:T(8,128)(2,1)} %get-tuple-element.42), channel_id=1, source_target_pairs={{0,15},{1,0},{2,1},{3,2},{4,3},{5,4},{6,5},{7,6},{8,7},{9,8},{10,9... | collective-permute-start | bytes 221192 | tf_op jit(solution)/shard_map/ppermute | solution.py:567
  43.8 12.7 %collective-permute-start.5 = (bf16[9,32,128]{2,1,0:T(8,128)(2,1)}, bf16[9,32,128]{2,1,0:T(8,128)(2,1)S(1)}, u32[]{:S(2)}, u32[]{:S(2)}) collective-permute-start(bf16[9,32,128]{2,1,0:T(8,128)(2,1)} %get-tuple-element.43), channel_id=1, source_target_pairs={{0,1},{1,2},{2,3},{3,4},{4,5},{5,6},{6,7},{7,8},{8,9},{9,10},{10,1... | collective-permute-start | bytes 221192 | tf_op jit(solution)/shard_map/ppermute | solution.py:567
  56.5 0.6 copy-start.6
  56.5 0.7 copy-start.7
  59.0 17.7 %all-to-all-start.1 = ((f32[16,8,128]{2,1,0:T(8,128)}), f32[16,8,128]{2,1,0:T(8,128)S(1)}, u32[]{:S(2)}, u32[]{:S(2)}) async-start(f32[16,8,128]{2,1,0:T(8,128)} %get-tuple-element.46), calls=%async_computation.1 | async-start | bytes 131072 | tf_op jit(solution)/shard_map/all_to_all | solution.py:625
  68.9 5.3 %collective-permute-start.6 = (bf16[11,32,128]{2,1,0:T(8,128)(2,1)}, bf16[11,32,128]{2,1,0:T(8,128)(2,1)S(1)}, u32[]{:S(2)}, u32[]{:S(2)}) collective-permute-start(bf16[11,32,128]{2,1,0:T(8,128)(2,1)} %get-tuple-element.47), channel_id=1, source_target_pairs={{0,240},{16,0},{32,16},{48,32},{64,48},{80,64},{96,80},{112,96},{1... | collective-permute-start | bytes 270344 | tf_op jit(solution)/shard_map/ppermute | solution.py:567
  69.0 5.2 %collective-permute-start.7 = (bf16[11,32,128]{2,1,0:T(8,128)(2,1)}, bf16[11,32,128]{2,1,0:T(8,128)(2,1)S(1)}, u32[]{:S(2)}, u32[]{:S(2)}) collective-permute-start(bf16[11,32,128]{2,1,0:T(8,128)(2,1)} %get-tuple-element.48), channel_id=1, source_target_pairs={{0,16},{16,32},{32,48},{48,64},{64,80},{80,96},{96,112},{112,128},... | collective-permute-start | bytes 270344 | tf_op jit(solution)/shard_map/ppermute | solution.py:567
  74.2 3.9 %copy-start.4 = (bf16[11,32,128]{2,1,0:T(8,128)(2,1)}, bf16[11,32,128]{2,1,0:T(8,128)(2,1)S(1)}, u32[]{:S(2)}) copy-start(bf16[11,32,128]{2,1,0:T(8,128)(2,1)S(1)} %collective-permute-done.6.refs_10_.refs_15_) | copy-start | bytes 270340
  74.2 3.9 %copy-start.5 = (bf16[11,32,128]{2,1,0:T(8,128)(2,1)}, bf16[11,32,128]{2,1,0:T(8,128)(2,1)S(1)}, u32[]{:S(2)}) copy-start(bf16[11,32,128]{2,1,0:T(8,128)(2,1)S(1)} %collective-permute-done.7.refs_11_.refs_16_) | copy-start | bytes 270340
  76.7 1.4 %copy-start.1 = (f32[16,8,128]{2,1,0:T(8,128)}, f32[16,8,128]{2,1,0:T(8,128)S(1)}, u32[]{:S(2)}) copy-start(f32[16,8,128]{2,1,0:T(8,128)S(1)} %all-to-all-done.1.refs_1_) | copy-start | bytes 196612
  76.7 5.2 %collective-permute-start.8 = (bf16[256,3456]{1,0:T(8,128)(2,1)}, bf16[256,3456]{1,0:T(8,128)(2,1)S(1)}, u32[]{:S(2)}, u32[]{:S(2)}) collective-permute-start(bf16[256,3456]{1,0:T(8,128)(2,1)} %all-gather.2.cloned.1.call-done.refs_7_), channel_id=1, source_target_pairs={{0,16},{16,0},{1,17},{17,1},{2,18},{18,2},{3,19},{19,3},{4,20},{20... | collective-permute-start | bytes 5308424 | tf_op jit(solution)/shard_map/ppermute | solution.py:630
  81.9 1.2 %copy-start.3 = (bf16[256,3456]{1,0:T(8,128)(2,1)}, bf16[256,3456]{1,0:T(8,128)(2,1)S(1)}, u32[]{:S(2)}) copy-start(bf16[256,3456]{1,0:T(8,128)(2,1)S(1)} %collective-permute-done.8.refs_2_) | copy-start | bytes 5308420
  95.7 4.6 %collective-permute-start.9 = (bf16[8,32,128]{2,1,0:T(8,128)(2,1)}, bf16[8,32,128]{2,1,0:T(8,128)(2,1)S(1)}, u32[]{:S(2)}, u32[]{:S(2)}) collective-permute-start(bf16[8,32,128]{2,1,0:T(8,128)(2,1)} %get-tuple-element.58), channel_id=1, source_target_pairs={{0,15},{1,0},{2,1},{3,2},{4,3},{5,4},{6,5},{7,6},{8,7},{9,8},{10,9... | collective-permute-start | bytes 196616 | tf_op jit(solution)/shard_map/ppermute | solution.py:567
  97.2 6.6 %collective-permute-start.10 = (bf16[8,32,128]{2,1,0:T(8,128)(2,1)}, bf16[8,32,128]{2,1,0:T(8,128)(2,1)S(1)}, u32[]{:S(2)}, u32[]{:S(2)}) collective-permute-start(bf16[8,32,128]{2,1,0:T(8,128)(2,1)} %get-tuple-element.59), channel_id=1, source_target_pairs={{0,1},{1,2},{2,3},{3,4},{4,5},{5,6},{6,7},{7,8},{8,9},{9,10},{10,1... | collective-permute-start | bytes 196616 | tf_op jit(solution)/shard_map/ppermute | solution.py:567
  97.2 6.6 %collective-permute-start.11 = (bf16[8,32,128]{2,1,0:T(8,128)(2,1)}, bf16[8,32,128]{2,1,0:T(8,128)(2,1)S(1)}, u32[]{:S(2)}, u32[]{:S(2)}) collective-permute-start(bf16[8,32,128]{2,1,0:T(8,128)(2,1)} %get-tuple-element.60), channel_id=1, source_target_pairs={{0,240},{16,0},{32,16},{48,32},{64,48},{80,64},{96,80},{112,96},{1... | collective-permute-start | bytes 196616 | tf_op jit(solution)/shard_map/ppermute | solution.py:567
  97.8 6.0 %collective-permute-start.12 = (bf16[8,32,128]{2,1,0:T(8,128)(2,1)}, bf16[8,32,128]{2,1,0:T(8,128)(2,1)S(1)}, u32[]{:S(2)}, u32[]{:S(2)}) collective-permute-start(bf16[8,32,128]{2,1,0:T(8,128)(2,1)} %get-tuple-element.61), channel_id=1, source_target_pairs={{0,16},{16,32},{32,48},{48,64},{64,80},{80,96},{96,112},{112,128},... | collective-permute-start | bytes 196616 | tf_op jit(solution)/shard_map/ppermute | solution.py:567
  100.3 3.6 %copy-start.9 = (bf16[8,32,128]{2,1,0:T(8,128)(2,1)}, bf16[8,32,128]{2,1,0:T(8,128)(2,1)S(1)}, u32[]{:S(2)}) copy-start(bf16[8,32,128]{2,1,0:T(8,128)(2,1)S(1)} %collective-permute-done.9.refs_7_) | copy-start | bytes 196612
  103.8 0.6 copy-start.11
  103.8 0.6 copy-start.13
  103.8 0.7 copy-start.15
Sparse Core Ops, SparseCore 0:
  10.5 52.6 all-gather.1

commit v3 on v2

--- a/solution.py
+++ b/solution.py
@@ -234,6 +234,15 @@
     return jnp.concatenate([both[0:8], both[8:16]], axis=1)
 
 
+def exact_parts(x):
+    parts = []
+    for _ in range(3):
+        part = x.astype(bf16).astype(f32)
+        parts.append(part)
+        x = x - part
+    return jnp.concatenate([*parts, jnp.zeros((4, 128), f32)], axis=0).astype(bf16)
+
+
 def stat_rows(mean, spread):
     return jnp.concatenate([mean, spread, jnp.zeros((4, 128), f32)], axis=0)
 
@@ -243,7 +252,7 @@
 
 
 def first_conv(ins, outs, signal, y_bank, z_bank, taps, gathered):
-    (coords, counts, links, weights, signal_in, y_own, z_own, *planes, features, pool, down) = ins
+    (coords, counts, links, weights, signal_in, y_own, z_own, *planes, features, pool, down, where, weight_columns) = ins
     level, own_tile, message = outs
     coords, counts, links, weight = coords.get(), counts.get(), links.get(), weights.get().at[0]
     signal[BLOCKS] = jnp.zeros((CHANS, VOXELS), bf16)
@@ -252,6 +261,10 @@
         one.get()
     base = features.get()
     level_ref = level.ref
+    start = pl.multiple_of((where.get()[0] & 1) * HALF_ROWS, 128)
+    half = weight_columns.get()[:, pl.ds(start, HALF_ROWS)]
+    for i in range(16):
+        message.ref[i, :, :HALF_ROWS] = half
 
     def finish(j, result):
         level_ref[j] = (base[j].astype(f32) + result).astype(bf16)
@@ -279,9 +292,9 @@
     total = total[:8]
     mean = jnp.mean(total, axis=0, keepdims=True)
     spread = jnp.sum((total - mean) * (total - mean), axis=0, keepdims=True)
-    extra = stat_rows(halves(mean), halves(spread))
+    extra = exact_parts(jnp.concatenate([halves(mean), halves(spread)], axis=0))
     for i in range(16):
-        message.ref[i] = extra
+        message.ref[i, :, HALF_ROWS:] = extra
     own_tile.ref[...] = total
 
 
@@ -314,7 +327,9 @@
 def row_sums(ins, outs):
     message, own_tile, y_above, y_below, z_low, z_high = (one.get() for one in ins)
     partial, z_low_out, z_high_out = (one.ref for one in outs)
-    mean, spread = merged_sums(message[:, 0:2, :], message[:, 2:4, :], 8.0)
+    sums = message[...].astype(f32)
+    sums = sums[:, 0:4] + sums[:, 4:8] + sums[:, 8:12]
+    mean, spread = merged_sums(sums[:, 0:2], sums[:, 2:4], 8.0)
     both = stat_rows(mean[0], spread[0])
     for i in range(16):
         partial[i] = both
@@ -505,7 +520,7 @@
 
 
 def call(kernel, arrays, outs, scratch, microseconds, spare=()):
-    own = [(i, to) for i, (_, to) in enumerate(arrays) if to is None or to == "smem"]
+    own = [(i, to) for i, (_, to) in enumerate(arrays) if not callable(to)]
     count, total = len(arrays), len(arrays) + len(spare)
 
     def body(*refs):
@@ -518,7 +533,8 @@
         arriving = []
         for i, (_, to) in enumerate(arrays):
             ref = placed[i] if i in placed else to(*work)
-            arriving.append(Arriving(pltpu.make_async_copy(ins[i], ref, in_sem.at[i]), ref))
+            source = ins[i].at[:, :, to] if isinstance(to, slice) else ins[i]
+            arriving.append(Arriving(pltpu.make_async_copy(source, ref, in_sem.at[i]), ref))
         leaving = [
             Leaving(pltpu.make_async_copy(staged[i], results[i], out_sem.at[i]), staged[i])
             for i in range(len(outs))
@@ -533,8 +549,13 @@
             one.copy.wait()
 
     hbm = pl.BlockSpec(memory_space=pltpu.HBM)
-    spaces = {None: pltpu.VMEM, "smem": pltpu.SMEM}
-    buffers = [spaces[to](arrays[i][0].shape, arrays[i][0].dtype) for i, to in own]
+    buffers = []
+    for i, to in own:
+        shape = arrays[i][0].shape
+        if isinstance(to, slice):
+            shape = (*shape[:-1], to.stop - to.start)
+        space = pltpu.SMEM if to == "smem" else pltpu.VMEM
+        buffers.append(space(shape, arrays[i][0].dtype))
     buffers += [pltpu.VMEM(s, d) for s, d in (*outs, *scratch)]
     return pl.pallas_call(
         body,
@@ -585,11 +606,6 @@
     major = lax.axis_index(MX)
     minor = lax.axis_index(MY)
     where = jnp.stack([major, minor]).astype(jnp.int32)
-    part = lax.dynamic_slice_in_dim(
-        coarse_weight.T, lax.axis_index("mx_1") * HALF_ROWS, HALF_ROWS, 1
-    )
-    near_half = lax.all_gather(part, MY, axis=0, tiled=True)
-
     def plainly(*arrays):
         return tuple((x, None) for x in arrays)
 
@@ -608,8 +624,8 @@
     level, own_tile, message = call(
         first_conv,
         (*live, (fine_weights, None), *zip((signal, *own), place_own),
-         *plainly(*planes, features, pool, down_weight)),
-        (FIELD, ((8, COARSE), f32), SUMS),
+         *plainly(*planes, features, pool, down_weight), (where, "smem"), (coarse_weight.T, None)),
+        (FIELD, ((8, COARSE), f32), ((16, 16, HALF_ROWS + 128), bf16)),
         (SIGNAL, BANK, BANK, TAP_STACK, ((9, 16, COARSE), f32)), 8,
     )
     message = lax.all_to_all(message, MY, 0, 0)
@@ -619,11 +635,13 @@
     )
     y_above, y_below = shifted(low_y, MY, -1), shifted(high_y, MY, 1)
     partial, low_z, high_z = call(
-        row_sums, plainly(message, own_tile, y_above, y_below, low_z, high_z),
+        row_sums,
+        ((message, slice(HALF_ROWS, HALF_ROWS + 128)), *plainly(own_tile, y_above, y_below, low_z, high_z)),
         (SUMS,) + (((11, CHANS, 128), bf16),) * 2, (), 1,
     )
     partial = lax.all_to_all(partial, MX, 0, 0)
     z_above, z_below = shifted(low_z, MX, -1), shifted(high_z, MX, 1)
+    near_half = message.reshape(COARSE, HALF_ROWS + 128)
     near_half, partial, z_above, z_below = lax.optimization_barrier(
         (near_half, partial, z_above, z_below)
     )

time: 120 us -> 118 us (0.983)
  between operations: 14.9 us -> 1.42 us
  waiting for transfers between devices: 11.2 us -> 24.6 us
  blocking collectives: 12.7 us -> 0 us
  starting transfers between devices: 28.9 us -> 39.2 us
    ppermute x12, waiting for transfers between devices: 8.66 us -> 22.1 us  [shifted(): lax.ppermute(x, axes, [(i, (i + step) % count) for i in range(count)])]
    all_to_all x1 -> x0, blocking collectives: 12.7 us -> none  [local(): message = lax.all_to_all(message, MY, 0, 0)]
    all_to_all x0 -> x1, starting transfers between devices: none -> 6.17 us  [local(): message = lax.all_to_all(message, MY, 0, 0)]
    all_to_all x1, starting transfers between devices: 9.89 us -> 13.2 us  [local(): partial = lax.all_to_all(partial, MX, 0, 0)]
    unnamed x32 -> x30, local copies, waits for them, and re-layouts: 4.06 us -> 3.79 us
  transfers between devices with their start and end apart: 15 -> 15, of which waited for: 5 -> 7; matrix products, arithmetic and copies ran while one was open for 2% -> 2% of each run, Pallas kernels for 21% -> 9%
where the time goes in v3:
time: 118 us; the launch traced here: 117 us
  Pallas kernels  46.2 us (39%)
  starting transfers between devices  39.2 us (33%)
  waiting for transfers between devices  24.6 us (21%)
  local copies, waits for them, and re-layouts  5.08 us (4%)
  between operations  1.42 us (1%)
    pallas_call x8, Pallas kernels, call(): pl.pallas_call(body, in_specs=[hbm] * total, out_specs=[hbm] * len(outs),...  46.2 us
    ppermute x12, waiting for transfers between devices, shifted(): lax.ppermute(x, axes, [(i, (i + step) % count) for i in range(count)])  22.1 us
    ppermute x12, starting transfers between devices, shifted(): lax.ppermute(x, axes, [(i, (i + step) % count) for i in range(count)])  19.2 us
    all_to_all x1, starting transfers between devices, local(): partial = lax.all_to_all(partial, MX, 0, 0)  13.2 us
    all_to_all x1, starting transfers between devices, local(): message = lax.all_to_all(message, MY, 0, 0)  6.17 us
    unnamed x30, local copies, waits for them, and re-layouts  3.79 us
    all_to_all x1, waiting for transfers between devices, local(): partial = lax.all_to_all(partial, MX, 0, 0)  2.52 us
  transfers between devices with their start and end apart: 15, of which 7 were waited for; matrix products, arithmetic and copies ran while one was open for 2% of the time, Pallas kernels for 9%

profile of v3, /device:TPU:1, one launch (start us, length us, event | category | flops | bytes accessed | tf_op | source)
XLA Modules:
  0.0 117.2 jit_solution(12395748904501818514)
XLA Ops:
  1.3 3.8 %shard_map.177 = (bf16[32,32,128]{2,1,0:T(8,128)(2,1)}, bf16[32,32,128]{2,1,0:T(8,128)(2,1)}, bf16[8,32,128]{2,1,0:T(8,128)(2,1)}, bf16[8,32,128]{2,1,0:T(8,128)...) custom-call(bf16[32,32,512]{2,1,0:T(8,128)(2,1)} %refs_11_.2, ...), custom_call_target="tpu_custom_call" | custom-call | flops 3000000000 | bytes 9000000 | tf_op jit(solution)/shard_map/pallas_call | solution.py:560
  5.0 5.8 %collective-permute-start = (bf16[8,32,128]{2,1,0:T(8,128)(2,1)}, bf16[8,32,128]{2,1,0:T(8,128)(2,1)S(1)}, u32[]{:S(2)}, u32[]{:S(2)}) collective-permute-start(bf16[8,32,128]{2,1,0:T(8,128)(2,1)} %get-tuple-element.35), channel_id=1, source_target_pairs={{0,15},{1,0},{2,1},{3,2},{4,3},{5,4},{6,5},{7,6},{8,7},{9,8},{10,9... | collective-permute-start | bytes 196616 | tf_op jit(solution)/shard_map/ppermute | solution.py:588
  10.9 0.0 collective-permute-start.1
  10.9 1.0 collective-permute-start.2
  11.8 1.5 %collective-permute-start.3 = (bf16[8,32,128]{2,1,0:T(8,128)(2,1)}, bf16[8,32,128]{2,1,0:T(8,128)(2,1)S(1)}, u32[]{:S(2)}, u32[]{:S(2)}) collective-permute-start(bf16[8,32,128]{2,1,0:T(8,128)(2,1)} %get-tuple-element.38), channel_id=1, source_target_pairs={{0,16},{16,32},{32,48},{48,64},{64,80},{80,96},{96,112},{112,128},... | collective-permute-start | bytes 196616 | tf_op jit(solution)/shard_map/ppermute | solution.py:588
  13.4 2.9 %shard_map.176.refs_4_ = bf16[32,32,512]{2,1,0:T(8,128)(2,1)} custom-call(bf16[32,32,512]{2,1,0:T(8,128)(2,1)} %refs_11_.2), custom_call_target="tpu_custom_call" | custom-call | flops 3000000000 | bytes 9000000 | tf_op jit(solution)/shard_map/pallas_call | solution.py:560
  16.2 0.7 pad_add_fusion.refs_14_.refs_0_
  16.9 0.0 collective-permute-done.refs_7_
  16.9 0.6 collective-permute-done.1.refs_8_
  17.5 0.0 collective-permute-done.2.refs_9_
  17.5 0.3 collective-permute-done.3.refs_10_
  17.8 0.3 copy-done.8
  18.1 0.0 copy-done.9
  18.2 0.3 copy-done.10
  18.4 9.9 %shard_map.178 = (bf16[32,32,512]{2,1,0:T(8,128)(2,1)}, f32[8,256]{1,0:T(8,128)}, bf16[16,16,3584]{2,1,0:T(8,128)(2,1)}) custom-call(s32[3,32]{1,0:T(4,128)} %refs_0_.9, s32[1]{0:T(128)S(6)} %copy.19.refs_3_.refs_1_.refs_5_, s32[6,32]{1,0:T(8,128)} %refs_2_.5, bf16[3,32,224]{2,1,0:T(8,128)(2,1)} %refs_3_.7, bf16[32,32,512]{2,1,0:T(8,128)(2,1)} %shard_map.176.refs_4_, ...), custom_call_target="tpu_custom_call" | custom-call | flops 8000000000 | bytes 24000000 | tf_op jit(solution)/shard_map/pallas_call | solution.py:560
  28.3 6.2 %all-to-all-start = ((bf16[16,16,3584]{2,1,0:T(8,128)(2,1)}), bf16[16,16,3584]{2,1,0:T(8,128)(2,1)S(1)}, u32[]{:S(2)}, u32[]{:S(2)}) async-start(bf16[16,16,3584]{2,1,0:T(8,128)(2,1)} %get-tuple-element.39), calls=%async_computation | async-start | bytes 3670016 | tf_op jit(solution)/shard_map/all_to_all | solution.py:631
  34.5 3.6 %shard_map.179 = (bf16[9,32,128]{2,1,0:T(8,128)(2,1)}, bf16[9,32,128]{2,1,0:T(8,128)(2,1)}, bf16[8,32,128]{2,1,0:T(8,128)(2,1)}, bf16[8,32,128]{2,1,0:T(8,128)(2,1)}) custom-call(s32[3,32]{1,0:T(4,128)} %refs_0_.9, s32[1]{0:T(128)S(6)} %copy.19.refs_3_.refs_1_.refs_5_, bf16[32,32,512]{2,1,0:T(8,128)(2,1)} %get-tuple-element.41.refs_2_.refs_9_, ...), custom_call_target="tpu_custom_call" | custom-call | flops 3000000000 | bytes 9000000 | tf_op jit(solution)/shard_map/pallas_call | solution.py:560
  38.1 4.8 %collective-permute-start.4 = (bf16[9,32,128]{2,1,0:T(8,128)(2,1)}, bf16[9,32,128]{2,1,0:T(8,128)(2,1)S(1)}, u32[]{:S(2)}, u32[]{:S(2)}) collective-permute-start(bf16[9,32,128]{2,1,0:T(8,128)(2,1)} %get-tuple-element.42), channel_id=1, source_target_pairs={{0,15},{1,0},{2,1},{3,2},{4,3},{5,4},{6,5},{7,6},{8,7},{9,8},{10,9... | collective-permute-start | bytes 221192 | tf_op jit(solution)/shard_map/ppermute | solution.py:588
  42.9 0.0 collective-permute-start.5
  42.9 8.9 %collective-permute-done.4.refs_2_.refs_8_.refs_13_ = bf16[9,32,128]{2,1,0:T(8,128)(2,1)S(1)} collective-permute-done((bf16[9,32,128]{2,1,0:T(8,128)(2,1)}, bf16[9,32,128]{2,1,0:T(8,128)(2,1)S(1)}, u32[]{:S(2)}, u32[]{:S(2)}) %collective-permute-start.4) | collective-permute-done | bytes 73760 | tf_op jit(solution)/shard_map/ppermute | solution.py:588
  51.8 5.1 %collective-permute-done.5.refs_3_.refs_9_.refs_14_ = bf16[9,32,128]{2,1,0:T(8,128)(2,1)S(1)} collective-permute-done((bf16[9,32,128]{2,1,0:T(8,128)(2,1)}, bf16[9,32,128]{2,1,0:T(8,128)(2,1)S(1)}, u32[]{:S(2)}, u32[]{:S(2)}) %collective-permute-start.5) | collective-permute-done | bytes 73760 | tf_op jit(solution)/shard_map/ppermute | solution.py:588
  56.9 0.0 all-to-all-done.refs_0_
  56.9 0.6 copy-done.6
  57.5 0.6 copy-done
  58.2 1.8 %shard_map.180 = (f32[16,8,128]{2,1,0:T(8,128)}, bf16[11,32,128]{2,1,0:T(8,128)(2,1)}, bf16[11,32,128]{2,1,0:T(8,128)(2,1)}) custom-call(bf16[16,16,3584]{2,1,0:T(8,128)(2,1)} %copy-done, f32[8,256]{1,0:T(8,128)} %get-tuple-element.40.refs_4_.refs_1_.refs_2_, bf16[9,32,128]{2,1,0:T(8,128)(2,1)} %copy-done.5, bf16[9,32,128]{2,1,0:T(8,128)(2,1)} %copy-done.6, ...), custom_call_target="tpu_custom_call" | custom-call | flops 1000000000 | bytes 3000000 | tf_op jit(solution)/shard_map/pallas_call | solution.py:560
  60.0 13.2 %all-to-all-start.1 = ((f32[16,8,128]{2,1,0:T(8,128)}), f32[16,8,128]{2,1,0:T(8,128)S(1)}, u32[]{:S(2)}, u32[]{:S(2)}) async-start(f32[16,8,128]{2,1,0:T(8,128)} %get-tuple-element.46), calls=%async_computation.1 | async-start | bytes 131072 | tf_op jit(solution)/shard_map/all_to_all | solution.py:642
  73.1 0.1 collective-permute-start.6
  73.3 1.6 %collective-permute-start.7 = (bf16[11,32,128]{2,1,0:T(8,128)(2,1)}, bf16[11,32,128]{2,1,0:T(8,128)(2,1)S(1)}, u32[]{:S(2)}, u32[]{:S(2)}) collective-permute-start(bf16[11,32,128]{2,1,0:T(8,128)(2,1)} %get-tuple-element.48), channel_id=1, source_target_pairs={{0,16},{16,32},{32,48},{48,64},{64,80},{80,96},{96,112},{112,128},... | collective-permute-start | bytes 270344 | tf_op jit(solution)/shard_map/ppermute | solution.py:588
  74.9 3.6 %collective-permute-done.6.refs_10_.refs_15_ = bf16[11,32,128]{2,1,0:T(8,128)(2,1)S(1)} collective-permute-done((bf16[11,32,128]{2,1,0:T(8,128)(2,1)}, bf16[11,32,128]{2,1,0:T(8,128)(2,1)S(1)}, u32[]{:S(2)}, u32[]{:S(2)}) %collective-permute-start.6) | collective-permute-done | bytes 90144 | tf_op jit(solution)/shard_map/ppermute | solution.py:588
  78.5 0.0 collective-permute-done.7.refs_11_.refs_16_
  78.5 2.5 %all-to-all-done.1.refs_1_ = f32[16,8,128]{2,1,0:T(8,128)S(1)} async-done(((f32[16,8,128]{2,1,0:T(8,128)}), f32[16,8,128]{2,1,0:T(8,128)S(1)}, u32[]{:S(2)}, u32[]{:S(2)}) %all-to-all-start.1) | async-done | bytes 65568 | tf_op jit(solution)/shard_map/all_to_all | solution.py:642
  81.0 0.7 collective-permute-start.8
  81.7 3.8 %shard_map.181 = (f32[32,256]{1,0:T(8,128)}, bf16[27,32,128]{2,1,0:T(8,128)(2,1)}) custom-call(s32[2]{0:T(128)} %pad_add_fusion.refs_14_.refs_0_, f32[16,8,128]{2,1,0:T(8,128)} %copy-done.1, f32[8,256]{1,0:T(8,128)} %get-tuple-element.40.refs_4_.refs_1_.refs_2_, f32[1,256]{1,0:T(1,128)} %bitcast.9, f32[1,256]{1,0:T(1,128)} %bitcast.10, ...), custom_call_target="tpu_custom_call" | custom-call | flops 4000000000 | bytes 12000000 | tf_op jit(solution)/shard_map/pallas_call | solution.py:560
  85.6 0.0 collective-permute-done.8.refs_2_
  85.6 1.2 %copy-done.2 = bf16[256,3584]{1,0:T(8,128)(2,1)} copy-done((bf16[256,3584]{1,0:T(8,128)(2,1)}, bf16[256,3584]{1,0:T(8,128)(2,1)S(1)}, u32[]{:S(2)}) %copy-start.2) | copy-done | bytes 1835032
  86.8 12.6 %shard_map.182 = (bf16[32,32,512]{2,1,0:T(8,128)(2,1)}, bf16[32,32,512]{2,1,0:T(8,128)(2,1)}, bf16[32,32,128]{2,1,0:T(8,128)(2,1)}, bf16[32,32,128]{2,1,0:T(8,12...) custom-call(f32[32,256]{1,0:T(8,128)} %get-tuple-element.53.refs_0_,, ...), custom_call_target="tpu_custom_call" | custom-call | flops 12000000000 | bytes 36000000 | tf_op jit(solution)/shard_map/pallas_call | solution.py:560
  99.4 2.6 %collective-permute-start.9 = (bf16[8,32,128]{2,1,0:T(8,128)(2,1)}, bf16[8,32,128]{2,1,0:T(8,128)(2,1)S(1)}, u32[]{:S(2)}, u32[]{:S(2)}) collective-permute-start(bf16[8,32,128]{2,1,0:T(8,128)(2,1)} %get-tuple-element.58), channel_id=1, source_target_pairs={{0,15},{1,0},{2,1},{3,2},{4,3},{5,4},{6,5},{7,6},{8,7},{9,8},{10,9... | collective-permute-start | bytes 196616 | tf_op jit(solution)/shard_map/ppermute | solution.py:588
  102.0 0.0 collective-permute-start.10
  102.0 0.8 collective-permute-start.11
  102.8 0.9 collective-permute-start.12
  103.7 1.3 %reshape.19 = bf16[2,2,2,256]{3,2,1,0:T(2,128)(2,1)} reshape(bf16[8,256]{1,0:T(8,128)(2,1)} %get-tuple-element.63) | data formatting | bytes 8192 | tf_op jit(solution)/shard_map/reshape | solution.py:670
  105.0 0.0 collective-permute-done.9.refs_7_
  105.0 3.6 %collective-permute-done.10.refs_8_ = bf16[8,32,128]{2,1,0:T(8,128)(2,1)S(1)} collective-permute-done((bf16[8,32,128]{2,1,0:T(8,128)(2,1)}, bf16[8,32,128]{2,1,0:T(8,128)(2,1)S(1)}, u32[]{:S(2)}, u32[]{:S(2)}) %collective-permute-start.10) | collective-permute-done | bytes 65568 | tf_op jit(solution)/shard_map/ppermute | solution.py:588
  108.6 0.0 collective-permute-done.11.refs_9_
  108.6 0.6 copy-done.12
  109.2 0.0 copy-done.13
  109.3 0.0 copy-done.14
  109.3 8.0 %shard_map.183 = bf16[32,32,512]{2,1,0:T(8,128)(2,1)} custom-call(s32[3,32]{1,0:T(4,128)} %refs_0_.9, s32[1]{0:T(128)S(6)} %copy.19.refs_3_.refs_1_.refs_5_, s32[6,32]{1,0:T(8,128)} %refs_2_.5, bf16[3,32,224]{2,1,0:T(8,128)(2,1)} %refs_3_.7, bf16[32,32,512]{2,1,0:T(8,128)(2,1)} %get-tuple-element.55.refs_4_, bf16[32,32,128]{2,1,0:T(8,128)(2,1)} %get-tuple-element.56.refs_5_, ...), custom_call_target="tpu_custom_call" | custom-call | flops 7000000000 | bytes 21000000 | tf_op jit(solution)/shard_map/pallas_call | solution.py:560
  (22 shorter events, 0.0 us)
Async XLA Ops:
  5.0 11.8 %collective-permute-start = (bf16[8,32,128]{2,1,0:T(8,128)(2,1)}, bf16[8,32,128]{2,1,0:T(8,128)(2,1)S(1)}, u32[]{:S(2)}, u32[]{:S(2)}) collective-permute-start(bf16[8,32,128]{2,1,0:T(8,128)(2,1)} %get-tuple-element.35), channel_id=1, source_target_pairs={{0,15},{1,0},{2,1},{3,2},{4,3},{5,4},{6,5},{7,6},{8,7},{9,8},{10,9... | collective-permute-start | bytes 196616 | tf_op jit(solution)/shard_map/ppermute | solution.py:588
  10.9 6.6 %collective-permute-start.1 = (bf16[8,32,128]{2,1,0:T(8,128)(2,1)}, bf16[8,32,128]{2,1,0:T(8,128)(2,1)S(1)}, u32[]{:S(2)}, u32[]{:S(2)}) collective-permute-start(bf16[8,32,128]{2,1,0:T(8,128)(2,1)} %get-tuple-element.36), channel_id=1, source_target_pairs={{0,1},{1,2},{2,3},{3,4},{4,5},{5,6},{6,7},{7,8},{8,9},{9,10},{10,1... | collective-permute-start | bytes 196616 | tf_op jit(solution)/shard_map/ppermute | solution.py:588
  10.9 6.6 %collective-permute-start.2 = (bf16[8,32,128]{2,1,0:T(8,128)(2,1)}, bf16[8,32,128]{2,1,0:T(8,128)(2,1)S(1)}, u32[]{:S(2)}, u32[]{:S(2)}) collective-permute-start(bf16[8,32,128]{2,1,0:T(8,128)(2,1)} %get-tuple-element.37), channel_id=1, source_target_pairs={{0,240},{16,0},{32,16},{48,32},{64,48},{80,64},{96,80},{112,96},{1... | collective-permute-start | bytes 196616 | tf_op jit(solution)/shard_map/ppermute | solution.py:588
  11.8 6.0 %collective-permute-start.3 = (bf16[8,32,128]{2,1,0:T(8,128)(2,1)}, bf16[8,32,128]{2,1,0:T(8,128)(2,1)S(1)}, u32[]{:S(2)}, u32[]{:S(2)}) collective-permute-start(bf16[8,32,128]{2,1,0:T(8,128)(2,1)} %get-tuple-element.38), channel_id=1, source_target_pairs={{0,16},{16,32},{32,48},{48,64},{64,80},{80,96},{96,112},{112,128},... | collective-permute-start | bytes 196616 | tf_op jit(solution)/shard_map/ppermute | solution.py:588
  16.9 0.9 copy-start.7
  17.5 0.6 copy-start.8
  17.5 0.6 copy-start.9
  17.8 0.6 copy-start.10
  28.3 28.6 %all-to-all-start = ((bf16[16,16,3584]{2,1,0:T(8,128)(2,1)}), bf16[16,16,3584]{2,1,0:T(8,128)(2,1)S(1)}, u32[]{:S(2)}, u32[]{:S(2)}) async-start(bf16[16,16,3584]{2,1,0:T(8,128)(2,1)} %get-tuple-element.39), calls=%async_computation | async-start | bytes 3670016 | tf_op jit(solution)/shard_map/all_to_all | solution.py:631
  38.1 13.7 %collective-permute-start.4 = (bf16[9,32,128]{2,1,0:T(8,128)(2,1)}, bf16[9,32,128]{2,1,0:T(8,128)(2,1)S(1)}, u32[]{:S(2)}, u32[]{:S(2)}) collective-permute-start(bf16[9,32,128]{2,1,0:T(8,128)(2,1)} %get-tuple-element.42), channel_id=1, source_target_pairs={{0,15},{1,0},{2,1},{3,2},{4,3},{5,4},{6,5},{7,6},{8,7},{9,8},{10,9... | collective-permute-start | bytes 221192 | tf_op jit(solution)/shard_map/ppermute | solution.py:588
  42.9 14.0 %collective-permute-start.5 = (bf16[9,32,128]{2,1,0:T(8,128)(2,1)}, bf16[9,32,128]{2,1,0:T(8,128)(2,1)S(1)}, u32[]{:S(2)}, u32[]{:S(2)}) collective-permute-start(bf16[9,32,128]{2,1,0:T(8,128)(2,1)} %get-tuple-element.43), channel_id=1, source_target_pairs={{0,1},{1,2},{2,3},{3,4},{4,5},{5,6},{6,7},{7,8},{8,9},{9,10},{10,1... | collective-permute-start | bytes 221192 | tf_op jit(solution)/shard_map/ppermute | solution.py:588
  51.8 5.1 %copy-start.5 = (bf16[9,32,128]{2,1,0:T(8,128)(2,1)}, bf16[9,32,128]{2,1,0:T(8,128)(2,1)S(1)}, u32[]{:S(2)}) copy-start(bf16[9,32,128]{2,1,0:T(8,128)(2,1)S(1)} %collective-permute-done.4.refs_2_.refs_8_.refs_13_) | copy-start | bytes 221188
  56.9 0.6 copy-start.6
  56.9 1.3 %copy-start = (bf16[16,16,3584]{2,1,0:T(8,128)(2,1)}, bf16[16,16,3584]{2,1,0:T(8,128)(2,1)S(1)}, u32[]{:S(2)}) copy-start(bf16[16,16,3584]{2,1,0:T(8,128)(2,1)S(1)} %all-to-all-done.refs_0_) | copy-start | bytes 5505028
  60.0 21.0 %all-to-all-start.1 = ((f32[16,8,128]{2,1,0:T(8,128)}), f32[16,8,128]{2,1,0:T(8,128)S(1)}, u32[]{:S(2)}, u32[]{:S(2)}) async-start(f32[16,8,128]{2,1,0:T(8,128)} %get-tuple-element.46), calls=%async_computation.1 | async-start | bytes 131072 | tf_op jit(solution)/shard_map/all_to_all | solution.py:642
  73.1 5.3 %collective-permute-start.6 = (bf16[11,32,128]{2,1,0:T(8,128)(2,1)}, bf16[11,32,128]{2,1,0:T(8,128)(2,1)S(1)}, u32[]{:S(2)}, u32[]{:S(2)}) collective-permute-start(bf16[11,32,128]{2,1,0:T(8,128)(2,1)} %get-tuple-element.47), channel_id=1, source_target_pairs={{0,240},{16,0},{32,16},{48,32},{64,48},{80,64},{96,80},{112,96},{1... | collective-permute-start | bytes 270344 | tf_op jit(solution)/shard_map/ppermute | solution.py:588
  73.3 5.2 %collective-permute-start.7 = (bf16[11,32,128]{2,1,0:T(8,128)(2,1)}, bf16[11,32,128]{2,1,0:T(8,128)(2,1)S(1)}, u32[]{:S(2)}, u32[]{:S(2)}) collective-permute-start(bf16[11,32,128]{2,1,0:T(8,128)(2,1)} %get-tuple-element.48), channel_id=1, source_target_pairs={{0,16},{16,32},{32,48},{48,64},{64,80},{80,96},{96,112},{112,128},... | collective-permute-start | bytes 270344 | tf_op jit(solution)/shard_map/ppermute | solution.py:588
  78.4 3.2 %copy-start.3 = (bf16[11,32,128]{2,1,0:T(8,128)(2,1)}, bf16[11,32,128]{2,1,0:T(8,128)(2,1)S(1)}, u32[]{:S(2)}) copy-start(bf16[11,32,128]{2,1,0:T(8,128)(2,1)S(1)} %collective-permute-done.6.refs_10_.refs_15_) | copy-start | bytes 270340
  78.5 3.2 %copy-start.4 = (bf16[11,32,128]{2,1,0:T(8,128)(2,1)}, bf16[11,32,128]{2,1,0:T(8,128)(2,1)S(1)}, u32[]{:S(2)}) copy-start(bf16[11,32,128]{2,1,0:T(8,128)(2,1)S(1)} %collective-permute-done.7.refs_11_.refs_16_) | copy-start | bytes 270340
  81.0 0.7 copy-start.1
  81.0 4.6 %collective-permute-start.8 = (bf16[256,3584]{1,0:T(8,128)(2,1)}, bf16[256,3584]{1,0:T(8,128)(2,1)S(1)}, u32[]{:S(2)}, u32[]{:S(2)}) collective-permute-start(bf16[256,3584]{1,0:T(8,128)(2,1)} %bitcast.6), channel_id=1, source_target_pairs={{0,16},{16,0},{1,17},{17,1},{2,18},{18,2},{3,19},{19,3},{4,20},{20... | collective-permute-start | bytes 5505032 | tf_op jit(solution)/shard_map/ppermute | solution.py:648
  85.6 1.2 %copy-start.2 = (bf16[256,3584]{1,0:T(8,128)(2,1)}, bf16[256,3584]{1,0:T(8,128)(2,1)S(1)}, u32[]{:S(2)}) copy-start(bf16[256,3584]{1,0:T(8,128)(2,1)S(1)} %collective-permute-done.8.refs_2_) | copy-start | bytes 5505028
  99.4 5.6 %collective-permute-start.9 = (bf16[8,32,128]{2,1,0:T(8,128)(2,1)}, bf16[8,32,128]{2,1,0:T(8,128)(2,1)S(1)}, u32[]{:S(2)}, u32[]{:S(2)}) collective-permute-start(bf16[8,32,128]{2,1,0:T(8,128)(2,1)} %get-tuple-element.58), channel_id=1, source_target_pairs={{0,15},{1,0},{2,1},{3,2},{4,3},{5,4},{6,5},{7,6},{8,7},{9,8},{10,9... | collective-permute-start | bytes 196616 | tf_op jit(solution)/shard_map/ppermute | solution.py:588
  102.0 6.6 %collective-permute-start.10 = (bf16[8,32,128]{2,1,0:T(8,128)(2,1)}, bf16[8,32,128]{2,1,0:T(8,128)(2,1)S(1)}, u32[]{:S(2)}, u32[]{:S(2)}) collective-permute-start(bf16[8,32,128]{2,1,0:T(8,128)(2,1)} %get-tuple-element.59), channel_id=1, source_target_pairs={{0,1},{1,2},{2,3},{3,4},{4,5},{5,6},{6,7},{7,8},{8,9},{9,10},{10,1... | collective-permute-start | bytes 196616 | tf_op jit(solution)/shard_map/ppermute | solution.py:588
  102.0 6.6 %collective-permute-start.11 = (bf16[8,32,128]{2,1,0:T(8,128)(2,1)}, bf16[8,32,128]{2,1,0:T(8,128)(2,1)S(1)}, u32[]{:S(2)}, u32[]{:S(2)}) collective-permute-start(bf16[8,32,128]{2,1,0:T(8,128)(2,1)} %get-tuple-element.60), channel_id=1, source_target_pairs={{0,240},{16,0},{32,16},{48,32},{64,48},{80,64},{96,80},{112,96},{1... | collective-permute-start | bytes 196616 | tf_op jit(solution)/shard_map/ppermute | solution.py:588
  102.8 5.8 %collective-permute-start.12 = (bf16[8,32,128]{2,1,0:T(8,128)(2,1)}, bf16[8,32,128]{2,1,0:T(8,128)(2,1)S(1)}, u32[]{:S(2)}, u32[]{:S(2)}) collective-permute-start(bf16[8,32,128]{2,1,0:T(8,128)(2,1)} %get-tuple-element.61), channel_id=1, source_target_pairs={{0,16},{16,32},{32,48},{48,64},{64,80},{80,96},{96,112},{112,128},... | collective-permute-start | bytes 196616 | tf_op jit(solution)/shard_map/ppermute | solution.py:588
  105.0 3.6 %copy-start.11 = (bf16[8,32,128]{2,1,0:T(8,128)(2,1)}, bf16[8,32,128]{2,1,0:T(8,128)(2,1)S(1)}, u32[]{:S(2)}) copy-start(bf16[8,32,128]{2,1,0:T(8,128)(2,1)S(1)} %collective-permute-done.9.refs_7_) | copy-start | bytes 196612
  108.6 0.6 copy-start.12
  108.6 0.6 copy-start.13
  108.6 0.7 copy-start.14

commit v4 on v3

--- a/solution.py
+++ b/solution.py
@@ -95,7 +95,8 @@
 
 def fill_planes(coords, counts, y_bank, z_bank, work, outs):
     lane = lanes()
-    work[...] = jnp.zeros_like(work)
+    for plane in work:
+        plane[...] = jnp.zeros_like(plane)
     in_low = (lane & 32) == 0
     in_back = lane >= 64
 
@@ -110,19 +111,19 @@
         for plane, edge, low in ((0, 0, True), (1, 3, False)):
             row = jnp.where(live & (y == edge), y_row, 8)
             mask = jnp.logical_xor(in_low if low else jnp.logical_not(in_low), odd)
-            work[plane, row] = jnp.where(mask, value, work[plane, row])
+            work[plane][row] = jnp.where(mask, value, work[plane][row])
         face = z_bank[j]
         turned = pltpu.roll(face, 64, 1)
         value = jnp.where(odd, turned, face)
         for plane, edge, low in ((2, 0, True), (3, 3, False)):
             row = jnp.where(live & (z == edge), z_row, 8)
             mask = jnp.logical_xor(in_back if low else jnp.logical_not(in_back), odd)
-            work[plane, row] = jnp.where(mask, value, work[plane, row])
+            work[plane][row] = jnp.where(mask, value, work[plane][row])
         return carry
 
     lax.fori_loop(0, BLOCKS, one, 0, unroll=4)
     for plane, out in enumerate(outs):
-        out[0:8] = work[plane, :8]
+        out[0:8] = work[plane][0:8]
 
 
 def received(plane_ref, p, back):
@@ -167,38 +168,49 @@
         half = [z_down] + [pltpu.roll(own[k], 64, 1) for k in range(4)] + [z_up]
         for k in range(4):
             to = tile(k)
-            taps[slot, 0:32, to] = own[k]
-            taps[slot, 32:64, to] = jnp.where(
+            taps[slot][0:32, to] = own[k]
+            taps[slot][32:64, to] = jnp.where(
                 along_x == 7,
                 pltpu.roll(signal[x_up, :, to], 7, 1),
                 pltpu.roll(own[k], 127, 1),
             )
-            taps[slot, 64:96, to] = jnp.where(
+            taps[slot][64:96, to] = jnp.where(
                 along_x == 0,
                 pltpu.roll(signal[x_down, :, to], 121, 1),
                 pltpu.roll(own[k], 1, 1),
             )
-            taps[slot, 96:128, to] = jnp.where(
+            taps[slot][96:128, to] = jnp.where(
                 along_yx >= 56, pltpu.roll(y_up, 56 - 8 * k, 1), pltpu.roll(own[k], 120, 1)
             )
-            taps[slot, 128:160, to] = jnp.where(
+            taps[slot][128:160, to] = jnp.where(
                 along_yx < 8, pltpu.roll(y_down, 96 - 8 * k, 1), pltpu.roll(own[k], 8, 1)
             )
-            taps[slot, 160:192, to] = jnp.where(front, half[k + 1], half[k + 2])
-            taps[slot, 192:224, to] = jnp.where(front, half[k], half[k + 1])
+            taps[slot][160:192, to] = jnp.where(front, half[k + 1], half[k + 2])
+            taps[slot][192:224, to] = jnp.where(front, half[k], half[k + 1])
+
+    def product(j, slot):
+        finish(j, jnp.dot(weight[...], taps[slot][...], preferred_element_type=f32))
+
+    build(0, 0)
+    build(1, 1)
 
     def some(i, carry):
-        for u in range(4):
-            build(i * 4 + u, u)
-        for u in range(4):
-            result = jnp.dot(weight[...], taps[u], preferred_element_type=f32)
-            finish(i * 4 + u, result)
+        j = i * 4
+        build(j + 2, 2)
+        product(j, 0)
+        build(j + 3, 3)
+        product(j + 1, 1)
+        after = jnp.minimum(j + 4, BLOCKS - 2)
+        build(after, 0)
+        product(j + 2, 2)
+        build(after + 1, 1)
+        product(j + 3, 3)
         return carry
 
     lax.fori_loop(0, BLOCKS // 4, some, 0)
 
 
-def first_faces(ins, outs, work):
+def first_faces(ins, outs, *work):
     features, faces, coords, counts = ins
     y_own, z_own, *planes = outs
     base, faces = features.get(), faces.get()
@@ -251,9 +263,10 @@
     return jnp.concatenate([row[:, :128], row[:, 128:]], axis=0)
 
 
-def first_conv(ins, outs, signal, y_bank, z_bank, taps, gathered):
+def first_conv(ins, outs, signal, y_bank, z_bank, *taps_gathered):
     (coords, counts, links, weights, signal_in, y_own, z_own, *planes, features, pool, down, where, weight_columns) = ins
     level, own_tile, message = outs
+    *taps, gathered = taps_gathered
     coords, counts, links, weight = coords.get(), counts.get(), links.get(), weights.get().at[0]
     signal[BLOCKS] = jnp.zeros((CHANS, VOXELS), bf16)
     bank_received([p.get() for p in planes], y_bank, z_bank)
@@ -265,6 +278,7 @@
     half = weight_columns.get()[:, pl.ds(start, HALF_ROWS)]
     for i in range(16):
         message.ref[i, :, :HALF_ROWS] = half
+    message.send(0)
 
     def finish(j, result):
         level_ref[j] = (base[j].astype(f32) + result).astype(bf16)
@@ -298,7 +312,7 @@
     own_tile.ref[...] = total
 
 
-def level_faces(ins, outs, y_bank, z_bank, work):
+def level_faces(ins, outs, y_bank, z_bank, *work):
     coords, counts, level, faces, own_tile = (one.get() for one in ins)
     take_faces(level, faces, y_bank, z_bank)
     fill_planes(coords, counts, y_bank, z_bank, work, [p.ref for p in outs])
@@ -407,10 +421,11 @@
         outs[1].ref[t] = patches[TAPS - base + t]
 
 
-def second_conv(ins, outs, joined, signal, y_bank, z_bank, taps, work, lifted, rows):
+def second_conv(ins, outs, joined, signal, y_bank, z_bank, *rest):
     (total, far_patches, far_half, up, coords, counts, links, weights, spread, level, faces,
      y_spread, z_spread, *planes) = ins
     second, signal2, y_own, z_own, *sent, coarse = outs
+    taps, work, (lifted, rows) = rest[:4], rest[4:8], rest[8:]
     far_patches = far_patches.get()
     total = times_half(total.get()[...], lambda t: far_patches[t], far_half.get())
     r0, r1, r2, r3 = (p.get() for p in planes)
@@ -481,7 +496,7 @@
     fill_planes(coords, counts, y_own.ref, z_own.ref, work, [p.ref for p in sent])
 
 
-def third_conv(ins, outs, signal, y_bank, z_bank, taps):
+def third_conv(ins, outs, signal, y_bank, z_bank, *taps):
     (coords, counts, links, weights, signal_in, y_own, z_own, *planes, second) = ins
     coords, counts, links, weight = coords.get(), counts.get(), links.get(), weights.get().at[2]
     signal[BLOCKS] = jnp.zeros((CHANS, VOXELS), bf16)
@@ -511,12 +526,14 @@
 
 
 class Leaving:
-    def __init__(self, copy, ref):
-        self.copy, self.ref, self.sent = copy, ref, False
-
-    def send(self):
-        self.copy.start()
-        self.sent = True
+    def __init__(self, copies, ref):
+        self.copies, self.ref, self.sent = copies, ref, set()
+
+    def send(self, *which):
+        for i in which or range(len(self.copies)):
+            if i not in self.sent:
+                self.copies[i].start()
+                self.sent.add(i)
 
 
 def call(kernel, arrays, outs, scratch, microseconds, spare=()):
@@ -535,18 +552,25 @@
             ref = placed[i] if i in placed else to(*work)
             source = ins[i].at[:, :, to] if isinstance(to, slice) else ins[i]
             arriving.append(Arriving(pltpu.make_async_copy(source, ref, in_sem.at[i]), ref))
-        leaving = [
-            Leaving(pltpu.make_async_copy(staged[i], results[i], out_sem.at[i]), staged[i])
-            for i in range(len(outs))
-        ]
+        leaving = []
+        for i, (_, _, *cut) in enumerate(outs):
+            pairs = [(staged[i], results[i])]
+            if cut:
+                pairs = [(a.at[:, :, to], b.at[:, :, to]) for a, b in pairs for to in cut]
+            leaving.append(
+                Leaving(
+                    [pltpu.make_async_copy(a, b, out_sem.at[2 * i + k]) for k, (a, b) in enumerate(pairs)],
+                    staged[i],
+                )
+            )
         kernel(arriving, leaving, *work)
         for one in arriving:
             one.get()
         for one in leaving:
-            if not one.sent:
-                one.send()
+            one.send()
         for one in leaving:
-            one.copy.wait()
+            for copy in one.copies:
+                copy.wait()
 
     hbm = pl.BlockSpec(memory_space=pltpu.HBM)
     buffers = []
@@ -556,14 +580,14 @@
             shape = (*shape[:-1], to.stop - to.start)
         space = pltpu.SMEM if to == "smem" else pltpu.VMEM
         buffers.append(space(shape, arrays[i][0].dtype))
-    buffers += [pltpu.VMEM(s, d) for s, d in (*outs, *scratch)]
+    buffers += [pltpu.VMEM(s, d) for s, d, *_ in (*outs, *scratch)]
     return pl.pallas_call(
         body,
         in_specs=[hbm] * total,
         out_specs=[hbm] * len(outs),
-        out_shape=[jax.ShapeDtypeStruct(s, d) for s, d in outs],
+        out_shape=[jax.ShapeDtypeStruct(s, d) for s, d, *_ in outs],
         scratch_shapes=buffers
-        + [pltpu.SemaphoreType.DMA((count,)), pltpu.SemaphoreType.DMA((len(outs),))],
+        + [pltpu.SemaphoreType.DMA((count,)), pltpu.SemaphoreType.DMA((2 * len(outs),))],
         compiler_params=pltpu.CompilerParams(vmem_limit_bytes=60 << 20),
         cost_estimate=pl.CostEstimate(
             flops=microseconds * 1_000_000_000,
@@ -578,9 +602,9 @@
 PLANE = ((8, CHANS, 128), bf16)
 SIGNAL = ((BLOCKS + 1, CHANS, VOXELS), bf16)
 BANK = ((BLOCKS + 33, CHANS, 128), bf16)
-TAP_STACK = ((4, 7 * CHANS, VOXELS), bf16)
+TAP_STACK = (((7 * CHANS, VOXELS), bf16),) * 4
 SUMS = ((16, 8, 128), f32)
-WORK = ((4, 9, CHANS, 128), bf16)
+WORK = (((9, CHANS, 128), bf16),) * 4
 
 
 def shifted(x, axes, step):
@@ -617,7 +641,7 @@
     )
     *own, low_y, high_y, low_z, high_z = call(
         first_faces, (*plainly(features, faces), *live[:2]),
-        (FACES, FACES) + (PLANE,) * 4, (WORK,), 3,
+        (FACES, FACES) + (PLANE,) * 4, WORK, 3,
     )
     planes = swap_planes((low_y, high_y, low_z, high_z))
     (signal,) = call(activate, plainly(features), (FIELD,), (), 3)
@@ -625,13 +649,13 @@
         first_conv,
         (*live, (fine_weights, None), *zip((signal, *own), place_own),
          *plainly(*planes, features, pool, down_weight), (where, "smem"), (coarse_weight.T, None)),
-        (FIELD, ((8, COARSE), f32), ((16, 16, HALF_ROWS + 128), bf16)),
-        (SIGNAL, BANK, BANK, TAP_STACK, ((9, 16, COARSE), f32)), 8,
+        (FIELD, ((8, COARSE), f32), ((16, 16, HALF_ROWS + 128), bf16, slice(0, HALF_ROWS), slice(HALF_ROWS, HALF_ROWS + 128))),
+        (SIGNAL, BANK, BANK, *TAP_STACK, ((9, 16, COARSE), f32)), 8,
     )
     message = lax.all_to_all(message, MY, 0, 0)
     low_y, high_y, low_z, high_z = call(
         level_faces, (*live[:2], *plainly(level, faces, own_tile)),
-        (((9, CHANS, 128), bf16),) * 2 + (PLANE,) * 2, (FACES, FACES, WORK), 3,
+        (((9, CHANS, 128), bf16),) * 2 + (PLANE,) * 2, (FACES, FACES, *WORK), 3,
     )
     y_above, y_below = shifted(low_y, MY, -1), shifted(high_y, MY, 1)
     partial, low_z, high_z = call(
@@ -660,12 +684,12 @@
         (*plainly(*front, far_half, up_weight), *live,
          *plainly(fine_weights, spread, level, faces, y_spread, z_spread, *planes)),
         (FIELD, FIELD, FACES, FACES) + (PLANE,) * 4 + (((8, COARSE), bf16),),
-        (FIELD, SIGNAL, BANK, BANK, TAP_STACK, WORK, ((8, 32, COARSE), f32), ((256, 256), bf16)), 12,
+        (FIELD, SIGNAL, BANK, BANK, *TAP_STACK, *WORK, ((8, 32, COARSE), f32), ((256, 256), bf16)), 12,
     )
     planes = swap_planes((low_y, high_y, low_z, high_z))
     (fine_out,) = call(
         third_conv, (*live, (fine_weights, None), *zip(own, place_own), *plainly(*planes, second)),
-        (FIELD,), (SIGNAL, BANK, BANK, TAP_STACK), 7,
+        (FIELD,), (SIGNAL, BANK, BANK, *TAP_STACK), 7,
     )
     return fine_out, coarse.reshape(2, 2, 2, COARSE)
 

time: 118 us -> 112 us (0.949)
  Pallas kernels: 46.2 us -> 40.1 us
    pallas_call x8, Pallas kernels: 46.2 us -> 40.1 us  [call(): pl.pallas_call(body, in_specs=[hbm] * total, out_specs=[hbm] * len(outs),...]
where the time goes in v4:
time: 112 us; the launch traced here: 111 us
  Pallas kernels  40.1 us (36%)
  starting transfers between devices  39.2 us (35%)
  waiting for transfers between devices  24.9 us (22%)
  local copies, waits for them, and re-layouts  5.08 us (5%)
  between operations  1.42 us (1%)
    pallas_call x8, Pallas kernels, call(): pl.pallas_call(body, in_specs=[hbm] * total, out_specs=[hbm] * len(outs),...  40.1 us
    ppermute x12, waiting for transfers between devices, shifted(): lax.ppermute(x, axes, [(i, (i + step) % count) for i in range(count)])  22.4 us
    ppermute x12, starting transfers between devices, shifted(): lax.ppermute(x, axes, [(i, (i + step) % count) for i in range(count)])  19.1 us
    all_to_all x1, starting transfers between devices, local(): partial = lax.all_to_all(partial, MX, 0, 0)  13.2 us
    all_to_all x1, starting transfers between devices, local(): message = lax.all_to_all(message, MY, 0, 0)  6.18 us
    unnamed x30, local copies, waits for them, and re-layouts  3.79 us
    all_to_all x1, waiting for transfers between devices, local(): partial = lax.all_to_all(partial, MX, 0, 0)  2.52 us
  transfers between devices with their start and end apart: 15, of which 7 were waited for; matrix products, arithmetic and copies ran while one was open for 2% of the time, Pallas kernels for 9%

profile of v4, /device:TPU:1, one launch (start us, length us, event | category | flops | bytes accessed | tf_op | source)
XLA Modules:
  0.0 111.3 jit_solution(16787864053646838325)
XLA Ops:
  1.3 3.5 %shard_map.177 = (bf16[32,32,128]{2,1,0:T(8,128)(2,1)}, bf16[32,32,128]{2,1,0:T(8,128)(2,1)}, bf16[8,32,128]{2,1,0:T(8,128)(2,1)}, bf16[8,32,128]{2,1,0:T(8,128)...) custom-call(bf16[32,32,512]{2,1,0:T(8,128)(2,1)} %refs_11_.2, ...), custom_call_target="tpu_custom_call" | custom-call | flops 3000000000 | bytes 9000000 | tf_op jit(solution)/shard_map/pallas_call | solution.py:584
  4.8 5.8 %collective-permute-start = (bf16[8,32,128]{2,1,0:T(8,128)(2,1)}, bf16[8,32,128]{2,1,0:T(8,128)(2,1)S(1)}, u32[]{:S(2)}, u32[]{:S(2)}) collective-permute-start(bf16[8,32,128]{2,1,0:T(8,128)(2,1)} %get-tuple-element.35), channel_id=1, source_target_pairs={{0,15},{1,0},{2,1},{3,2},{4,3},{5,4},{6,5},{7,6},{8,7},{9,8},{10,9... | collective-permute-start | bytes 196616 | tf_op jit(solution)/shard_map/ppermute | solution.py:612
  10.6 0.0 collective-permute-start.1
  10.6 1.0 collective-permute-start.2
  11.6 1.5 %collective-permute-start.3 = (bf16[8,32,128]{2,1,0:T(8,128)(2,1)}, bf16[8,32,128]{2,1,0:T(8,128)(2,1)S(1)}, u32[]{:S(2)}, u32[]{:S(2)}) collective-permute-start(bf16[8,32,128]{2,1,0:T(8,128)(2,1)} %get-tuple-element.38), channel_id=1, source_target_pairs={{0,16},{16,32},{32,48},{48,64},{64,80},{80,96},{96,112},{112,128},... | collective-permute-start | bytes 196616 | tf_op jit(solution)/shard_map/ppermute | solution.py:612
  13.1 2.9 %shard_map.176.refs_4_ = bf16[32,32,512]{2,1,0:T(8,128)(2,1)} custom-call(bf16[32,32,512]{2,1,0:T(8,128)(2,1)} %refs_11_.2), custom_call_target="tpu_custom_call" | custom-call | flops 3000000000 | bytes 9000000 | tf_op jit(solution)/shard_map/pallas_call | solution.py:584
  16.0 0.7 pad_add_fusion.refs_14_.refs_0_
  16.6 0.0 collective-permute-done.refs_7_
  16.7 0.6 collective-permute-done.1.refs_8_
  17.3 0.0 collective-permute-done.2.refs_9_
  17.3 0.3 collective-permute-done.3.refs_10_
  17.6 0.3 copy-done.8
  17.9 0.0 copy-done.9
  17.9 0.3 copy-done.10
  18.2 7.6 %shard_map.178 = (bf16[32,32,512]{2,1,0:T(8,128)(2,1)}, f32[8,256]{1,0:T(8,128)}, bf16[16,16,3584]{2,1,0:T(8,128)(2,1)}) custom-call(s32[3,32]{1,0:T(4,128)} %refs_0_.9, s32[1]{0:T(128)S(6)} %copy.19.refs_3_.refs_1_.refs_5_, s32[6,32]{1,0:T(8,128)} %refs_2_.5, bf16[3,32,224]{2,1,0:T(8,128)(2,1)} %refs_3_.7, bf16[32,32,512]{2,1,0:T(8,128)(2,1)} %shard_map.176.refs_4_, ...), custom_call_target="tpu_custom_call" | custom-call | flops 8000000000 | bytes 24000000 | tf_op jit(solution)/shard_map/pallas_call | solution.py:584
  25.8 6.2 %all-to-all-start = ((bf16[16,16,3584]{2,1,0:T(8,128)(2,1)}), bf16[16,16,3584]{2,1,0:T(8,128)(2,1)S(1)}, u32[]{:S(2)}, u32[]{:S(2)}) async-start(bf16[16,16,3584]{2,1,0:T(8,128)(2,1)} %get-tuple-element.39), calls=%async_computation | async-start | bytes 3670016 | tf_op jit(solution)/shard_map/all_to_all | solution.py:655
  32.0 3.4 %shard_map.179 = (bf16[9,32,128]{2,1,0:T(8,128)(2,1)}, bf16[9,32,128]{2,1,0:T(8,128)(2,1)}, bf16[8,32,128]{2,1,0:T(8,128)(2,1)}, bf16[8,32,128]{2,1,0:T(8,128)(2,1)}) custom-call(s32[3,32]{1,0:T(4,128)} %refs_0_.9, s32[1]{0:T(128)S(6)} %copy.19.refs_3_.refs_1_.refs_5_, bf16[32,32,512]{2,1,0:T(8,128)(2,1)} %get-tuple-element.41.refs_2_.refs_9_, ...), custom_call_target="tpu_custom_call" | custom-call | flops 3000000000 | bytes 9000000 | tf_op jit(solution)/shard_map/pallas_call | solution.py:584
  35.4 4.8 %collective-permute-start.4 = (bf16[9,32,128]{2,1,0:T(8,128)(2,1)}, bf16[9,32,128]{2,1,0:T(8,128)(2,1)S(1)}, u32[]{:S(2)}, u32[]{:S(2)}) collective-permute-start(bf16[9,32,128]{2,1,0:T(8,128)(2,1)} %get-tuple-element.42), channel_id=1, source_target_pairs={{0,15},{1,0},{2,1},{3,2},{4,3},{5,4},{6,5},{7,6},{8,7},{9,8},{10,9... | collective-permute-start | bytes 221192 | tf_op jit(solution)/shard_map/ppermute | solution.py:612
  40.2 0.0 collective-permute-start.5
  40.2 9.2 %collective-permute-done.4.refs_2_.refs_8_.refs_13_ = bf16[9,32,128]{2,1,0:T(8,128)(2,1)S(1)} collective-permute-done((bf16[9,32,128]{2,1,0:T(8,128)(2,1)}, bf16[9,32,128]{2,1,0:T(8,128)(2,1)S(1)}, u32[]{:S(2)}, u32[]{:S(2)}) %collective-permute-start.4) | collective-permute-done | bytes 73760 | tf_op jit(solution)/shard_map/ppermute | solution.py:612
  49.3 5.1 %collective-permute-done.5.refs_3_.refs_9_.refs_14_ = bf16[9,32,128]{2,1,0:T(8,128)(2,1)S(1)} collective-permute-done((bf16[9,32,128]{2,1,0:T(8,128)(2,1)}, bf16[9,32,128]{2,1,0:T(8,128)(2,1)S(1)}, u32[]{:S(2)}, u32[]{:S(2)}) %collective-permute-start.5) | collective-permute-done | bytes 73760 | tf_op jit(solution)/shard_map/ppermute | solution.py:612
  54.5 0.0 all-to-all-done.refs_0_
  54.5 0.6 copy-done.6
  55.1 0.6 copy-done
  55.7 1.8 %shard_map.180 = (f32[16,8,128]{2,1,0:T(8,128)}, bf16[11,32,128]{2,1,0:T(8,128)(2,1)}, bf16[11,32,128]{2,1,0:T(8,128)(2,1)}) custom-call(bf16[16,16,3584]{2,1,0:T(8,128)(2,1)} %copy-done, f32[8,256]{1,0:T(8,128)} %get-tuple-element.40.refs_4_.refs_1_.refs_2_, bf16[9,32,128]{2,1,0:T(8,128)(2,1)} %copy-done.5, bf16[9,32,128]{2,1,0:T(8,128)(2,1)} %copy-done.6, ...), custom_call_target="tpu_custom_call" | custom-call | flops 1000000000 | bytes 3000000 | tf_op jit(solution)/shard_map/pallas_call | solution.py:584
  57.6 13.2 %all-to-all-start.1 = ((f32[16,8,128]{2,1,0:T(8,128)}), f32[16,8,128]{2,1,0:T(8,128)S(1)}, u32[]{:S(2)}, u32[]{:S(2)}) async-start(f32[16,8,128]{2,1,0:T(8,128)} %get-tuple-element.46), calls=%async_computation.1 | async-start | bytes 131072 | tf_op jit(solution)/shard_map/all_to_all | solution.py:666
  70.7 0.1 collective-permute-start.6
  70.8 1.6 %collective-permute-start.7 = (bf16[11,32,128]{2,1,0:T(8,128)(2,1)}, bf16[11,32,128]{2,1,0:T(8,128)(2,1)S(1)}, u32[]{:S(2)}, u32[]{:S(2)}) collective-permute-start(bf16[11,32,128]{2,1,0:T(8,128)(2,1)} %get-tuple-element.48), channel_id=1, source_target_pairs={{0,16},{16,32},{32,48},{48,64},{64,80},{80,96},{96,112},{112,128},... | collective-permute-start | bytes 270344 | tf_op jit(solution)/shard_map/ppermute | solution.py:612
  72.5 3.6 %collective-permute-done.6.refs_10_.refs_15_ = bf16[11,32,128]{2,1,0:T(8,128)(2,1)S(1)} collective-permute-done((bf16[11,32,128]{2,1,0:T(8,128)(2,1)}, bf16[11,32,128]{2,1,0:T(8,128)(2,1)S(1)}, u32[]{:S(2)}, u32[]{:S(2)}) %collective-permute-start.6) | collective-permute-done | bytes 90144 | tf_op jit(solution)/shard_map/ppermute | solution.py:612
  76.0 0.0 collective-permute-done.7.refs_11_.refs_16_
  76.0 2.5 %all-to-all-done.1.refs_1_ = f32[16,8,128]{2,1,0:T(8,128)S(1)} async-done(((f32[16,8,128]{2,1,0:T(8,128)}), f32[16,8,128]{2,1,0:T(8,128)S(1)}, u32[]{:S(2)}, u32[]{:S(2)}) %all-to-all-start.1) | async-done | bytes 65568 | tf_op jit(solution)/shard_map/all_to_all | solution.py:666
  78.6 0.7 collective-permute-start.8
  79.3 3.9 %shard_map.181 = (f32[32,256]{1,0:T(8,128)}, bf16[27,32,128]{2,1,0:T(8,128)(2,1)}) custom-call(s32[2]{0:T(128)} %pad_add_fusion.refs_14_.refs_0_, f32[16,8,128]{2,1,0:T(8,128)} %copy-done.1, f32[8,256]{1,0:T(8,128)} %get-tuple-element.40.refs_4_.refs_1_.refs_2_, f32[1,256]{1,0:T(1,128)} %bitcast.9, f32[1,256]{1,0:T(1,128)} %bitcast.10, ...), custom_call_target="tpu_custom_call" | custom-call | flops 4000000000 | bytes 12000000 | tf_op jit(solution)/shard_map/pallas_call | solution.py:584
  83.1 0.0 collective-permute-done.8.refs_2_
  83.2 1.2 %copy-done.2 = bf16[256,3584]{1,0:T(8,128)(2,1)} copy-done((bf16[256,3584]{1,0:T(8,128)(2,1)}, bf16[256,3584]{1,0:T(8,128)(2,1)S(1)}, u32[]{:S(2)}) %copy-start.2) | copy-done | bytes 1835032
  84.4 10.5 %shard_map.182 = (bf16[32,32,512]{2,1,0:T(8,128)(2,1)}, bf16[32,32,512]{2,1,0:T(8,128)(2,1)}, bf16[32,32,128]{2,1,0:T(8,128)(2,1)}, bf16[32,32,128]{2,1,0:T(8,12...) custom-call(f32[32,256]{1,0:T(8,128)} %get-tuple-element.53.refs_0_,, ...), custom_call_target="tpu_custom_call" | custom-call | flops 12000000000 | bytes 36000000 | tf_op jit(solution)/shard_map/pallas_call | solution.py:584
  95.0 2.6 %collective-permute-start.9 = (bf16[8,32,128]{2,1,0:T(8,128)(2,1)}, bf16[8,32,128]{2,1,0:T(8,128)(2,1)S(1)}, u32[]{:S(2)}, u32[]{:S(2)}) collective-permute-start(bf16[8,32,128]{2,1,0:T(8,128)(2,1)} %get-tuple-element.58), channel_id=1, source_target_pairs={{0,15},{1,0},{2,1},{3,2},{4,3},{5,4},{6,5},{7,6},{8,7},{9,8},{10,9... | collective-permute-start | bytes 196616 | tf_op jit(solution)/shard_map/ppermute | solution.py:612
  97.5 0.0 collective-permute-start.10
  97.5 0.8 collective-permute-start.11
  98.3 0.9 collective-permute-start.12
  99.3 1.3 %reshape.19 = bf16[2,2,2,256]{3,2,1,0:T(2,128)(2,1)} reshape(bf16[8,256]{1,0:T(8,128)(2,1)} %get-tuple-element.63) | data formatting | bytes 8192 | tf_op jit(solution)/shard_map/reshape | solution.py:694
  100.6 0.0 collective-permute-done.9.refs_7_
  100.6 3.6 %collective-permute-done.10.refs_8_ = bf16[8,32,128]{2,1,0:T(8,128)(2,1)S(1)} collective-permute-done((bf16[8,32,128]{2,1,0:T(8,128)(2,1)}, bf16[8,32,128]{2,1,0:T(8,128)(2,1)S(1)}, u32[]{:S(2)}, u32[]{:S(2)}) %collective-permute-start.10) | collective-permute-done | bytes 65568 | tf_op jit(solution)/shard_map/ppermute | solution.py:612
  104.2 0.0 collective-permute-done.11.refs_9_
  104.2 0.6 copy-done.12
  104.8 0.0 copy-done.13
  104.8 0.0 copy-done.14
  104.8 6.5 %shard_map.183 = bf16[32,32,512]{2,1,0:T(8,128)(2,1)} custom-call(s32[3,32]{1,0:T(4,128)} %refs_0_.9, s32[1]{0:T(128)S(6)} %copy.19.refs_3_.refs_1_.refs_5_, s32[6,32]{1,0:T(8,128)} %refs_2_.5, bf16[3,32,224]{2,1,0:T(8,128)(2,1)} %refs_3_.7, bf16[32,32,512]{2,1,0:T(8,128)(2,1)} %get-tuple-element.55.refs_4_, bf16[32,32,128]{2,1,0:T(8,128)(2,1)} %get-tuple-element.56.refs_5_, ...), custom_call_target="tpu_custom_call" | custom-call | flops 7000000000 | bytes 21000000 | tf_op jit(solution)/shard_map/pallas_call | solution.py:584
  (22 shorter events, 0.0 us)
Async XLA Ops:
  4.8 11.9 %collective-permute-start = (bf16[8,32,128]{2,1,0:T(8,128)(2,1)}, bf16[8,32,128]{2,1,0:T(8,128)(2,1)S(1)}, u32[]{:S(2)}, u32[]{:S(2)}) collective-permute-start(bf16[8,32,128]{2,1,0:T(8,128)(2,1)} %get-tuple-element.35), channel_id=1, source_target_pairs={{0,15},{1,0},{2,1},{3,2},{4,3},{5,4},{6,5},{7,6},{8,7},{9,8},{10,9... | collective-permute-start | bytes 196616 | tf_op jit(solution)/shard_map/ppermute | solution.py:612
  10.6 6.6 %collective-permute-start.1 = (bf16[8,32,128]{2,1,0:T(8,128)(2,1)}, bf16[8,32,128]{2,1,0:T(8,128)(2,1)S(1)}, u32[]{:S(2)}, u32[]{:S(2)}) collective-permute-start(bf16[8,32,128]{2,1,0:T(8,128)(2,1)} %get-tuple-element.36), channel_id=1, source_target_pairs={{0,1},{1,2},{2,3},{3,4},{4,5},{5,6},{6,7},{7,8},{8,9},{9,10},{10,1... | collective-permute-start | bytes 196616 | tf_op jit(solution)/shard_map/ppermute | solution.py:612
  10.6 6.6 %collective-permute-start.2 = (bf16[8,32,128]{2,1,0:T(8,128)(2,1)}, bf16[8,32,128]{2,1,0:T(8,128)(2,1)S(1)}, u32[]{:S(2)}, u32[]{:S(2)}) collective-permute-start(bf16[8,32,128]{2,1,0:T(8,128)(2,1)} %get-tuple-element.37), channel_id=1, source_target_pairs={{0,240},{16,0},{32,16},{48,32},{64,48},{80,64},{96,80},{112,96},{1... | collective-permute-start | bytes 196616 | tf_op jit(solution)/shard_map/ppermute | solution.py:612
  11.6 6.0 %collective-permute-start.3 = (bf16[8,32,128]{2,1,0:T(8,128)(2,1)}, bf16[8,32,128]{2,1,0:T(8,128)(2,1)S(1)}, u32[]{:S(2)}, u32[]{:S(2)}) collective-permute-start(bf16[8,32,128]{2,1,0:T(8,128)(2,1)} %get-tuple-element.38), channel_id=1, source_target_pairs={{0,16},{16,32},{32,48},{48,64},{64,80},{80,96},{96,112},{112,128},... | collective-permute-start | bytes 196616 | tf_op jit(solution)/shard_map/ppermute | solution.py:612
  16.6 0.9 copy-start.7
  17.3 0.6 copy-start.8
  17.3 0.6 copy-start.9
  17.6 0.6 copy-start.10
  25.8 28.6 %all-to-all-start = ((bf16[16,16,3584]{2,1,0:T(8,128)(2,1)}), bf16[16,16,3584]{2,1,0:T(8,128)(2,1)S(1)}, u32[]{:S(2)}, u32[]{:S(2)}) async-start(bf16[16,16,3584]{2,1,0:T(8,128)(2,1)} %get-tuple-element.39), calls=%async_computation | async-start | bytes 3670016 | tf_op jit(solution)/shard_map/all_to_all | solution.py:655
  35.4 13.9 %collective-permute-start.4 = (bf16[9,32,128]{2,1,0:T(8,128)(2,1)}, bf16[9,32,128]{2,1,0:T(8,128)(2,1)S(1)}, u32[]{:S(2)}, u32[]{:S(2)}) collective-permute-start(bf16[9,32,128]{2,1,0:T(8,128)(2,1)} %get-tuple-element.42), channel_id=1, source_target_pairs={{0,15},{1,0},{2,1},{3,2},{4,3},{5,4},{6,5},{7,6},{8,7},{9,8},{10,9... | collective-permute-start | bytes 221192 | tf_op jit(solution)/shard_map/ppermute | solution.py:612
  40.2 14.3 %collective-permute-start.5 = (bf16[9,32,128]{2,1,0:T(8,128)(2,1)}, bf16[9,32,128]{2,1,0:T(8,128)(2,1)S(1)}, u32[]{:S(2)}, u32[]{:S(2)}) collective-permute-start(bf16[9,32,128]{2,1,0:T(8,128)(2,1)} %get-tuple-element.43), channel_id=1, source_target_pairs={{0,1},{1,2},{2,3},{3,4},{4,5},{5,6},{6,7},{7,8},{8,9},{9,10},{10,1... | collective-permute-start | bytes 221192 | tf_op jit(solution)/shard_map/ppermute | solution.py:612
  49.3 5.2 %copy-start.5 = (bf16[9,32,128]{2,1,0:T(8,128)(2,1)}, bf16[9,32,128]{2,1,0:T(8,128)(2,1)S(1)}, u32[]{:S(2)}) copy-start(bf16[9,32,128]{2,1,0:T(8,128)(2,1)S(1)} %collective-permute-done.4.refs_2_.refs_8_.refs_13_) | copy-start | bytes 221188
  54.5 0.6 copy-start.6
  54.5 1.3 %copy-start = (bf16[16,16,3584]{2,1,0:T(8,128)(2,1)}, bf16[16,16,3584]{2,1,0:T(8,128)(2,1)S(1)}, u32[]{:S(2)}) copy-start(bf16[16,16,3584]{2,1,0:T(8,128)(2,1)S(1)} %all-to-all-done.refs_0_) | copy-start | bytes 5505028
  57.6 21.0 %all-to-all-start.1 = ((f32[16,8,128]{2,1,0:T(8,128)}), f32[16,8,128]{2,1,0:T(8,128)S(1)}, u32[]{:S(2)}, u32[]{:S(2)}) async-start(f32[16,8,128]{2,1,0:T(8,128)} %get-tuple-element.46), calls=%async_computation.1 | async-start | bytes 131072 | tf_op jit(solution)/shard_map/all_to_all | solution.py:666
  70.7 5.3 %collective-permute-start.6 = (bf16[11,32,128]{2,1,0:T(8,128)(2,1)}, bf16[11,32,128]{2,1,0:T(8,128)(2,1)S(1)}, u32[]{:S(2)}, u32[]{:S(2)}) collective-permute-start(bf16[11,32,128]{2,1,0:T(8,128)(2,1)} %get-tuple-element.47), channel_id=1, source_target_pairs={{0,240},{16,0},{32,16},{48,32},{64,48},{80,64},{96,80},{112,96},{1... | collective-permute-start | bytes 270344 | tf_op jit(solution)/shard_map/ppermute | solution.py:612
  70.8 5.2 %collective-permute-start.7 = (bf16[11,32,128]{2,1,0:T(8,128)(2,1)}, bf16[11,32,128]{2,1,0:T(8,128)(2,1)S(1)}, u32[]{:S(2)}, u32[]{:S(2)}) collective-permute-start(bf16[11,32,128]{2,1,0:T(8,128)(2,1)} %get-tuple-element.48), channel_id=1, source_target_pairs={{0,16},{16,32},{32,48},{48,64},{64,80},{80,96},{96,112},{112,128},... | collective-permute-start | bytes 270344 | tf_op jit(solution)/shard_map/ppermute | solution.py:612
  76.0 3.2 %copy-start.3 = (bf16[11,32,128]{2,1,0:T(8,128)(2,1)}, bf16[11,32,128]{2,1,0:T(8,128)(2,1)S(1)}, u32[]{:S(2)}) copy-start(bf16[11,32,128]{2,1,0:T(8,128)(2,1)S(1)} %collective-permute-done.6.refs_10_.refs_15_) | copy-start | bytes 270340
  76.0 3.2 %copy-start.4 = (bf16[11,32,128]{2,1,0:T(8,128)(2,1)}, bf16[11,32,128]{2,1,0:T(8,128)(2,1)S(1)}, u32[]{:S(2)}) copy-start(bf16[11,32,128]{2,1,0:T(8,128)(2,1)S(1)} %collective-permute-done.7.refs_11_.refs_16_) | copy-start | bytes 270340
  78.5 0.7 copy-start.1
  78.6 4.6 %collective-permute-start.8 = (bf16[256,3584]{1,0:T(8,128)(2,1)}, bf16[256,3584]{1,0:T(8,128)(2,1)S(1)}, u32[]{:S(2)}, u32[]{:S(2)}) collective-permute-start(bf16[256,3584]{1,0:T(8,128)(2,1)} %bitcast.6), channel_id=1, source_target_pairs={{0,16},{16,0},{1,17},{17,1},{2,18},{18,2},{3,19},{19,3},{4,20},{20... | collective-permute-start | bytes 5505032 | tf_op jit(solution)/shard_map/ppermute | solution.py:672
  83.2 1.2 %copy-start.2 = (bf16[256,3584]{1,0:T(8,128)(2,1)}, bf16[256,3584]{1,0:T(8,128)(2,1)S(1)}, u32[]{:S(2)}) copy-start(bf16[256,3584]{1,0:T(8,128)(2,1)S(1)} %collective-permute-done.8.refs_2_) | copy-start | bytes 5505028
  95.0 5.6 %collective-permute-start.9 = (bf16[8,32,128]{2,1,0:T(8,128)(2,1)}, bf16[8,32,128]{2,1,0:T(8,128)(2,1)S(1)}, u32[]{:S(2)}, u32[]{:S(2)}) collective-permute-start(bf16[8,32,128]{2,1,0:T(8,128)(2,1)} %get-tuple-element.58), channel_id=1, source_target_pairs={{0,15},{1,0},{2,1},{3,2},{4,3},{5,4},{6,5},{7,6},{8,7},{9,8},{10,9... | collective-permute-start | bytes 196616 | tf_op jit(solution)/shard_map/ppermute | solution.py:612
  97.5 6.6 %collective-permute-start.10 = (bf16[8,32,128]{2,1,0:T(8,128)(2,1)}, bf16[8,32,128]{2,1,0:T(8,128)(2,1)S(1)}, u32[]{:S(2)}, u32[]{:S(2)}) collective-permute-start(bf16[8,32,128]{2,1,0:T(8,128)(2,1)} %get-tuple-element.59), channel_id=1, source_target_pairs={{0,1},{1,2},{2,3},{3,4},{4,5},{5,6},{6,7},{7,8},{8,9},{9,10},{10,1... | collective-permute-start | bytes 196616 | tf_op jit(solution)/shard_map/ppermute | solution.py:612
  97.5 6.6 %collective-permute-start.11 = (bf16[8,32,128]{2,1,0:T(8,128)(2,1)}, bf16[8,32,128]{2,1,0:T(8,128)(2,1)S(1)}, u32[]{:S(2)}, u32[]{:S(2)}) collective-permute-start(bf16[8,32,128]{2,1,0:T(8,128)(2,1)} %get-tuple-element.60), channel_id=1, source_target_pairs={{0,240},{16,0},{32,16},{48,32},{64,48},{80,64},{96,80},{112,96},{1... | collective-permute-start | bytes 196616 | tf_op jit(solution)/shard_map/ppermute | solution.py:612
  98.3 5.8 %collective-permute-start.12 = (bf16[8,32,128]{2,1,0:T(8,128)(2,1)}, bf16[8,32,128]{2,1,0:T(8,128)(2,1)S(1)}, u32[]{:S(2)}, u32[]{:S(2)}) collective-permute-start(bf16[8,32,128]{2,1,0:T(8,128)(2,1)} %get-tuple-element.61), channel_id=1, source_target_pairs={{0,16},{16,32},{32,48},{48,64},{64,80},{80,96},{96,112},{112,128},... | collective-permute-start | bytes 196616 | tf_op jit(solution)/shard_map/ppermute | solution.py:612
  100.6 3.6 %copy-start.11 = (bf16[8,32,128]{2,1,0:T(8,128)(2,1)}, bf16[8,32,128]{2,1,0:T(8,128)(2,1)S(1)}, u32[]{:S(2)}) copy-start(bf16[8,32,128]{2,1,0:T(8,128)(2,1)S(1)} %collective-permute-done.9.refs_7_) | copy-start | bytes 196612
  104.2 0.6 copy-start.12
  104.2 0.6 copy-start.13
  104.2 0.7 copy-start.14

commit v5 on v4

--- a/solution.py
+++ b/solution.py
@@ -372,8 +372,8 @@
     return total
 
 
-def coarse_front(ins, outs, active, raw, patches):
-    where, partial, own_tile, gain, bias, patch, plain, near_half, *planes = ins
+def coarse_sums(ins, active, raw, patches):
+    where, partial, own_tile, gain, bias, patch, plain, near_half, far_half, *planes = ins
     where, partial = where.get(), partial.get()
     major, minor = where[0], where[1]
     mean, spread_sum = merged_sums(partial[:, 0:2, :], partial[:, 2:4, :], 128.0)
@@ -415,19 +415,16 @@
         rest = rest - high.astype(f32)
         total += jnp.dot(plain[...], high, preferred_element_type=f32)
     base = (major & 1) * TAPS
-    half = near_half.get()
-    outs[0].ref[...] = times_half(total, lambda t: patches[base + t], half)
-    for t in range(TAPS):
-        outs[1].ref[t] = patches[TAPS - base + t]
+    total = times_half(total, lambda t: patches[base + t], near_half.get())
+    return times_half(total, lambda t: patches[TAPS - base + t], far_half.get())
 
 
 def second_conv(ins, outs, joined, signal, y_bank, z_bank, *rest):
-    (total, far_patches, far_half, up, coords, counts, links, weights, spread, level, faces,
-     y_spread, z_spread, *planes) = ins
+    first, planes = ins[:9], ins[9:13]
+    (up, coords, counts, links, weights, spread, level, faces, y_spread, z_spread) = ins[13:]
     second, signal2, y_own, z_own, *sent, coarse = outs
-    taps, work, (lifted, rows) = rest[:4], rest[4:8], rest[8:]
-    far_patches = far_patches.get()
-    total = times_half(total.get()[...], lambda t: far_patches[t], far_half.get())
+    taps, work, (lifted, rows, *coarse_work) = rest[:4], rest[4:8], rest[8:]
+    total = coarse_sums((*first, *planes), *coarse_work)
     r0, r1, r2, r3 = (p.get() for p in planes)
     result = total.astype(bf16)
     coarse.ref[...] = result[0:8]
@@ -663,28 +660,20 @@
         ((message, slice(HALF_ROWS, HALF_ROWS + 128)), *plainly(own_tile, y_above, y_below, low_z, high_z)),
         (SUMS,) + (((11, CHANS, 128), bf16),) * 2, (), 1,
     )
+    near_half = message.reshape(COARSE, HALF_ROWS + 128)
+    near_half, partial = lax.optimization_barrier((near_half, partial))
     partial = lax.all_to_all(partial, MX, 0, 0)
+    far_half = lax.ppermute(near_half, "mx_1", [(0, 1), (1, 0)])
     z_above, z_below = shifted(low_z, MX, -1), shifted(high_z, MX, 1)
-    near_half = message.reshape(COARSE, HALF_ROWS + 128)
-    near_half, partial, z_above, z_below = lax.optimization_barrier(
-        (near_half, partial, z_above, z_below)
-    )
-    far_half = lax.ppermute(near_half, "mx_1", [(0, 1), (1, 0)])
-    planes = (y_above, y_below, z_above, z_below)
-    front = call(
-        coarse_front,
+    second, *own, low_y, high_y, low_z, high_z, coarse = call(
+        second_conv,
         ((where, "smem"),
          *plainly(partial, own_tile, norm_gain.reshape(1, COARSE), norm_bias.reshape(1, COARSE),
-                  patch, plain, near_half, *planes)),
-        (((32, COARSE), f32), ((TAPS, 32, 128), bf16)),
-        (((128, COARSE), f32), ((128, COARSE), f32), ((2 * TAPS, 32, 128), bf16)), 4,
-    )
-    second, *own, low_y, high_y, low_z, high_z, coarse = call(
-        second_conv,
-        (*plainly(*front, far_half, up_weight), *live,
-         *plainly(fine_weights, spread, level, faces, y_spread, z_spread, *planes)),
+                  patch, plain, near_half, far_half, y_above, y_below, z_above, z_below, up_weight),
+         *live, *plainly(fine_weights, spread, level, faces, y_spread, z_spread)),
         (FIELD, FIELD, FACES, FACES) + (PLANE,) * 4 + (((8, COARSE), bf16),),
-        (FIELD, SIGNAL, BANK, BANK, *TAP_STACK, *WORK, ((8, 32, COARSE), f32), ((256, 256), bf16)), 12,
+        (FIELD, SIGNAL, BANK, BANK, *TAP_STACK, *WORK, ((8, 32, COARSE), f32), ((256, 256), bf16),
+         ((128, COARSE), f32), ((128, COARSE), f32), ((2 * TAPS, 32, 128), bf16)), 14,
     )
     planes = swap_planes((low_y, high_y, low_z, high_z))
     (fine_out,) = call(

time: 112 us -> 110 us (0.982)
  Pallas kernels: 40.1 us -> 38.6 us
    all_to_all x1, starting transfers between devices: 13.2 us -> 7.43 us  [local(): partial = lax.all_to_all(partial, MX, 0, 0)]
    ppermute x1, starting transfers between devices: 0.72 us -> 5.97 us  [local(): far_half = lax.ppermute(near_half, 'mx_1', [(0, 1), (1, 0)])]
    pallas_call x8 -> x7, Pallas kernels: 40.1 us -> 38.6 us  [call(): pl.pallas_call(body, in_specs=[hbm] * total, out_specs=[hbm] * len(outs),...]
  transfers between devices with their start and end apart: 15 -> 15, of which waited for: 7 -> 7; matrix products, arithmetic and copies ran while one was open for 2% -> 2% of each run, Pallas kernels for 9% -> 6%
where the time goes in v5:
time: 110 us; the launch traced here: 109 us
  starting transfers between devices  38.7 us (35%)
  Pallas kernels  38.6 us (35%)
  waiting for transfers between devices  24.9 us (23%)
  local copies, waits for them, and re-layouts  5.06 us (5%)
  between operations  1.4 us (1%)
    pallas_call x7, Pallas kernels, call(): pl.pallas_call(body, in_specs=[hbm] * total, out_specs=[hbm] * len(outs),...  38.6 us
    ppermute x12, waiting for transfers between devices, shifted(): lax.ppermute(x, axes, [(i, (i + step) % count) for i in range(count)])  22.4 us
    ppermute x12, starting transfers between devices, shifted(): lax.ppermute(x, axes, [(i, (i + step) % count) for i in range(count)])  19.1 us
    all_to_all x1, starting transfers between devices, local(): partial = lax.all_to_all(partial, MX, 0, 0)  7.43 us
    all_to_all x1, starting transfers between devices, local(): message = lax.all_to_all(message, MY, 0, 0)  6.18 us
    ppermute x1, starting transfers between devices, local(): far_half = lax.ppermute(near_half, 'mx_1', [(0, 1), (1, 0)])  5.97 us
    unnamed x30, local copies, waits for them, and re-layouts  3.78 us
    all_to_all x1, waiting for transfers between devices, local(): partial = lax.all_to_all(partial, MX, 0, 0)  2.52 us
  transfers between devices with their start and end apart: 15, of which 7 were waited for; matrix products, arithmetic and copies ran while one was open for 2% of the time, Pallas kernels for 6%

profile of v5, /device:TPU:1, one launch (start us, length us, event | category | flops | bytes accessed | tf_op | source)
XLA Modules:
  0.0 109.3 jit_solution(1971645603498382821)
XLA Ops:
  1.3 3.5 %shard_map.177 = (bf16[32,32,128]{2,1,0:T(8,128)(2,1)}, bf16[32,32,128]{2,1,0:T(8,128)(2,1)}, bf16[8,32,128]{2,1,0:T(8,128)(2,1)}, bf16[8,32,128]{2,1,0:T(8,128)...) custom-call(bf16[32,32,512]{2,1,0:T(8,128)(2,1)} %refs_11_.1, ...), custom_call_target="tpu_custom_call" | custom-call | flops 3000000000 | bytes 9000000 | tf_op jit(solution)/shard_map/pallas_call | solution.py:581
  4.8 5.8 %collective-permute-start = (bf16[8,32,128]{2,1,0:T(8,128)(2,1)}, bf16[8,32,128]{2,1,0:T(8,128)(2,1)S(1)}, u32[]{:S(2)}, u32[]{:S(2)}) collective-permute-start(bf16[8,32,128]{2,1,0:T(8,128)(2,1)} %get-tuple-element.31), channel_id=1, source_target_pairs={{0,15},{1,0},{2,1},{3,2},{4,3},{5,4},{6,5},{7,6},{8,7},{9,8},{10,9... | collective-permute-start | bytes 196616 | tf_op jit(solution)/shard_map/ppermute | solution.py:609
  10.6 0.0 collective-permute-start.1
  10.6 1.0 collective-permute-start.2
  11.6 1.5 %collective-permute-start.3 = (bf16[8,32,128]{2,1,0:T(8,128)(2,1)}, bf16[8,32,128]{2,1,0:T(8,128)(2,1)S(1)}, u32[]{:S(2)}, u32[]{:S(2)}) collective-permute-start(bf16[8,32,128]{2,1,0:T(8,128)(2,1)} %get-tuple-element.34), channel_id=1, source_target_pairs={{0,16},{16,32},{32,48},{48,64},{64,80},{80,96},{96,112},{112,128},... | collective-permute-start | bytes 196616 | tf_op jit(solution)/shard_map/ppermute | solution.py:609
  13.1 2.9 %shard_map.176.refs_4_ = bf16[32,32,512]{2,1,0:T(8,128)(2,1)} custom-call(bf16[32,32,512]{2,1,0:T(8,128)(2,1)} %refs_11_.1), custom_call_target="tpu_custom_call" | custom-call | flops 3000000000 | bytes 9000000 | tf_op jit(solution)/shard_map/pallas_call | solution.py:581
  16.0 0.6 pad_add_fusion.refs_14_.refs_0_
  16.6 0.0 collective-permute-done.refs_7_
  16.7 0.6 collective-permute-done.1.refs_8_
  17.3 0.0 collective-permute-done.2.refs_9_
  17.3 0.3 collective-permute-done.3.refs_10_
  17.6 0.3 copy-done.8
  17.9 0.0 copy-done.9
  18.0 0.2 copy-done.10
  18.2 7.7 %shard_map.178 = (bf16[32,32,512]{2,1,0:T(8,128)(2,1)}, f32[8,256]{1,0:T(8,128)}, bf16[16,16,3584]{2,1,0:T(8,128)(2,1)}) custom-call(s32[3,32]{1,0:T(4,128)} %refs_0_.9, s32[1]{0:T(128)S(6)} %copy.19.refs_3_.refs_1_.refs_15_, s32[6,32]{1,0:T(8,128)} %refs_2_.5, bf16[3,32,224]{2,1,0:T(8,128)(2,1)} %refs_3_.5, bf16[32,32,512]{2,1,0:T(8,128)(2,1)} %shard_map.176.refs_4_, ...), custom_call_target="tpu_custom_call" | custom-call | flops 8000000000 | bytes 24000000 | tf_op jit(solution)/shard_map/pallas_call | solution.py:581
  25.9 6.2 %all-to-all-start = ((bf16[16,16,3584]{2,1,0:T(8,128)(2,1)}), bf16[16,16,3584]{2,1,0:T(8,128)(2,1)S(1)}, u32[]{:S(2)}, u32[]{:S(2)}) async-start(bf16[16,16,3584]{2,1,0:T(8,128)(2,1)} %get-tuple-element.35), calls=%async_computation | async-start | bytes 3670016 | tf_op jit(solution)/shard_map/all_to_all | solution.py:652
  32.0 3.4 %shard_map.179 = (bf16[9,32,128]{2,1,0:T(8,128)(2,1)}, bf16[9,32,128]{2,1,0:T(8,128)(2,1)}, bf16[8,32,128]{2,1,0:T(8,128)(2,1)}, bf16[8,32,128]{2,1,0:T(8,128)(2,1)}) custom-call(s32[3,32]{1,0:T(4,128)} %refs_0_.9, s32[1]{0:T(128)S(6)} %copy.19.refs_3_.refs_1_.refs_15_, bf16[32,32,512]{2,1,0:T(8,128)(2,1)} %get-tuple-element.37.refs_2_.refs_19_, ...), custom_call_target="tpu_custom_call" | custom-call | flops 3000000000 | bytes 9000000 | tf_op jit(solution)/shard_map/pallas_call | solution.py:581
  35.4 4.8 %collective-permute-start.4 = (bf16[9,32,128]{2,1,0:T(8,128)(2,1)}, bf16[9,32,128]{2,1,0:T(8,128)(2,1)S(1)}, u32[]{:S(2)}, u32[]{:S(2)}) collective-permute-start(bf16[9,32,128]{2,1,0:T(8,128)(2,1)} %get-tuple-element.38), channel_id=1, source_target_pairs={{0,15},{1,0},{2,1},{3,2},{4,3},{5,4},{6,5},{7,6},{8,7},{9,8},{10,9... | collective-permute-start | bytes 221192 | tf_op jit(solution)/shard_map/ppermute | solution.py:609
  40.2 0.0 collective-permute-start.5
  40.2 9.1 %collective-permute-done.4.refs_2_.refs_9_ = bf16[9,32,128]{2,1,0:T(8,128)(2,1)S(1)} collective-permute-done((bf16[9,32,128]{2,1,0:T(8,128)(2,1)}, bf16[9,32,128]{2,1,0:T(8,128)(2,1)S(1)}, u32[]{:S(2)}, u32[]{:S(2)}) %collective-permute-start.4) | collective-permute-done | bytes 73760 | tf_op jit(solution)/shard_map/ppermute | solution.py:609
  49.3 5.2 %collective-permute-done.5.refs_3_.refs_10_ = bf16[9,32,128]{2,1,0:T(8,128)(2,1)S(1)} collective-permute-done((bf16[9,32,128]{2,1,0:T(8,128)(2,1)}, bf16[9,32,128]{2,1,0:T(8,128)(2,1)S(1)}, u32[]{:S(2)}, u32[]{:S(2)}) %collective-permute-start.5) | collective-permute-done | bytes 73760 | tf_op jit(solution)/shard_map/ppermute | solution.py:609
  54.5 0.0 all-to-all-done.refs_0_
  54.5 0.6 copy-done.6
  55.1 0.6 copy-done
  55.7 1.8 %shard_map.180 = (f32[16,8,128]{2,1,0:T(8,128)}, bf16[11,32,128]{2,1,0:T(8,128)(2,1)}, bf16[11,32,128]{2,1,0:T(8,128)(2,1)}) custom-call(bf16[16,16,3584]{2,1,0:T(8,128)(2,1)} %copy-done, f32[8,256]{1,0:T(8,128)} %get-tuple-element.36.refs_4_.refs_1_.refs_2_, bf16[9,32,128]{2,1,0:T(8,128)(2,1)} %copy-done.5, bf16[9,32,128]{2,1,0:T(8,128)(2,1)} %copy-done.6, ...), custom_call_target="tpu_custom_call" | custom-call | flops 1000000000 | bytes 3000000 | tf_op jit(solution)/shard_map/pallas_call | solution.py:581
  57.6 6.0 %collective-permute-start.6 = (bf16[256,3584]{1,0:T(8,128)(2,1)}, bf16[256,3584]{1,0:T(8,128)(2,1)S(1)}, u32[]{:S(2)}, u32[]{:S(2)}) collective-permute-start(bf16[256,3584]{1,0:T(8,128)(2,1)} %bitcast.6), channel_id=1, source_target_pairs={{0,16},{16,0},{1,17},{17,1},{2,18},{18,2},{3,19},{19,3},{4,20},{20... | collective-permute-start | bytes 5505032 | tf_op jit(solution)/shard_map/ppermute | solution.py:666
  63.5 7.4 %all-to-all-start.1 = ((f32[16,8,128]{2,1,0:T(8,128)}), f32[16,8,128]{2,1,0:T(8,128)S(1)}, u32[]{:S(2)}, u32[]{:S(2)}) async-start(f32[16,8,128]{2,1,0:T(8,128)} %get-tuple-element.43), calls=%async_computation.1 | async-start | bytes 131072 | tf_op jit(solution)/shard_map/all_to_all | solution.py:665
  71.0 0.1 collective-permute-start.7
  71.1 1.6 %collective-permute-start.8 = (bf16[11,32,128]{2,1,0:T(8,128)(2,1)}, bf16[11,32,128]{2,1,0:T(8,128)(2,1)S(1)}, u32[]{:S(2)}, u32[]{:S(2)}) collective-permute-start(bf16[11,32,128]{2,1,0:T(8,128)(2,1)} %get-tuple-element.46), channel_id=1, source_target_pairs={{0,16},{16,32},{32,48},{48,64},{64,80},{80,96},{96,112},{112,128},... | collective-permute-start | bytes 270344 | tf_op jit(solution)/shard_map/ppermute | solution.py:609
  72.7 3.6 %collective-permute-done.7.refs_11_ = bf16[11,32,128]{2,1,0:T(8,128)(2,1)S(1)} collective-permute-done((bf16[11,32,128]{2,1,0:T(8,128)(2,1)}, bf16[11,32,128]{2,1,0:T(8,128)(2,1)S(1)}, u32[]{:S(2)}, u32[]{:S(2)}) %collective-permute-start.7) | collective-permute-done | bytes 90144 | tf_op jit(solution)/shard_map/ppermute | solution.py:609
  76.3 0.0 collective-permute-done.8.refs_12_
  76.3 2.5 %all-to-all-done.1.refs_1_ = f32[16,8,128]{2,1,0:T(8,128)S(1)} async-done(((f32[16,8,128]{2,1,0:T(8,128)}), f32[16,8,128]{2,1,0:T(8,128)S(1)}, u32[]{:S(2)}, u32[]{:S(2)}) %all-to-all-start.1) | async-done | bytes 65568 | tf_op jit(solution)/shard_map/all_to_all | solution.py:665
  78.8 0.0 collective-permute-done.6.refs_8_
  78.8 0.6 copy-done.1
  79.4 0.6 copy-done.2
  80.1 12.9 %shard_map.181 = (bf16[32,32,512]{2,1,0:T(8,128)(2,1)}, bf16[32,32,512]{2,1,0:T(8,128)(2,1)}, bf16[32,32,128]{2,1,0:T(8,128)(2,1)}, bf16[32,32,128]{2,1,0:T(8,12...) custom-call(s32[2]{0:T(128)} %pad_add_fusion.refs_14_.refs_0_, ...), custom_call_target="tpu_custom_call" | custom-call | flops 14000000000 | bytes 42000000 | tf_op jit(solution)/shard_map/pallas_call | solution.py:581
  92.9 2.5 %collective-permute-start.9 = (bf16[8,32,128]{2,1,0:T(8,128)(2,1)}, bf16[8,32,128]{2,1,0:T(8,128)(2,1)S(1)}, u32[]{:S(2)}, u32[]{:S(2)}) collective-permute-start(bf16[8,32,128]{2,1,0:T(8,128)(2,1)} %get-tuple-element.50), channel_id=1, source_target_pairs={{0,15},{1,0},{2,1},{3,2},{4,3},{5,4},{6,5},{7,6},{8,7},{9,8},{10,9... | collective-permute-start | bytes 196616 | tf_op jit(solution)/shard_map/ppermute | solution.py:609
  95.5 0.0 collective-permute-start.10
  95.5 0.9 collective-permute-start.11
  96.4 0.8 collective-permute-start.12
  97.2 1.3 %reshape.19 = bf16[2,2,2,256]{3,2,1,0:T(2,128)(2,1)} reshape(bf16[8,256]{1,0:T(8,128)(2,1)} %get-tuple-element.55) | data formatting | bytes 8192 | tf_op jit(solution)/shard_map/reshape | solution.py:683
  98.5 0.0 collective-permute-done.9.refs_7_
  98.5 3.6 %collective-permute-done.10.refs_8_ = bf16[8,32,128]{2,1,0:T(8,128)(2,1)S(1)} collective-permute-done((bf16[8,32,128]{2,1,0:T(8,128)(2,1)}, bf16[8,32,128]{2,1,0:T(8,128)(2,1)S(1)}, u32[]{:S(2)}, u32[]{:S(2)}) %collective-permute-start.10) | collective-permute-done | bytes 65568 | tf_op jit(solution)/shard_map/ppermute | solution.py:609
  102.1 0.0 collective-permute-done.12.refs_10_
  102.2 0.6 copy-done.12
  102.8 0.0 copy-done.13
  102.8 0.0 copy-done.14
  102.8 6.5 %shard_map.182 = bf16[32,32,512]{2,1,0:T(8,128)(2,1)} custom-call(s32[3,32]{1,0:T(4,128)} %refs_0_.9, s32[1]{0:T(128)S(6)} %copy.19.refs_3_.refs_1_.refs_15_, s32[6,32]{1,0:T(8,128)} %refs_2_.5, bf16[3,32,224]{2,1,0:T(8,128)(2,1)} %refs_3_.5, bf16[32,32,512]{2,1,0:T(8,128)(2,1)} %get-tuple-element.47.refs_4_, ...), custom_call_target="tpu_custom_call" | custom-call | flops 7000000000 | bytes 21000000 | tf_op jit(solution)/shard_map/pallas_call | solution.py:581
  (21 shorter events, 0.0 us)
Async XLA Ops:
  4.8 11.8 %collective-permute-start = (bf16[8,32,128]{2,1,0:T(8,128)(2,1)}, bf16[8,32,128]{2,1,0:T(8,128)(2,1)S(1)}, u32[]{:S(2)}, u32[]{:S(2)}) collective-permute-start(bf16[8,32,128]{2,1,0:T(8,128)(2,1)} %get-tuple-element.31), channel_id=1, source_target_pairs={{0,15},{1,0},{2,1},{3,2},{4,3},{5,4},{6,5},{7,6},{8,7},{9,8},{10,9... | collective-permute-start | bytes 196616 | tf_op jit(solution)/shard_map/ppermute | solution.py:609
  10.6 6.6 %collective-permute-start.1 = (bf16[8,32,128]{2,1,0:T(8,128)(2,1)}, bf16[8,32,128]{2,1,0:T(8,128)(2,1)S(1)}, u32[]{:S(2)}, u32[]{:S(2)}) collective-permute-start(bf16[8,32,128]{2,1,0:T(8,128)(2,1)} %get-tuple-element.32), channel_id=1, source_target_pairs={{0,1},{1,2},{2,3},{3,4},{4,5},{5,6},{6,7},{7,8},{8,9},{9,10},{10,1... | collective-permute-start | bytes 196616 | tf_op jit(solution)/shard_map/ppermute | solution.py:609
  10.6 6.6 %collective-permute-start.2 = (bf16[8,32,128]{2,1,0:T(8,128)(2,1)}, bf16[8,32,128]{2,1,0:T(8,128)(2,1)S(1)}, u32[]{:S(2)}, u32[]{:S(2)}) collective-permute-start(bf16[8,32,128]{2,1,0:T(8,128)(2,1)} %get-tuple-element.33), channel_id=1, source_target_pairs={{0,240},{16,0},{32,16},{48,32},{64,48},{80,64},{96,80},{112,96},{1... | collective-permute-start | bytes 196616 | tf_op jit(solution)/shard_map/ppermute | solution.py:609
  11.6 6.0 %collective-permute-start.3 = (bf16[8,32,128]{2,1,0:T(8,128)(2,1)}, bf16[8,32,128]{2,1,0:T(8,128)(2,1)S(1)}, u32[]{:S(2)}, u32[]{:S(2)}) collective-permute-start(bf16[8,32,128]{2,1,0:T(8,128)(2,1)} %get-tuple-element.34), channel_id=1, source_target_pairs={{0,16},{16,32},{32,48},{48,64},{64,80},{80,96},{96,112},{112,128},... | collective-permute-start | bytes 196616 | tf_op jit(solution)/shard_map/ppermute | solution.py:609
  16.6 0.9 copy-start.7
  17.3 0.6 copy-start.8
  17.3 0.7 copy-start.9
  17.6 0.6 copy-start.10
  25.9 28.6 %all-to-all-start = ((bf16[16,16,3584]{2,1,0:T(8,128)(2,1)}), bf16[16,16,3584]{2,1,0:T(8,128)(2,1)S(1)}, u32[]{:S(2)}, u32[]{:S(2)}) async-start(bf16[16,16,3584]{2,1,0:T(8,128)(2,1)} %get-tuple-element.35), calls=%async_computation | async-start | bytes 3670016 | tf_op jit(solution)/shard_map/all_to_all | solution.py:652
  35.4 13.9 %collective-permute-start.4 = (bf16[9,32,128]{2,1,0:T(8,128)(2,1)}, bf16[9,32,128]{2,1,0:T(8,128)(2,1)S(1)}, u32[]{:S(2)}, u32[]{:S(2)}) collective-permute-start(bf16[9,32,128]{2,1,0:T(8,128)(2,1)} %get-tuple-element.38), channel_id=1, source_target_pairs={{0,15},{1,0},{2,1},{3,2},{4,3},{5,4},{6,5},{7,6},{8,7},{9,8},{10,9... | collective-permute-start | bytes 221192 | tf_op jit(solution)/shard_map/ppermute | solution.py:609
  40.2 14.3 %collective-permute-start.5 = (bf16[9,32,128]{2,1,0:T(8,128)(2,1)}, bf16[9,32,128]{2,1,0:T(8,128)(2,1)S(1)}, u32[]{:S(2)}, u32[]{:S(2)}) collective-permute-start(bf16[9,32,128]{2,1,0:T(8,128)(2,1)} %get-tuple-element.39), channel_id=1, source_target_pairs={{0,1},{1,2},{2,3},{3,4},{4,5},{5,6},{6,7},{7,8},{8,9},{9,10},{10,1... | collective-permute-start | bytes 221192 | tf_op jit(solution)/shard_map/ppermute | solution.py:609
  49.3 5.2 %copy-start.5 = (bf16[9,32,128]{2,1,0:T(8,128)(2,1)}, bf16[9,32,128]{2,1,0:T(8,128)(2,1)S(1)}, u32[]{:S(2)}) copy-start(bf16[9,32,128]{2,1,0:T(8,128)(2,1)S(1)} %collective-permute-done.4.refs_2_.refs_9_) | copy-start | bytes 221188
  54.5 0.6 copy-start.6
  54.5 1.3 %copy-start = (bf16[16,16,3584]{2,1,0:T(8,128)(2,1)}, bf16[16,16,3584]{2,1,0:T(8,128)(2,1)S(1)}, u32[]{:S(2)}) copy-start(bf16[16,16,3584]{2,1,0:T(8,128)(2,1)S(1)} %all-to-all-done.refs_0_) | copy-start | bytes 5505028
  57.6 21.2 %collective-permute-start.6 = (bf16[256,3584]{1,0:T(8,128)(2,1)}, bf16[256,3584]{1,0:T(8,128)(2,1)S(1)}, u32[]{:S(2)}, u32[]{:S(2)}) collective-permute-start(bf16[256,3584]{1,0:T(8,128)(2,1)} %bitcast.6), channel_id=1, source_target_pairs={{0,16},{16,0},{1,17},{17,1},{2,18},{18,2},{3,19},{19,3},{4,20},{20... | collective-permute-start | bytes 5505032 | tf_op jit(solution)/shard_map/ppermute | solution.py:666
  63.5 15.3 %all-to-all-start.1 = ((f32[16,8,128]{2,1,0:T(8,128)}), f32[16,8,128]{2,1,0:T(8,128)S(1)}, u32[]{:S(2)}, u32[]{:S(2)}) async-start(f32[16,8,128]{2,1,0:T(8,128)} %get-tuple-element.43), calls=%async_computation.1 | async-start | bytes 131072 | tf_op jit(solution)/shard_map/all_to_all | solution.py:665
  71.0 5.3 %collective-permute-start.7 = (bf16[11,32,128]{2,1,0:T(8,128)(2,1)}, bf16[11,32,128]{2,1,0:T(8,128)(2,1)S(1)}, u32[]{:S(2)}, u32[]{:S(2)}) collective-permute-start(bf16[11,32,128]{2,1,0:T(8,128)(2,1)} %get-tuple-element.45), channel_id=1, source_target_pairs={{0,240},{16,0},{32,16},{48,32},{64,48},{80,64},{96,80},{112,96},{1... | collective-permute-start | bytes 270344 | tf_op jit(solution)/shard_map/ppermute | solution.py:609
  71.1 5.2 %collective-permute-start.8 = (bf16[11,32,128]{2,1,0:T(8,128)(2,1)}, bf16[11,32,128]{2,1,0:T(8,128)(2,1)S(1)}, u32[]{:S(2)}, u32[]{:S(2)}) collective-permute-start(bf16[11,32,128]{2,1,0:T(8,128)(2,1)} %get-tuple-element.46), channel_id=1, source_target_pairs={{0,16},{16,32},{32,48},{48,64},{64,80},{80,96},{96,112},{112,128},... | collective-permute-start | bytes 270344 | tf_op jit(solution)/shard_map/ppermute | solution.py:609
  76.3 2.5 %copy-start.3 = (bf16[11,32,128]{2,1,0:T(8,128)(2,1)}, bf16[11,32,128]{2,1,0:T(8,128)(2,1)S(1)}, u32[]{:S(2)}) copy-start(bf16[11,32,128]{2,1,0:T(8,128)(2,1)S(1)} %collective-permute-done.7.refs_11_) | copy-start | bytes 270340
  76.3 2.5 %copy-start.4 = (bf16[11,32,128]{2,1,0:T(8,128)(2,1)}, bf16[11,32,128]{2,1,0:T(8,128)(2,1)S(1)}, u32[]{:S(2)}) copy-start(bf16[11,32,128]{2,1,0:T(8,128)(2,1)S(1)} %collective-permute-done.8.refs_12_) | copy-start | bytes 270340
  78.8 0.6 copy-start.1
  78.8 1.2 %copy-start.2 = (bf16[256,3584]{1,0:T(8,128)(2,1)}, bf16[256,3584]{1,0:T(8,128)(2,1)S(1)}, u32[]{:S(2)}) copy-start(bf16[256,3584]{1,0:T(8,128)(2,1)S(1)} %collective-permute-done.6.refs_8_) | copy-start | bytes 5505028
  92.9 5.6 %collective-permute-start.9 = (bf16[8,32,128]{2,1,0:T(8,128)(2,1)}, bf16[8,32,128]{2,1,0:T(8,128)(2,1)S(1)}, u32[]{:S(2)}, u32[]{:S(2)}) collective-permute-start(bf16[8,32,128]{2,1,0:T(8,128)(2,1)} %get-tuple-element.50), channel_id=1, source_target_pairs={{0,15},{1,0},{2,1},{3,2},{4,3},{5,4},{6,5},{7,6},{8,7},{9,8},{10,9... | collective-permute-start | bytes 196616 | tf_op jit(solution)/shard_map/ppermute | solution.py:609
  95.5 6.6 %collective-permute-start.10 = (bf16[8,32,128]{2,1,0:T(8,128)(2,1)}, bf16[8,32,128]{2,1,0:T(8,128)(2,1)S(1)}, u32[]{:S(2)}, u32[]{:S(2)}) collective-permute-start(bf16[8,32,128]{2,1,0:T(8,128)(2,1)} %get-tuple-element.51), channel_id=1, source_target_pairs={{0,1},{1,2},{2,3},{3,4},{4,5},{5,6},{6,7},{7,8},{8,9},{9,10},{10,1... | collective-permute-start | bytes 196616 | tf_op jit(solution)/shard_map/ppermute | solution.py:609
  95.5 6.6 %collective-permute-start.11 = (bf16[8,32,128]{2,1,0:T(8,128)(2,1)}, bf16[8,32,128]{2,1,0:T(8,128)(2,1)S(1)}, u32[]{:S(2)}, u32[]{:S(2)}) collective-permute-start(bf16[8,32,128]{2,1,0:T(8,128)(2,1)} %get-tuple-element.52), channel_id=1, source_target_pairs={{0,240},{16,0},{32,16},{48,32},{64,48},{80,64},{96,80},{112,96},{1... | collective-permute-start | bytes 196616 | tf_op jit(solution)/shard_map/ppermute | solution.py:609
  96.4 5.7 %collective-permute-start.12 = (bf16[8,32,128]{2,1,0:T(8,128)(2,1)}, bf16[8,32,128]{2,1,0:T(8,128)(2,1)S(1)}, u32[]{:S(2)}, u32[]{:S(2)}) collective-permute-start(bf16[8,32,128]{2,1,0:T(8,128)(2,1)} %get-tuple-element.53), channel_id=1, source_target_pairs={{0,16},{16,32},{32,48},{48,64},{64,80},{80,96},{96,112},{112,128},... | collective-permute-start | bytes 196616 | tf_op jit(solution)/shard_map/ppermute | solution.py:609
  98.5 3.6 %copy-start.11 = (bf16[8,32,128]{2,1,0:T(8,128)(2,1)}, bf16[8,32,128]{2,1,0:T(8,128)(2,1)S(1)}, u32[]{:S(2)}) copy-start(bf16[8,32,128]{2,1,0:T(8,128)(2,1)S(1)} %collective-permute-done.9.refs_7_) | copy-start | bytes 196612
  102.1 0.6 copy-start.12
  102.1 0.7 copy-start.13
  102.1 0.7 copy-start.14

commit v6 on v5

--- a/solution.py
+++ b/solution.py
@@ -339,20 +339,17 @@
 
 
 def row_sums(ins, outs):
-    message, own_tile, y_above, y_below, z_low, z_high = (one.get() for one in ins)
-    partial, z_low_out, z_high_out = (one.ref for one in outs)
+    message, own_tile, y_above, y_below = (one.get() for one in ins)
+    partial, strip = (one.ref for one in outs)
     sums = message[...].astype(f32)
     sums = sums[:, 0:4] + sums[:, 4:8] + sums[:, 8:12]
     mean, spread = merged_sums(sums[:, 0:2], sums[:, 2:4], 8.0)
     both = stat_rows(mean[0], spread[0])
     for i in range(16):
         partial[i] = both
-    packed = packed_tile(own_tile[...])
-    for out, plane in ((z_low_out, z_low), (z_high_out, z_high)):
-        out[0:8] = plane[...]
-        out[8] = y_below[8]
-        out[9] = packed
-        out[10] = y_above[8]
+    strip[0] = y_below[8]
+    strip[1] = packed_tile(own_tile[...])
+    strip[2] = y_above[8]
 
 
 def group_total(x):
@@ -385,11 +382,11 @@
     group_mean = jnp.concatenate([group_mean[0:1], group_mean[1:2]], axis=1)
     variance = jnp.concatenate([variance[0:1], variance[1:2]], axis=1)
     scale = gain[...] / jnp.sqrt(variance + NORM_EPS)
-    r0, r1, r2, r3 = (p.get() for p in planes)
+    y_above, y_below, strip_above, strip_below = (p.get() for p in planes)
     tiles = [
-        [unpacked_tile(r3[8]), unpacked_tile(r3[9]), unpacked_tile(r3[10])],
-        [unpacked_tile(r1[8]), own_tile.get()[...], unpacked_tile(r0[8])],
-        [unpacked_tile(r2[8]), unpacked_tile(r2[9]), unpacked_tile(r2[10])],
+        [unpacked_tile(strip_below[step]) for step in range(3)],
+        [unpacked_tile(y_below[8]), own_tile.get()[...], unpacked_tile(y_above[8])],
+        [unpacked_tile(strip_above[step]) for step in range(3)],
     ]
     active[...] = jnp.zeros_like(active)
     raw[...] = jnp.zeros_like(raw)
@@ -420,11 +417,11 @@
 
 
 def second_conv(ins, outs, joined, signal, y_bank, z_bank, *rest):
-    first, planes = ins[:9], ins[9:13]
-    (up, coords, counts, links, weights, spread, level, faces, y_spread, z_spread) = ins[13:]
+    first, strips, planes = ins[:9], ins[9:11], ins[11:15]
+    (up, coords, counts, links, weights, spread, level, faces, y_spread, z_spread) = ins[15:]
     second, signal2, y_own, z_own, *sent, coarse = outs
     taps, work, (lifted, rows, *coarse_work) = rest[:4], rest[4:8], rest[8:]
-    total = coarse_sums((*first, *planes), *coarse_work)
+    total = coarse_sums((*first, *planes[:2], *strips), *coarse_work)
     r0, r1, r2, r3 = (p.get() for p in planes)
     result = total.astype(bf16)
     coarse.ref[...] = result[0:8]
@@ -654,22 +651,22 @@
         level_faces, (*live[:2], *plainly(level, faces, own_tile)),
         (((9, CHANS, 128), bf16),) * 2 + (PLANE,) * 2, (FACES, FACES, *WORK), 3,
     )
-    y_above, y_below = shifted(low_y, MY, -1), shifted(high_y, MY, 1)
-    partial, low_z, high_z = call(
+    planes = swap_planes((low_y, high_y, low_z, high_z))
+    partial, strip = call(
         row_sums,
-        ((message, slice(HALF_ROWS, HALF_ROWS + 128)), *plainly(own_tile, y_above, y_below, low_z, high_z)),
-        (SUMS,) + (((11, CHANS, 128), bf16),) * 2, (), 1,
+        ((message, slice(HALF_ROWS, HALF_ROWS + 128)), *plainly(own_tile, *planes[:2])),
+        (SUMS, ((3, CHANS, 128), bf16)), (), 1, planes[2:],
     )
     near_half = message.reshape(COARSE, HALF_ROWS + 128)
     near_half, partial = lax.optimization_barrier((near_half, partial))
     partial = lax.all_to_all(partial, MX, 0, 0)
     far_half = lax.ppermute(near_half, "mx_1", [(0, 1), (1, 0)])
-    z_above, z_below = shifted(low_z, MX, -1), shifted(high_z, MX, 1)
+    strips = (shifted(strip, MX, -1), shifted(strip, MX, 1))
     second, *own, low_y, high_y, low_z, high_z, coarse = call(
         second_conv,
         ((where, "smem"),
          *plainly(partial, own_tile, norm_gain.reshape(1, COARSE), norm_bias.reshape(1, COARSE),
-                  patch, plain, near_half, far_half, y_above, y_below, z_above, z_below, up_weight),
+                  patch, plain, near_half, far_half, *strips, *planes, up_weight),
          *live, *plainly(fine_weights, spread, level, faces, y_spread, z_spread)),
         (FIELD, FIELD, FACES, FACES) + (PLANE,) * 4 + (((8, COARSE), bf16),),
         (FIELD, SIGNAL, BANK, BANK, *TAP_STACK, *WORK, ((8, 32, COARSE), f32), ((256, 256), bf16),

time: 110 us -> 110 us (level)
  starting transfers between devices: 38.7 us -> 43.6 us
  waiting for transfers between devices: 24.9 us -> 20.3 us
    ppermute x12 -> x14, starting transfers between devices: 19.1 us -> 24.1 us  [shifted(): lax.ppermute(x, axes, [(i, (i + step) % count) for i in range(count)])]
    ppermute x12 -> x14, waiting for transfers between devices: 22.4 us -> 17.8 us  [shifted(): lax.ppermute(x, axes, [(i, (i + step) % count) for i in range(count)])]
    unnamed x30 -> x34, local copies, waits for them, and re-layouts: 3.78 us -> 4.37 us
  transfers between devices with their start and end apart: 15 -> 17, of which waited for: 7 -> 10; matrix products, arithmetic and copies ran while one was open for 2% -> 2% of each run, Pallas kernels for 6% -> 6%
where the time goes in v6:
time: 110 us
  starting transfers between devices  43.6 us (40%)
  Pallas kernels  38.5 us (35%)
  waiting for transfers between devices  20.3 us (18%)
  local copies, waits for them, and re-layouts  5.65 us (5%)
  between operations  1.42 us (1%)
    pallas_call x7, Pallas kernels, call(): pl.pallas_call(body, in_specs=[hbm] * total, out_specs=[hbm] * len(outs),...  38.5 us
    ppermute x14, starting transfers between devices, shifted(): lax.ppermute(x, axes, [(i, (i + step) % count) for i in range(count)])  24.1 us
    ppermute x14, waiting for transfers between devices, shifted(): lax.ppermute(x, axes, [(i, (i + step) % count) for i in range(count)])  17.8 us
    all_to_all x1, starting transfers between devices, local(): partial = lax.all_to_all(partial, MX, 0, 0)  7.32 us
    all_to_all x1, starting transfers between devices, local(): message = lax.all_to_all(message, MY, 0, 0)  6.17 us
    ppermute x1, starting transfers between devices, local(): far_half = lax.ppermute(near_half, 'mx_1', [(0, 1), (1, 0)])  5.97 us
    unnamed x34, local copies, waits for them, and re-layouts  4.37 us
    all_to_all x1, waiting for transfers between devices, local(): partial = lax.all_to_all(partial, MX, 0, 0)  2.47 us
  transfers between devices with their start and end apart: 17, of which 10 were waited for; matrix products, arithmetic and copies ran while one was open for 2% of the time, Pallas kernels for 6%

profile of v6, /device:TPU:1, one launch (start us, length us, event | category | flops | bytes accessed | tf_op | source)
XLA Modules:
  0.0 110.0 jit_solution(1048737850322085109)
XLA Ops:
  1.3 3.5 %shard_map.177 = (bf16[32,32,128]{2,1,0:T(8,128)(2,1)}, bf16[32,32,128]{2,1,0:T(8,128)(2,1)}, bf16[8,32,128]{2,1,0:T(8,128)(2,1)}, bf16[8,32,128]{2,1,0:T(8,128)...) custom-call(bf16[32,32,512]{2,1,0:T(8,128)(2,1)} %refs_11_.1, ...), custom_call_target="tpu_custom_call" | custom-call | flops 3000000000 | bytes 9000000 | tf_op jit(solution)/shard_map/pallas_call | solution.py:578
  4.8 5.8 %collective-permute-start = (bf16[8,32,128]{2,1,0:T(8,128)(2,1)}, bf16[8,32,128]{2,1,0:T(8,128)(2,1)S(1)}, u32[]{:S(2)}, u32[]{:S(2)}) collective-permute-start(bf16[8,32,128]{2,1,0:T(8,128)(2,1)} %get-tuple-element.30), channel_id=1, source_target_pairs={{0,15},{1,0},{2,1},{3,2},{4,3},{5,4},{6,5},{7,6},{8,7},{9,8},{10,9... | collective-permute-start | bytes 196616 | tf_op jit(solution)/shard_map/ppermute | solution.py:606
  10.7 0.0 collective-permute-start.1
  10.7 1.0 collective-permute-start.2
  11.6 1.5 %collective-permute-start.3 = (bf16[8,32,128]{2,1,0:T(8,128)(2,1)}, bf16[8,32,128]{2,1,0:T(8,128)(2,1)S(1)}, u32[]{:S(2)}, u32[]{:S(2)}) collective-permute-start(bf16[8,32,128]{2,1,0:T(8,128)(2,1)} %get-tuple-element.33), channel_id=1, source_target_pairs={{0,16},{16,32},{32,48},{48,64},{64,80},{80,96},{96,112},{112,128},... | collective-permute-start | bytes 196616 | tf_op jit(solution)/shard_map/ppermute | solution.py:606
  13.1 2.9 %shard_map.176.refs_4_ = bf16[32,32,512]{2,1,0:T(8,128)(2,1)} custom-call(bf16[32,32,512]{2,1,0:T(8,128)(2,1)} %refs_11_.1), custom_call_target="tpu_custom_call" | custom-call | flops 3000000000 | bytes 9000000 | tf_op jit(solution)/shard_map/pallas_call | solution.py:578
  16.0 0.6 pad_add_fusion.refs_14_.refs_0_
  16.6 0.0 collective-permute-done.refs_7_
  16.6 0.7 collective-permute-done.1.refs_8_
  17.3 0.3 collective-permute-done.3.refs_10_
  17.6 0.3 copy-done.8
  17.9 0.0 copy-done.9
  18.0 0.2 copy-done.10
  18.2 7.7 %shard_map.178 = (bf16[32,32,512]{2,1,0:T(8,128)(2,1)}, f32[8,256]{1,0:T(8,128)}, bf16[16,16,3584]{2,1,0:T(8,128)(2,1)}) custom-call(s32[3,32]{1,0:T(4,128)} %refs_0_.9, s32[1]{0:T(128)S(6)} %copy.19.refs_3_.refs_1_.refs_17_, s32[6,32]{1,0:T(8,128)} %refs_2_.5, bf16[3,32,224]{2,1,0:T(8,128)(2,1)} %refs_3_.5, bf16[32,32,512]{2,1,0:T(8,128)(2,1)} %shard_map.176.refs_4_, ...), custom_call_target="tpu_custom_call" | custom-call | flops 8000000000 | bytes 24000000 | tf_op jit(solution)/shard_map/pallas_call | solution.py:578
  25.9 6.2 %all-to-all-start = ((bf16[16,16,3584]{2,1,0:T(8,128)(2,1)}), bf16[16,16,3584]{2,1,0:T(8,128)(2,1)S(1)}, u32[]{:S(2)}, u32[]{:S(2)}) async-start(bf16[16,16,3584]{2,1,0:T(8,128)(2,1)} %get-tuple-element.34), calls=%async_computation | async-start | bytes 3670016 | tf_op jit(solution)/shard_map/all_to_all | solution.py:649
  32.1 3.4 %shard_map.179 = (bf16[9,32,128]{2,1,0:T(8,128)(2,1)}, bf16[9,32,128]{2,1,0:T(8,128)(2,1)}, bf16[8,32,128]{2,1,0:T(8,128)(2,1)}, bf16[8,32,128]{2,1,0:T(8,128)(2,1)}) custom-call(s32[3,32]{1,0:T(4,128)} %refs_0_.9, s32[1]{0:T(128)S(6)} %copy.19.refs_3_.refs_1_.refs_17_, bf16[32,32,512]{2,1,0:T(8,128)(2,1)} %get-tuple-element.36.refs_2_.refs_21_, ...), custom_call_target="tpu_custom_call" | custom-call | flops 3000000000 | bytes 9000000 | tf_op jit(solution)/shard_map/pallas_call | solution.py:578
  35.4 4.8 %collective-permute-start.4 = (bf16[9,32,128]{2,1,0:T(8,128)(2,1)}, bf16[9,32,128]{2,1,0:T(8,128)(2,1)S(1)}, u32[]{:S(2)}, u32[]{:S(2)}) collective-permute-start(bf16[9,32,128]{2,1,0:T(8,128)(2,1)} %get-tuple-element.37), channel_id=1, source_target_pairs={{0,15},{1,0},{2,1},{3,2},{4,3},{5,4},{6,5},{7,6},{8,7},{9,8},{10,9... | collective-permute-start | bytes 221192 | tf_op jit(solution)/shard_map/ppermute | solution.py:606
  40.2 5.0 %collective-permute-start.6 = (bf16[8,32,128]{2,1,0:T(8,128)(2,1)}, bf16[8,32,128]{2,1,0:T(8,128)(2,1)S(1)}, u32[]{:S(2)}, u32[]{:S(2)}) collective-permute-start(bf16[8,32,128]{2,1,0:T(8,128)(2,1)} %get-tuple-element.39), channel_id=1, source_target_pairs={{0,240},{16,0},{32,16},{48,32},{64,48},{80,64},{96,80},{112,96},{1... | collective-permute-start | bytes 196616 | tf_op jit(solution)/shard_map/ppermute | solution.py:606
  45.2 1.1 %collective-permute-done.6.refs_4_.refs_13_ = bf16[8,32,128]{2,1,0:T(8,128)(2,1)S(1)} collective-permute-done((bf16[8,32,128]{2,1,0:T(8,128)(2,1)}, bf16[8,32,128]{2,1,0:T(8,128)(2,1)S(1)}, u32[]{:S(2)}, u32[]{:S(2)}) %collective-permute-start.6) | collective-permute-done | bytes 65568 | tf_op jit(solution)/shard_map/ppermute | solution.py:606
  46.3 0.5 collective-permute-done.7.refs_5_.refs_14_
  46.9 2.5 %collective-permute-done.4.refs_2_.refs_11_ = bf16[9,32,128]{2,1,0:T(8,128)(2,1)S(1)} collective-permute-done((bf16[9,32,128]{2,1,0:T(8,128)(2,1)}, bf16[9,32,128]{2,1,0:T(8,128)(2,1)S(1)}, u32[]{:S(2)}, u32[]{:S(2)}) %collective-permute-start.4) | collective-permute-done | bytes 73760 | tf_op jit(solution)/shard_map/ppermute | solution.py:606
  49.3 5.1 %collective-permute-done.5.refs_3_.refs_12_ = bf16[9,32,128]{2,1,0:T(8,128)(2,1)S(1)} collective-permute-done((bf16[9,32,128]{2,1,0:T(8,128)(2,1)}, bf16[9,32,128]{2,1,0:T(8,128)(2,1)S(1)}, u32[]{:S(2)}, u32[]{:S(2)}) %collective-permute-start.5) | collective-permute-done | bytes 73760 | tf_op jit(solution)/shard_map/ppermute | solution.py:606
  54.5 0.6 copy-done.4
  55.1 1.3 %copy-done = bf16[16,16,3584]{2,1,0:T(8,128)(2,1)} copy-done((bf16[16,16,3584]{2,1,0:T(8,128)(2,1)}, bf16[16,16,3584]{2,1,0:T(8,128)(2,1)S(1)}, u32[]{:S(2)}) %copy-start) | copy-done | bytes 1835032
  56.4 1.7 %shard_map.180 = (f32[16,8,128]{2,1,0:T(8,128)}, bf16[3,32,128]{2,1,0:T(8,128)(2,1)}) custom-call(bf16[16,16,3584]{2,1,0:T(8,128)(2,1)} %copy-done, f32[8,256]{1,0:T(8,128)} %get-tuple-element.35.refs_4_.refs_1_.refs_2_, bf16[9,32,128]{2,1,0:T(8,128)(2,1)} %copy-done.3, bf16[9,32,128]{2,1,0:T(8,128)(2,1)} %copy-done.4, bf16[8,32,128]{2,1,0:T(8,128)(2,1)} %copy-done.5, ...), custom_call_target="tpu_custom_call" | custom-call | flops 1000000000 | bytes 3000000 | tf_op jit(solution)/shard_map/pallas_call | solution.py:578
  58.1 6.0 %collective-permute-start.8 = (bf16[256,3584]{1,0:T(8,128)(2,1)}, bf16[256,3584]{1,0:T(8,128)(2,1)S(1)}, u32[]{:S(2)}, u32[]{:S(2)}) collective-permute-start(bf16[256,3584]{1,0:T(8,128)(2,1)} %bitcast.6), channel_id=1, source_target_pairs={{0,16},{16,0},{1,17},{17,1},{2,18},{18,2},{3,19},{19,3},{4,20},{20... | collective-permute-start | bytes 5505032 | tf_op jit(solution)/shard_map/ppermute | solution.py:663
  64.1 7.3 %all-to-all-start.1 = ((f32[16,8,128]{2,1,0:T(8,128)}), f32[16,8,128]{2,1,0:T(8,128)S(1)}, u32[]{:S(2)}, u32[]{:S(2)}) async-start(f32[16,8,128]{2,1,0:T(8,128)} %get-tuple-element.42), calls=%async_computation.1 | async-start | bytes 131072 | tf_op jit(solution)/shard_map/all_to_all | solution.py:662
  71.4 1.6 %collective-permute-start.10 = (bf16[3,32,128]{2,1,0:T(8,128)(2,1)}, bf16[3,32,128]{2,1,0:T(8,128)(2,1)S(1)}, u32[]{:S(2)}, u32[]{:S(2)}) collective-permute-start(bf16[3,32,128]{2,1,0:T(8,128)(2,1)} %get-tuple-element.44), channel_id=1, source_target_pairs={{0,16},{16,32},{32,48},{48,64},{64,80},{80,96},{96,112},{112,128},... | collective-permute-start | bytes 73736 | tf_op jit(solution)/shard_map/ppermute | solution.py:606
  73.0 0.0 collective-permute-start.9
  73.0 1.2 %collective-permute-done.10.refs_10_ = bf16[3,32,128]{2,1,0:T(8,128)(2,1)S(1)} collective-permute-done((bf16[3,32,128]{2,1,0:T(8,128)(2,1)}, bf16[3,32,128]{2,1,0:T(8,128)(2,1)S(1)}, u32[]{:S(2)}, u32[]{:S(2)}) %collective-permute-start.10) | collective-permute-done | bytes 24608 | tf_op jit(solution)/shard_map/ppermute | solution.py:606
  74.2 2.8 %collective-permute-done.9.refs_9_ = bf16[3,32,128]{2,1,0:T(8,128)(2,1)S(1)} collective-permute-done((bf16[3,32,128]{2,1,0:T(8,128)(2,1)}, bf16[3,32,128]{2,1,0:T(8,128)(2,1)S(1)}, u32[]{:S(2)}, u32[]{:S(2)}) %collective-permute-start.9) | collective-permute-done | bytes 24608 | tf_op jit(solution)/shard_map/ppermute | solution.py:606
  77.0 2.5 %all-to-all-done.1.refs_1_ = f32[16,8,128]{2,1,0:T(8,128)S(1)} async-done(((f32[16,8,128]{2,1,0:T(8,128)}), f32[16,8,128]{2,1,0:T(8,128)S(1)}, u32[]{:S(2)}, u32[]{:S(2)}) %all-to-all-start.1) | async-done | bytes 65568 | tf_op jit(solution)/shard_map/all_to_all | solution.py:662
  79.4 0.0 collective-permute-done.8.refs_8_
  79.5 0.6 copy-done.1
  80.1 0.6 copy-done.2
  80.7 12.9 %shard_map.181 = (bf16[32,32,512]{2,1,0:T(8,128)(2,1)}, bf16[32,32,512]{2,1,0:T(8,128)(2,1)}, bf16[32,32,128]{2,1,0:T(8,128)(2,1)}, bf16[32,32,128]{2,1,0:T(8,12...) custom-call(s32[2]{0:T(128)} %pad_add_fusion.refs_14_.refs_0_, ...), custom_call_target="tpu_custom_call" | custom-call | flops 14000000000 | bytes 42000000 | tf_op jit(solution)/shard_map/pallas_call | solution.py:578
  93.5 2.7 %collective-permute-start.11 = (bf16[8,32,128]{2,1,0:T(8,128)(2,1)}, bf16[8,32,128]{2,1,0:T(8,128)(2,1)S(1)}, u32[]{:S(2)}, u32[]{:S(2)}) collective-permute-start(bf16[8,32,128]{2,1,0:T(8,128)(2,1)} %get-tuple-element.48), channel_id=1, source_target_pairs={{0,15},{1,0},{2,1},{3,2},{4,3},{5,4},{6,5},{7,6},{8,7},{9,8},{10,9... | collective-permute-start | bytes 196616 | tf_op jit(solution)/shard_map/ppermute | solution.py:606
  96.2 0.0 collective-permute-start.12
  96.2 0.3 collective-permute-start.13
  96.5 1.4 %collective-permute-start.14 = (bf16[8,32,128]{2,1,0:T(8,128)(2,1)}, bf16[8,32,128]{2,1,0:T(8,128)(2,1)S(1)}, u32[]{:S(2)}, u32[]{:S(2)}) collective-permute-start(bf16[8,32,128]{2,1,0:T(8,128)(2,1)} %get-tuple-element.51), channel_id=1, source_target_pairs={{0,16},{16,32},{32,48},{48,64},{64,80},{80,96},{96,112},{112,128},... | collective-permute-start | bytes 196616 | tf_op jit(solution)/shard_map/ppermute | solution.py:606
  98.0 1.3 %reshape.19 = bf16[2,2,2,256]{3,2,1,0:T(2,128)(2,1)} reshape(bf16[8,256]{1,0:T(8,128)(2,1)} %get-tuple-element.53) | data formatting | bytes 8192 | tf_op jit(solution)/shard_map/reshape | solution.py:680
  99.2 0.0 collective-permute-done.11.refs_7_
  99.2 3.6 %collective-permute-done.12.refs_8_ = bf16[8,32,128]{2,1,0:T(8,128)(2,1)S(1)} collective-permute-done((bf16[8,32,128]{2,1,0:T(8,128)(2,1)}, bf16[8,32,128]{2,1,0:T(8,128)(2,1)S(1)}, u32[]{:S(2)}, u32[]{:S(2)}) %collective-permute-start.12) | collective-permute-done | bytes 65568 | tf_op jit(solution)/shard_map/ppermute | solution.py:606
  102.9 0.0 collective-permute-done.13.refs_9_
  102.9 0.6 copy-done.12
  103.5 0.0 copy-done.13
  103.5 0.0 copy-done.14
  103.5 6.5 %shard_map.182 = bf16[32,32,512]{2,1,0:T(8,128)(2,1)} custom-call(s32[3,32]{1,0:T(4,128)} %refs_0_.9, s32[1]{0:T(128)S(6)} %copy.19.refs_3_.refs_1_.refs_17_, s32[6,32]{1,0:T(8,128)} %refs_2_.5, bf16[3,32,224]{2,1,0:T(8,128)(2,1)} %refs_3_.5, bf16[32,32,512]{2,1,0:T(8,128)(2,1)} %get-tuple-element.45.refs_4_, ...), custom_call_target="tpu_custom_call" | custom-call | flops 7000000000 | bytes 21000000 | tf_op jit(solution)/shard_map/pallas_call | solution.py:578
  (29 shorter events, 0.1 us)
Async XLA Ops:
  4.8 11.8 %collective-permute-start = (bf16[8,32,128]{2,1,0:T(8,128)(2,1)}, bf16[8,32,128]{2,1,0:T(8,128)(2,1)S(1)}, u32[]{:S(2)}, u32[]{:S(2)}) collective-permute-start(bf16[8,32,128]{2,1,0:T(8,128)(2,1)} %get-tuple-element.30), channel_id=1, source_target_pairs={{0,15},{1,0},{2,1},{3,2},{4,3},{5,4},{6,5},{7,6},{8,7},{9,8},{10,9... | collective-permute-start | bytes 196616 | tf_op jit(solution)/shard_map/ppermute | solution.py:606
  10.7 6.6 %collective-permute-start.1 = (bf16[8,32,128]{2,1,0:T(8,128)(2,1)}, bf16[8,32,128]{2,1,0:T(8,128)(2,1)S(1)}, u32[]{:S(2)}, u32[]{:S(2)}) collective-permute-start(bf16[8,32,128]{2,1,0:T(8,128)(2,1)} %get-tuple-element.31), channel_id=1, source_target_pairs={{0,1},{1,2},{2,3},{3,4},{4,5},{5,6},{6,7},{7,8},{8,9},{9,10},{10,1... | collective-permute-start | bytes 196616 | tf_op jit(solution)/shard_map/ppermute | solution.py:606
  10.7 6.6 %collective-permute-start.2 = (bf16[8,32,128]{2,1,0:T(8,128)(2,1)}, bf16[8,32,128]{2,1,0:T(8,128)(2,1)S(1)}, u32[]{:S(2)}, u32[]{:S(2)}) collective-permute-start(bf16[8,32,128]{2,1,0:T(8,128)(2,1)} %get-tuple-element.32), channel_id=1, source_target_pairs={{0,240},{16,0},{32,16},{48,32},{64,48},{80,64},{96,80},{112,96},{1... | collective-permute-start | bytes 196616 | tf_op jit(solution)/shard_map/ppermute | solution.py:606
  11.6 6.0 %collective-permute-start.3 = (bf16[8,32,128]{2,1,0:T(8,128)(2,1)}, bf16[8,32,128]{2,1,0:T(8,128)(2,1)S(1)}, u32[]{:S(2)}, u32[]{:S(2)}) collective-permute-start(bf16[8,32,128]{2,1,0:T(8,128)(2,1)} %get-tuple-element.33), channel_id=1, source_target_pairs={{0,16},{16,32},{32,48},{48,64},{64,80},{80,96},{96,112},{112,128},... | collective-permute-start | bytes 196616 | tf_op jit(solution)/shard_map/ppermute | solution.py:606
  16.6 1.0 copy-start.7
  17.3 0.6 copy-start.8
  17.3 0.7 copy-start.9
  17.6 0.6 copy-start.10
  25.9 28.6 %all-to-all-start = ((bf16[16,16,3584]{2,1,0:T(8,128)(2,1)}), bf16[16,16,3584]{2,1,0:T(8,128)(2,1)S(1)}, u32[]{:S(2)}, u32[]{:S(2)}) async-start(bf16[16,16,3584]{2,1,0:T(8,128)(2,1)} %get-tuple-element.34), calls=%async_computation | async-start | bytes 3670016 | tf_op jit(solution)/shard_map/all_to_all | solution.py:649
  35.4 13.9 %collective-permute-start.4 = (bf16[9,32,128]{2,1,0:T(8,128)(2,1)}, bf16[9,32,128]{2,1,0:T(8,128)(2,1)S(1)}, u32[]{:S(2)}, u32[]{:S(2)}) collective-permute-start(bf16[9,32,128]{2,1,0:T(8,128)(2,1)} %get-tuple-element.37), channel_id=1, source_target_pairs={{0,15},{1,0},{2,1},{3,2},{4,3},{5,4},{6,5},{7,6},{8,7},{9,8},{10,9... | collective-permute-start | bytes 221192 | tf_op jit(solution)/shard_map/ppermute | solution.py:606
  40.2 14.3 %collective-permute-start.5 = (bf16[9,32,128]{2,1,0:T(8,128)(2,1)}, bf16[9,32,128]{2,1,0:T(8,128)(2,1)S(1)}, u32[]{:S(2)}, u32[]{:S(2)}) collective-permute-start(bf16[9,32,128]{2,1,0:T(8,128)(2,1)} %get-tuple-element.38), channel_id=1, source_target_pairs={{0,1},{1,2},{2,3},{3,4},{4,5},{5,6},{6,7},{7,8},{8,9},{9,10},{10,1... | collective-permute-start | bytes 221192 | tf_op jit(solution)/shard_map/ppermute | solution.py:606
  40.2 6.1 %collective-permute-start.6 = (bf16[8,32,128]{2,1,0:T(8,128)(2,1)}, bf16[8,32,128]{2,1,0:T(8,128)(2,1)S(1)}, u32[]{:S(2)}, u32[]{:S(2)}) collective-permute-start(bf16[8,32,128]{2,1,0:T(8,128)(2,1)} %get-tuple-element.39), channel_id=1, source_target_pairs={{0,240},{16,0},{32,16},{48,32},{64,48},{80,64},{96,80},{112,96},{1... | collective-permute-start | bytes 196616 | tf_op jit(solution)/shard_map/ppermute | solution.py:606
  45.2 1.7 %collective-permute-start.7 = (bf16[8,32,128]{2,1,0:T(8,128)(2,1)}, bf16[8,32,128]{2,1,0:T(8,128)(2,1)S(1)}, u32[]{:S(2)}, u32[]{:S(2)}) collective-permute-start(bf16[8,32,128]{2,1,0:T(8,128)(2,1)} %get-tuple-element.40), channel_id=1, source_target_pairs={{0,16},{16,32},{32,48},{48,64},{64,80},{80,96},{96,112},{112,128},... | collective-permute-start | bytes 196616 | tf_op jit(solution)/shard_map/ppermute | solution.py:606
  46.3 8.2 %copy-start.5 = (bf16[8,32,128]{2,1,0:T(8,128)(2,1)}, bf16[8,32,128]{2,1,0:T(8,128)(2,1)S(1)}, u32[]{:S(2)}) copy-start(bf16[8,32,128]{2,1,0:T(8,128)(2,1)S(1)} %collective-permute-done.6.refs_4_.refs_13_) | copy-start | bytes 196612
  46.8 7.6 %copy-start.6 = (bf16[8,32,128]{2,1,0:T(8,128)(2,1)}, bf16[8,32,128]{2,1,0:T(8,128)(2,1)S(1)}, u32[]{:S(2)}) copy-start(bf16[8,32,128]{2,1,0:T(8,128)(2,1)S(1)} %collective-permute-done.7.refs_5_.refs_14_) | copy-start | bytes 196612
  49.3 5.2 %copy-start.3 = (bf16[9,32,128]{2,1,0:T(8,128)(2,1)}, bf16[9,32,128]{2,1,0:T(8,128)(2,1)S(1)}, u32[]{:S(2)}) copy-start(bf16[9,32,128]{2,1,0:T(8,128)(2,1)S(1)} %collective-permute-done.4.refs_2_.refs_11_) | copy-start | bytes 221188
  54.5 0.6 copy-start.4
  55.1 1.3 %copy-start = (bf16[16,16,3584]{2,1,0:T(8,128)(2,1)}, bf16[16,16,3584]{2,1,0:T(8,128)(2,1)S(1)}, u32[]{:S(2)}) copy-start(bf16[16,16,3584]{2,1,0:T(8,128)(2,1)S(1)} %all-to-all-done.refs_0_) | copy-start | bytes 5505028
  58.1 21.3 %collective-permute-start.8 = (bf16[256,3584]{1,0:T(8,128)(2,1)}, bf16[256,3584]{1,0:T(8,128)(2,1)S(1)}, u32[]{:S(2)}, u32[]{:S(2)}) collective-permute-start(bf16[256,3584]{1,0:T(8,128)(2,1)} %bitcast.6), channel_id=1, source_target_pairs={{0,16},{16,0},{1,17},{17,1},{2,18},{18,2},{3,19},{19,3},{4,20},{20... | collective-permute-start | bytes 5505032 | tf_op jit(solution)/shard_map/ppermute | solution.py:663
  64.1 15.4 %all-to-all-start.1 = ((f32[16,8,128]{2,1,0:T(8,128)}), f32[16,8,128]{2,1,0:T(8,128)S(1)}, u32[]{:S(2)}, u32[]{:S(2)}) async-start(f32[16,8,128]{2,1,0:T(8,128)} %get-tuple-element.42), calls=%async_computation.1 | async-start | bytes 131072 | tf_op jit(solution)/shard_map/all_to_all | solution.py:662
  71.4 2.8 %collective-permute-start.10 = (bf16[3,32,128]{2,1,0:T(8,128)(2,1)}, bf16[3,32,128]{2,1,0:T(8,128)(2,1)S(1)}, u32[]{:S(2)}, u32[]{:S(2)}) collective-permute-start(bf16[3,32,128]{2,1,0:T(8,128)(2,1)} %get-tuple-element.44), channel_id=1, source_target_pairs={{0,16},{16,32},{32,48},{48,64},{64,80},{80,96},{96,112},{112,128},... | collective-permute-start | bytes 73736 | tf_op jit(solution)/shard_map/ppermute | solution.py:606
  73.0 3.9 %collective-permute-start.9 = (bf16[3,32,128]{2,1,0:T(8,128)(2,1)}, bf16[3,32,128]{2,1,0:T(8,128)(2,1)S(1)}, u32[]{:S(2)}, u32[]{:S(2)}) collective-permute-start(bf16[3,32,128]{2,1,0:T(8,128)(2,1)} %get-tuple-element.44), channel_id=1, source_target_pairs={{0,240},{16,0},{32,16},{48,32},{64,48},{80,64},{96,80},{112,96},{1... | collective-permute-start | bytes 73736 | tf_op jit(solution)/shard_map/ppermute | solution.py:606
  74.2 5.3 %copy-start.15 = (bf16[3,32,128]{2,1,0:T(8,128)(2,1)}, bf16[3,32,128]{2,1,0:T(8,128)(2,1)S(1)}, u32[]{:S(2)}) copy-start(bf16[3,32,128]{2,1,0:T(8,128)(2,1)S(1)} %collective-permute-done.10.refs_10_) | copy-start | bytes 73732
  77.0 2.5 %copy-start.16 = (bf16[3,32,128]{2,1,0:T(8,128)(2,1)}, bf16[3,32,128]{2,1,0:T(8,128)(2,1)S(1)}, u32[]{:S(2)}) copy-start(bf16[3,32,128]{2,1,0:T(8,128)(2,1)S(1)} %collective-permute-done.9.refs_9_) | copy-start | bytes 73732
  79.4 0.6 copy-start.1
  79.4 1.2 %copy-start.2 = (bf16[256,3584]{1,0:T(8,128)(2,1)}, bf16[256,3584]{1,0:T(8,128)(2,1)S(1)}, u32[]{:S(2)}) copy-start(bf16[256,3584]{1,0:T(8,128)(2,1)S(1)} %collective-permute-done.8.refs_8_) | copy-start | bytes 5505028
  93.5 5.7 %collective-permute-start.11 = (bf16[8,32,128]{2,1,0:T(8,128)(2,1)}, bf16[8,32,128]{2,1,0:T(8,128)(2,1)S(1)}, u32[]{:S(2)}, u32[]{:S(2)}) collective-permute-start(bf16[8,32,128]{2,1,0:T(8,128)(2,1)} %get-tuple-element.48), channel_id=1, source_target_pairs={{0,15},{1,0},{2,1},{3,2},{4,3},{5,4},{6,5},{7,6},{8,7},{9,8},{10,9... | collective-permute-start | bytes 196616 | tf_op jit(solution)/shard_map/ppermute | solution.py:606
  96.2 6.6 %collective-permute-start.12 = (bf16[8,32,128]{2,1,0:T(8,128)(2,1)}, bf16[8,32,128]{2,1,0:T(8,128)(2,1)S(1)}, u32[]{:S(2)}, u32[]{:S(2)}) collective-permute-start(bf16[8,32,128]{2,1,0:T(8,128)(2,1)} %get-tuple-element.49), channel_id=1, source_target_pairs={{0,1},{1,2},{2,3},{3,4},{4,5},{5,6},{6,7},{7,8},{8,9},{9,10},{10,1... | collective-permute-start | bytes 196616 | tf_op jit(solution)/shard_map/ppermute | solution.py:606
  96.2 6.6 %collective-permute-start.13 = (bf16[8,32,128]{2,1,0:T(8,128)(2,1)}, bf16[8,32,128]{2,1,0:T(8,128)(2,1)S(1)}, u32[]{:S(2)}, u32[]{:S(2)}) collective-permute-start(bf16[8,32,128]{2,1,0:T(8,128)(2,1)} %get-tuple-element.50), channel_id=1, source_target_pairs={{0,240},{16,0},{32,16},{48,32},{64,48},{80,64},{96,80},{112,96},{1... | collective-permute-start | bytes 196616 | tf_op jit(solution)/shard_map/ppermute | solution.py:606
  96.5 6.4 %collective-permute-start.14 = (bf16[8,32,128]{2,1,0:T(8,128)(2,1)}, bf16[8,32,128]{2,1,0:T(8,128)(2,1)S(1)}, u32[]{:S(2)}, u32[]{:S(2)}) collective-permute-start(bf16[8,32,128]{2,1,0:T(8,128)(2,1)} %get-tuple-element.51), channel_id=1, source_target_pairs={{0,16},{16,32},{32,48},{48,64},{64,80},{80,96},{96,112},{112,128},... | collective-permute-start | bytes 196616 | tf_op jit(solution)/shard_map/ppermute | solution.py:606
  99.2 3.6 %copy-start.11 = (bf16[8,32,128]{2,1,0:T(8,128)(2,1)}, bf16[8,32,128]{2,1,0:T(8,128)(2,1)S(1)}, u32[]{:S(2)}) copy-start(bf16[8,32,128]{2,1,0:T(8,128)(2,1)S(1)} %collective-permute-done.11.refs_7_) | copy-start | bytes 196612
  102.8 0.6 copy-start.12
  102.9 0.7 copy-start.13
  102.9 0.7 copy-start.14
